TPU v7x, 32 devices: a whole 2x2x4 slice. The times are simulated.
32 devices in a mesh: row: 8 (over y, x, core), col: 4 (over z).
Axes of the slice: x: 2, y: 2, z: 4, core: 2. Of those that a mesh axis runs over, the one named last changes fastest.
Arguments:
- diag: float32 [4, 1024, 1024], P(None, 'row'), as said below
- panel_rows: float32 [16, 8, 64, 1024], P('row', None, None, 'col')
- panel_cols: float32 [4, 8, 64, 1024], P('col', None, 'row')
- trailing: float32 [16, 4, 8, 64, 1024], P('row', 'col')
- sketch: float32 [64, 1024], replicated, may hold values from -6 to 6
- panel_rank: int32 [16], P('row'), may hold values from 16 to 64
- col_rank: int32 [4], P('col'), may hold values from 16 to 64
- tile_rank: int32 [16, 4], P('row', 'col'), may hold values from 32 to 64
- keep_rank: int32 [16, 4], P('row', 'col'), may hold values from 8 to 32
Outputs:
- new_tiles: float32 [16, 4, 8, 64, 1024], P('row', 'col')
Inputs may be any that keep to these rules, and one draw needn't show every extreme that they name: `keep_rank`: recompression ranks, never above the tile's rank. diag[0] is symmetric positive definite with smallest eigenvalue 0.5 or more; the tangents are symmetric.
All inputs are finite; a program needn't handle non-finite values.
Results may differ from a plain program's by a relative error of at most 0.0003.
Values sent between devices are 32-bit elements; how exact they have to be, the bound alone decides.
No kernel may reach another device: no remote copies, remote signals or barrier semaphores. Data moves between devices by JAX's collectives and lax.ppermute only.
A program may use at most 192 MiB of HBM per device.

v0:
```python
import math

import jax
import jax.numpy as jnp
from jax import lax
from jax.sharding import PartitionSpec as P

HIGHEST_PRECISION = lax.Precision.HIGHEST


def highest_accuracy(left, right):
    return jnp.dot(left, right, precision=HIGHEST_PRECISION, preferred_element_type=jnp.float32)


def rank_mask(rank_values, rank_count):
    return (jnp.arange(rank_count, dtype=jnp.int32) < rank_values[..., None]).astype(jnp.float32)


def inverse_apply(lower_factor, rank_rows):
    half_solved = jax.scipy.linalg.solve_triangular(lower_factor, rank_rows.T, lower=True)
    full_solved = jax.scipy.linalg.solve_triangular(lower_factor, half_solved, lower=True, trans=1)
    return full_solved.T


def sketch_apply(active_sketch, previous_left_factor, previous_right_factor, u_row, mix_in, u_col):
    return highest_accuracy(
        highest_accuracy(active_sketch, previous_right_factor.T), previous_left_factor
    ) - highest_accuracy(
        highest_accuracy(highest_accuracy(active_sketch, u_col.T), mix_in.T), u_row
    )


def basis_apply(
    row_basis_matrix, previous_left_factor, previous_right_factor, u_row, mix_in, u_col
):
    return highest_accuracy(
        highest_accuracy(row_basis_matrix, previous_left_factor.T), previous_right_factor
    ) - highest_accuracy(
        highest_accuracy(highest_accuracy(row_basis_matrix, u_row.T), mix_in), u_col
    )


def compress_all(
    previous_left_factor,
    previous_right_factor,
    u_row,
    mix_in,
    u_col,
    du_old,
    dv_old,
    du_row,
    dmix_in,
    du_col,
    active_sketch,
    live_mask,
):
    sketched = sketch_apply(
        active_sketch, previous_left_factor, previous_right_factor, u_row, mix_in, u_col
    )
    gram_matrix = highest_accuracy(sketched, sketched.T) + jnp.diag(1.0 - live_mask)
    factor = jnp.linalg.cholesky(gram_matrix)
    row_basis_matrix = jax.scipy.linalg.solve_triangular(factor, sketched, lower=True)
    coefficients = basis_apply(
        row_basis_matrix, previous_left_factor, previous_right_factor, u_row, mix_in, u_col
    )
    up_scale = math.sqrt(previous_left_factor.shape[1])
    down_scale = math.sqrt(previous_left_factor.shape[0])

    def tangent_direction(
        previous_left_derivative,
        previous_right_derivative,
        row_left_derivative,
        mixing_derivative,
        column_left_derivative,
    ):
        sketch_derivative = highest_accuracy(
            highest_accuracy(active_sketch, previous_right_derivative.T), previous_left_factor
        ) + highest_accuracy(
            highest_accuracy(active_sketch, previous_right_factor.T), previous_left_derivative
        )
        sketch_derivative = sketch_derivative - highest_accuracy(
            highest_accuracy(highest_accuracy(active_sketch, column_left_derivative.T), mix_in.T),
            u_row,
        )
        sketch_derivative = sketch_derivative - highest_accuracy(
            highest_accuracy(highest_accuracy(active_sketch, u_col.T), mixing_derivative.T), u_row
        )
        sketch_derivative = sketch_derivative - highest_accuracy(
            highest_accuracy(highest_accuracy(active_sketch, u_col.T), mix_in.T),
            row_left_derivative,
        )
        d_gram = highest_accuracy(sketch_derivative, sketched.T) + highest_accuracy(
            sketched, sketch_derivative.T
        )
        inner = jax.scipy.linalg.solve_triangular(factor, d_gram, lower=True)
        middle = jax.scipy.linalg.solve_triangular(factor, inner.T, lower=True)
        lower_part = jnp.tril(middle) - 0.5 * jnp.diag(jnp.diagonal(middle))
        d_factor = highest_accuracy(factor, lower_part)
        d_basis = jax.scipy.linalg.solve_triangular(
            factor, sketch_derivative - highest_accuracy(d_factor, row_basis_matrix), lower=True
        )
        coefficient_derivative = basis_apply(
            d_basis, previous_left_factor, previous_right_factor, u_row, mix_in, u_col
        )
        coefficient_derivative = (
            coefficient_derivative
            + highest_accuracy(
                highest_accuracy(row_basis_matrix, previous_left_derivative.T),
                previous_right_factor,
            )
            + highest_accuracy(
                highest_accuracy(row_basis_matrix, previous_left_factor.T),
                previous_right_derivative,
            )
        )
        coefficient_derivative = coefficient_derivative - highest_accuracy(
            highest_accuracy(highest_accuracy(row_basis_matrix, row_left_derivative.T), mix_in),
            u_col,
        )
        coefficient_derivative = coefficient_derivative - highest_accuracy(
            highest_accuracy(highest_accuracy(row_basis_matrix, u_row.T), mixing_derivative), u_col
        )
        coefficient_derivative = coefficient_derivative - highest_accuracy(
            highest_accuracy(highest_accuracy(row_basis_matrix, u_row.T), mix_in),
            column_left_derivative,
        )
        return (d_basis * up_scale, coefficient_derivative / down_scale)

    tangent_basis, tangent_coeff = jax.vmap(tangent_direction)(
        du_old, dv_old, du_row, dmix_in, du_col
    )
    return (row_basis_matrix * up_scale, coefficients / down_scale, tangent_basis, tangent_coeff)


def update_tile(
    row_tile, row_solved, col_tile, col_solved, col_products, old_tile, tile_mask, keep_mask, sketch
):
    old_tile = old_tile * tile_mask[None, :, None]
    mixing = highest_accuracy(row_tile[4], col_solved.T)
    tangent_mix = jnp.stack(
        [
            highest_accuracy(row_tile[5 + direction], col_solved.T)
            + highest_accuracy(row_solved, col_tile[5 + direction].T)
            - highest_accuracy(row_solved, col_products[direction].T)
            for direction in range(3)
        ]
    )
    active_sketch = sketch * keep_mask[:, None]
    basis_out, coeff_out, tangent_basis, tangent_coeff = compress_all(
        old_tile[0],
        old_tile[4],
        row_tile[0],
        mixing,
        col_tile[0],
        old_tile[1:4],
        old_tile[5:8],
        row_tile[1:4],
        tangent_mix,
        col_tile[1:4],
        active_sketch,
        keep_mask,
    )
    return jnp.concatenate([basis_out[None], tangent_basis, coeff_out[None], tangent_coeff], axis=0)


def on_device(
    diag, panel_rows, panel_cols, trailing, sketch, panel_rank, col_rank, tile_rank, keep_rank
):
    rank_count = sketch.shape[0]
    tile_width = sketch.shape[1]
    primal = lax.all_gather(diag[0], "row", axis=0, tiled=True)
    lower_factor = jnp.linalg.cholesky(primal)
    rows_kept = (
        lax.all_gather(panel_rows, "col", axis=3, tiled=True)
        * rank_mask(panel_rank, rank_count)[:, None, :, None]
    )
    cols_kept = (
        lax.all_gather(panel_cols, "row", axis=2, tiled=True)
        * rank_mask(col_rank, rank_count)[:, None, :, None]
    )
    col_tile = cols_kept[0]
    col_solved = inverse_apply(lower_factor, col_tile[4])
    slab_products = jnp.einsum("aj,tij->tai", col_solved, diag[1:], precision=HIGHEST_PRECISION)
    col_products = lax.all_gather(slab_products, "row", axis=2, tiled=True)
    local_rows = rows_kept.shape[0]
    row_solved = inverse_apply(lower_factor, rows_kept[:, 4].reshape(-1, tile_width)).reshape(
        local_rows, rank_count, tile_width
    )
    tile_live = rank_mask(tile_rank[:, 0], rank_count)
    keep_live = rank_mask(keep_rank[:, 0], rank_count)

    def one_tile(row_tile, row_z, old_tile, tile_mask, keep_mask):
        return update_tile(
            row_tile,
            row_z,
            col_tile,
            col_solved,
            col_products,
            old_tile,
            tile_mask,
            keep_mask,
            sketch,
        )

    updated = jax.vmap(one_tile)(rows_kept, row_solved, trailing[:, 0], tile_live, keep_live)
    return updated[:, None]


def solution(mesh):
    in_specs = (
        P(None, "row", None),
        P("row", None, None, "col"),
        P("col", None, "row", None),
        P("row", "col", None, None, None),
        P(),
        P("row"),
        P("col"),
        P("row", "col"),
        P("row", "col"),
    )
    out_specs = P("row", "col", None, None, None)
    return jax.shard_map(
        on_device, mesh=mesh, in_specs=in_specs, out_specs=out_specs, check_vma=False
    )
```

profile of v0, /device:TPU:0, one launch (start us, length us, event | category | flops | bytes accessed | tf_op | source)
XLA Modules:
  0.0 666.3 jit_solution(1411058238016009759)
XLA Ops:
  24.3 15.6 %all-gather.5.cloned.1.call-done = f32[1,8,64,1024]{3,2,1,0:T(8,128)} async-done(((f32[1,8,8,1024]{3,2,1,0:T(8,128)}), f32[1,8,64,1024]{3,2,1,0:T(8,128)}) %all-gather.5.cloned.1.call-update) | async-done | bytes 2097168 | tf_op jit(solution)/shard_map/all_gather | solution.py:178
  45.1 77.2 %all-gather.7.cloned.1.call-done = f32[2,8,64,1024]{3,2,0,1:T(8,128)} async-done(((f32[2,8,64,256]{3,2,0,1:T(8,128)}), f32[2,8,64,1024]{3,2,0,1:T(8,128)}) %all-gather.7.cloned.1.call-update) | async-done | bytes 4194320 | tf_op jit(solution)/shard_map/all_gather | solution.py:174
  131.1 29.1 %all-gather.9.cloned.1.call-done = f32[1,1024,1024]{1,2,0:T(8,128)} async-done(((f32[1,128,1024]{1,2,0:T(8,128)}), f32[1,1024,1024]{1,2,0:T(8,128)}) %all-gather.9.cloned.1.call-update) | async-done | bytes 4194320 | tf_op jit(solution)/shard_map/all_gather | solution.py:171
  160.2 5.5 copy.105
  165.6 4.4 fusion
  172.1 11.7 %cholesky.241 = f32[128,128]{1,0:T(8,128)S(1)} custom-call(f32[128,128]{1,0:T(8,128)S(1)} %cholesky.622), custom_call_target="Cholesky" | custom-call | tf_op jit(solution)/shard_map/jit(cholesky)/cholesky | solution.py:172
  183.8 9.8 %custom-call.86 = f32[1,128,128]{1,2,0:T(8,128)S(1)} custom-call(f32[1,128,128]{2,1,0:T(8,128)S(1)} %get-tuple-element.70), custom_call_target="InvertDiagBlocksLowerTriangular" | custom-call | tf_op jit(solution)/shard_map/jit(cholesky)/cholesky | solution.py:172
  200.1 11.9 %cholesky.264 = f32[128,128]{1,0:T(8,128)S(1)} custom-call(f32[128,128]{1,0:T(8,128)S(1)} %cholesky.626), custom_call_target="Cholesky" | custom-call | tf_op jit(solution)/shard_map/jit(cholesky)/cholesky | solution.py:172
  212.6 9.8 %custom-call.87 = f32[1,128,128]{1,2,0:T(8,128)S(1)} custom-call(f32[1,128,128]{2,1,0:T(8,128)S(1)} %get-tuple-element.67), custom_call_target="InvertDiagBlocksLowerTriangular" | custom-call | tf_op jit(solution)/shard_map/jit(cholesky)/cholesky | solution.py:172
  225.7 11.7 %cholesky.502 = f32[128,128]{1,0:T(8,128)S(1)} custom-call(f32[128,128]{1,0:T(8,128)S(1)} %cholesky.631), custom_call_target="Cholesky" | custom-call | tf_op jit(solution)/shard_map/jit(cholesky)/cholesky | solution.py:172
  238.8 9.8 %custom-call.88 = f32[1,128,128]{1,2,0:T(8,128)S(1)} custom-call(f32[1,128,128]{2,1,0:T(8,128)S(1)} %get-tuple-element.64), custom_call_target="InvertDiagBlocksLowerTriangular" | custom-call | tf_op jit(solution)/shard_map/jit(cholesky)/cholesky | solution.py:172
  252.1 12.1 %cholesky.521 = f32[128,128]{1,0:T(8,128)S(1)} custom-call(f32[128,128]{1,0:T(8,128)S(1)} %cholesky.636), custom_call_target="Cholesky" | custom-call | tf_op jit(solution)/shard_map/jit(cholesky)/cholesky | solution.py:172
  265.5 9.8 %custom-call.89 = f32[1,128,128]{1,2,0:T(8,128)S(1)} custom-call(f32[1,128,128]{2,1,0:T(8,128)S(1)} %get-tuple-element.61), custom_call_target="InvertDiagBlocksLowerTriangular" | custom-call | tf_op jit(solution)/shard_map/jit(cholesky)/cholesky | solution.py:172
  278.7 11.7 %cholesky.540 = f32[128,128]{1,0:T(8,128)S(1)} custom-call(f32[128,128]{1,0:T(8,128)S(1)} %cholesky.641), custom_call_target="Cholesky" | custom-call | tf_op jit(solution)/shard_map/jit(cholesky)/cholesky | solution.py:172
  291.7 10.0 %custom-call.90 = f32[1,128,128]{1,2,0:T(8,128)S(1)} custom-call(f32[1,128,128]{2,1,0:T(8,128)S(1)} %get-tuple-element.58), custom_call_target="InvertDiagBlocksLowerTriangular" | custom-call | tf_op jit(solution)/shard_map/jit(cholesky)/cholesky | solution.py:172
  305.0 11.7 %cholesky.560 = f32[128,128]{1,0:T(8,128)S(1)} custom-call(f32[128,128]{1,0:T(8,128)S(1)} %cholesky.646), custom_call_target="Cholesky" | custom-call | tf_op jit(solution)/shard_map/jit(cholesky)/cholesky | solution.py:172
  318.0 9.8 %custom-call.91 = f32[1,128,128]{1,2,0:T(8,128)S(1)} custom-call(f32[1,128,128]{2,1,0:T(8,128)S(1)} %get-tuple-element.55), custom_call_target="InvertDiagBlocksLowerTriangular" | custom-call | tf_op jit(solution)/shard_map/jit(cholesky)/cholesky | solution.py:172
  330.8 11.9 %cholesky.580 = f32[128,128]{1,0:T(8,128)S(1)} custom-call(f32[128,128]{1,0:T(8,128)S(1)} %cholesky.651), custom_call_target="Cholesky" | custom-call | tf_op jit(solution)/shard_map/jit(cholesky)/cholesky | solution.py:172
  344.0 9.8 %custom-call.92 = f32[1,128,128]{1,2,0:T(8,128)S(1)} custom-call(f32[1,128,128]{2,1,0:T(8,128)S(1)} %get-tuple-element.52), custom_call_target="InvertDiagBlocksLowerTriangular" | custom-call | tf_op jit(solution)/shard_map/jit(cholesky)/cholesky | solution.py:172
  356.5 11.7 %cholesky.598 = f32[128,128]{1,0:T(8,128)S(1)} custom-call(f32[128,128]{1,0:T(8,128)S(1)} %convolution_subtract_fusion.21), custom_call_target="Cholesky" | custom-call | tf_op jit(solution)/shard_map/jit(cholesky)/cholesky | solution.py:172
  375.2 4.9 select_select_fusion
  380.1 28.7 %while.1 = (s32[]{:T(128)}, f32[1024,1024]{1,0:T(8,128)}, s32[8,2]{0,1:T(2,128)S(1)}, f32[8,128,128]{2,1,0:T(8,128)}, s32[]{:T(128)}) while((s32[]{:T(128)}, f32[1024,1024]{1,0:T(8,128)}, s32[8,2]{0,1:T(2,128)S(1)}, f32[8,128,128]{2,1,0:T(8,128)}, s32[]{:T(128)}) %tuple.84), condition=%wide.while_cond, body=%wide.while_body.sunk | while | flops 2 | bytes 132705 | solution.py:21
  408.8 79.8 %custom-call.93 = f32[8,128,128]{1,2,0:T(8,128)S(1)} custom-call(f32[8,128,128]{2,1,0:T(8,128)} %get-tuple-element.13), custom_call_target="InvertDiagBlocksLowerTriangular" | custom-call | tf_op jit(solution)/shard_map/jit(_solve_triangular)/triangular_solve | solution.py:21
  515.2 11.7 %custom-call.94 = f32[2,64,64]{2,1,0:T(8,128)S(1)} custom-call(f32[2,64,64]{2,1,0:T(8,128)S(1)} %fusion.264), custom_call_target="Cholesky" | custom-call | tf_op jit(solution)/shard_map/vmap(jit(cholesky))/cholesky | solution.py:61
  527.5 10.0 %custom-call.95 = f32[2,1,64,64]{2,3,1,0:T(8,128)S(1)} custom-call(f32[2,1,64,64]{3,2,1,0:T(8,128)S(1)} %select_bitcast_fusion), custom_call_target="InvertDiagBlocksLowerTriangular" | custom-call | tf_op jit(solution)/shard_map/vmap(jit(_solve_triangular))/triangular_solve | solution.py:62
  545.2 3.6 fusion.31
  568.8 13.1 %all_gather.15 = f32[3,64,1024]{2,1,0:T(8,128)S(1)} all-gather(f32[3,64,128]{2,1,0:T(8,128)} %fusion.31), channel_id=1, replica_groups=mesh['row'=8,'col'=4] {'row'}, dimensions={2}, use_global_device_ids=true | all-gather | bytes 884736 | tf_op jit(solution)/shard_map/all_gather | solution.py:184
  603.6 4.4 copy.125
  614.1 5.3 copy.127
  619.4 5.3 fusion.1
  624.7 3.3 copy.130
  628.0 4.0 copy.131
  (326 shorter events, 205.0 us)
Async XLA Ops:
  6.5 3.2 slice-start
  6.5 4.9 copy-start.29
  6.5 5.1 copy-start.30
  6.5 5.1 copy-start.31
  6.5 33.4 %all-gather.5.cloned.1.call-start = ((), (), s32[]{:S(2)}) async-start(), calls=%async_computation | async-start | bytes 2359296 | tf_op jit(solution)/shard_map/all_gather | solution.py:178
  7.3 115.0 %all-gather.7.cloned.1.call-start = ((), (), s32[]{:S(2)}) async-start(), calls=%async_computation.1 | async-start | bytes 5242880 | tf_op jit(solution)/shard_map/all_gather | solution.py:174
  9.6 150.5 %all-gather.9.cloned.1.call-start = ((), (), s32[]{:S(2)}) async-start(), calls=%async_computation.2 | async-start | bytes 4718592 | tf_op jit(solution)/shard_map/all_gather | solution.py:171
  11.4 515.6 %copy-start.27 = (pred[64,64]{1,0:T(8,128)(4,1)}, pred[64,64]{1,0:T(8,128)(4,1)S(1)}, u32[]{:S(2)}) copy-start(pred[64,64]{1,0:T(8,128)(4,1)S(1)} %iota_compare_fusion.5) | copy-start | bytes 12292
  11.8 3.2 copy-start.11
  14.9 6.8 %copy-start.1 = (f32[2,8,64,1024]{3,2,0,1:T(8,128)}, f32[2,8,64,1024]{3,2,0,1:T(8,128)S(1)}, u32[]{:S(2)}) copy-start(f32[2,8,64,1024]{3,2,0,1:T(8,128)S(1)} %bitcast_multiply_fusion) | copy-start | bytes 12582916
  15.6 4.1 copy-start.18
  43.1 469.4 %copy-start.20 = (f32[2,64,64]{2,1,0:T(8,128)}, f32[2,64,64]{2,1,0:T(8,128)S(1)}, u32[]{:S(2)}) copy-start(f32[2,64,64]{2,1,0:T(8,128)S(1)} %fusion.38) | copy-start | bytes 98308
  125.0 2.0 copy-start.2
  170.1 2.0 copy-start.5
  496.2 16.5 %copy-start.12 = (f32[2,64,1024]{2,1,0:T(8,128)S(1)}, f32[2,64,1024]{2,1,0:T(8,128)}, u32[]{:S(2)}) copy-start(f32[2,64,1024]{2,1,0:T(8,128)} %fusion.82) | copy-start | bytes 1572868
  537.5 16.9 %copy-start = (f32[1024,1024]{1,0:T(8,128)S(1)}, f32[1024,1024]{1,0:T(8,128)}, u32[]{:S(2)}) copy-start(f32[1024,1024]{1,0:T(8,128)} %get-tuple-element.169) | copy-start | bytes 12582916
  537.5 18.3 %copy-start.13 = (f32[128,1024]{0,1:T(8,128)S(1)}, f32[128,1024]{0,1:T(8,128)}, u32[]{:S(2)}) copy-start(f32[128,1024]{0,1:T(8,128)} %copy.111) | copy-start | bytes 1572868
  566.7 22.3 %copy-start.21 = (f32[2,64,64]{2,1,0:T(8,128)S(1)}, f32[2,64,64]{2,1,0:T(8,128)}, u32[]{:S(2)}) copy-start(f32[2,64,64]{2,1,0:T(8,128)} %copy-done.20) | copy-start | bytes 98308
  583.5 8.7 %copy-start.24 = (f32[2,64,64]{2,1,0:T(8,128)S(1)}, f32[2,64,64]{2,1,0:T(8,128)}, u32[]{:S(2)}) copy-start(f32[2,64,64]{2,1,0:T(8,128)} %copy-done.23) | copy-start | bytes 98308
  586.2 7.5 %copy-start.15 = (f32[2,64,3,64]{3,1,2,0:T(8,128)S(1)}, f32[2,64,3,64]{3,1,2,0:T(8,128)}, u32[]{:S(2)}) copy-start(f32[2,64,3,64]{3,1,2,0:T(8,128)} %fusion.46) | copy-start | bytes 294916
  589.6 6.9 %copy-start.7 = (f32[2,3,64,1024]{3,2,0,1:T(8,128)S(1)}, f32[2,3,64,1024]{3,2,0,1:T(8,128)}, u32[]{:S(2)}) copy-start(f32[2,3,64,1024]{3,2,0,1:T(8,128)} %get-tuple-element.27) | copy-start | bytes 4718596
  589.6 6.9 %copy-start.9 = (f32[2,64,3,1024]{3,1,2,0:T(8,128)S(1)}, f32[2,64,3,1024]{3,1,2,0:T(8,128)}, u32[]{:S(2)}) copy-start(f32[2,64,3,1024]{3,1,2,0:T(8,128)} %fusion.64) | copy-start | bytes 4718596
  589.6 6.9 %copy-start.19 = (f32[2,64,64]{2,1,0:T(8,128)S(1)}, f32[2,64,64]{2,1,0:T(8,128)}, u32[]{:S(2)}) copy-start(f32[2,64,64]{2,1,0:T(8,128)} %copy-done.18) | copy-start | bytes 98308
  599.8 11.3 %copy-start.26 = (f32[2,64,64]{2,1,0:T(8,128)S(1)}, f32[2,64,64]{2,1,0:T(8,128)}, u32[]{:S(2)}) copy-start(f32[2,64,64]{2,1,0:T(8,128)} %copy-done.25) | copy-start | bytes 98308
  599.8 11.3 %copy-start.28 = (pred[64,64]{1,0:T(8,128)(4,1)S(1)}, pred[64,64]{1,0:T(8,128)(4,1)}, u32[]{:S(2)}) copy-start(pred[64,64]{1,0:T(8,128)(4,1)} %copy-done.27) | copy-start | bytes 12292
  632.0 5.4 copy-start.17
  634.6 4.5 copy-start.22
  634.6 4.7 copy-start.4
  639.3 6.1 copy-start.10
  641.6 7.4 %copy-start.14 = (f32[3,2,64,64]{3,2,1,0:T(8,128)S(1)}, f32[3,2,64,64]{3,2,1,0:T(8,128)}, u32[]{:S(2)}) copy-start(f32[3,2,64,64]{3,2,1,0:T(8,128)} %get-tuple-element.31) | copy-start | bytes 294916
  645.4 5.3 copy-start.8
  647.6 7.6 %copy-start.6 = (f32[2,3,64,1024]{3,2,0,1:T(8,128)S(1)}, f32[2,3,64,1024]{3,2,0,1:T(8,128)}, u32[]{:S(2)}) copy-start(f32[2,3,64,1024]{3,2,0,1:T(8,128)} %get-tuple-element.24) | copy-start | bytes 4718596
  (4 other events, 4.4 us)
Sparse Core Ops, SparseCore 0:
  9.3 30.5 all-gather.4
  41.5 80.7 all-gather.6
  124.2 35.9 all-gather.8
where the time goes:
time: 675 us; the launch traced here: 666 us
  other arithmetic  295 us (44%)
  matrix products  140 us (21%)
  waiting for transfers between devices  123 us (18%)
  local copies, waits for them, and re-layouts  75.1 us (11%)
  between operations  20.8 us (3%)
  blocking collectives  13.1 us (2%)
    another operation x30, other arithmetic, on_device(): lower_factor = jnp.linalg.cholesky(primal)  172 us
    another operation x3, other arithmetic, inverse_apply(): jax.scipy.linalg.solve_triangular(lower_factor, half_solved, lower=True,...  84.7 us
    all_gather x1, waiting for transfers between devices, on_device(): lax.all_gather(panel_rows, 'col', axis=3, tiled=True)  77.2 us
    dot_general x48, matrix products, highest_accuracy(): jnp.dot(left, right, precision=HIGHEST_PRECISION, preferred_element_type=...  71.7 us
    all_gather x1, waiting for transfers between devices, on_device(): primal = lax.all_gather(diag[0], 'row', axis=0, tiled=True)  29.1 us
    another operation x24, local copies, waits for them, and re-layouts  28.6 us
    another operation x14, matrix products, on_device(): lower_factor = jnp.linalg.cholesky(primal)  22.9 us
    another operation x30, matrix products, inverse_apply(): jax.scipy.linalg.solve_triangular(lower_factor, rank_rows.T, lower=True)  17.8 us
  transfers between devices with their start and end apart: 3, of which 3 were waited for; matrix products, arithmetic and copies ran while one was open for 4% of the time, Pallas kernels for 0%

commit v1 on v0

v1 whole, which is shorter than its diff:
```python
import functools
import math

import jax
import jax.numpy as jnp
from jax import lax
from jax.experimental import pallas as pl
from jax.experimental.pallas import tpu as pltpu
from jax.sharding import PartitionSpec as P

HIGHEST = lax.Precision.HIGHEST
F32 = jnp.float32
BF16 = jnp.bfloat16
BLOCK = 128
SUB = 8
VMEM_LIMIT = 48 * 1024 * 1024

NN = (((1,), (0,)), ((), ()))
NT = (((1,), (1,)), ((), ()))


def mm(left, right, dims=NN):
    return lax.dot_general(left, right, dims, precision=HIGHEST, preferred_element_type=F32)


def split3(x):
    hi = x.astype(BF16)
    rest = x - hi.astype(F32)
    mid = rest.astype(BF16)
    lo = (rest - mid.astype(F32)).astype(BF16)
    return hi, mid, lo


def left_terms(x):
    hi, mid, lo = split3(x)
    return jnp.concatenate([hi, hi, mid, mid, hi, lo], axis=1)


def right_terms(x):
    hi, mid, lo = split3(x)
    return jnp.concatenate([hi, mid, hi, mid, lo, hi], axis=0)


def lane_rep(x, lane):
    return jnp.broadcast_to(x[:, lane : lane + 1], (SUB, BLOCK))


def sub_rep(x, row):
    return jnp.broadcast_to(x[row : row + 1, :], (SUB, BLOCK))


def tree_sum(terms):
    while len(terms) > 1:
        terms = [
            terms[i] + terms[i + 1] if i + 1 < len(terms) else terms[i]
            for i in range(0, len(terms), 2)
        ]
    return terms[0]


def sub_index():
    return lax.broadcasted_iota(jnp.int32, (SUB, BLOCK), 0)


def lane_index():
    return lax.broadcasted_iota(jnp.int32, (SUB, BLOCK), 1)


def micro_inverse(cols, want_factor):
    sub = sub_index()
    low = None
    pivots = jnp.zeros((SUB, BLOCK), F32)
    if want_factor:
        low = [jnp.where(sub == k, 1.0, 0.0) for k in range(SUB)]
    for j in range(SUB):
        here = sub == j
        piv = sub_rep(cols[j], j)
        inv_piv = 1.0 / piv
        factor = jnp.where(here, -1.0, cols[j])
        if want_factor:
            pivots = jnp.where(here, piv, pivots)
            below = jnp.where(sub > j, cols[j], 0.0)
            for k in range(j + 1):
                low[k] = low[k] - below * (sub_rep(low[k], j) * inv_piv)
        fresh = []
        for k in range(SUB):
            if k == j:
                fresh.append(-factor * inv_piv)
            else:
                row = sub_rep(cols[k], j) * inv_piv
                fresh.append(jnp.where(here, 0.0, cols[k]) - factor * row)
        cols = fresh
    if want_factor:
        scale = lax.rsqrt(pivots)
        return cols, [scale * c for c in low]
    return cols, None


def block_inverse(rows):
    rows = list(rows)
    count = len(rows)
    sub, lane = sub_index(), lane_index()
    for g in range(count):
        at = g * SUB
        inside = (lane >= at) & (lane < at + SUB)
        inv, _ = micro_inverse([lane_rep(rows[g], at + k) for k in range(SUB)], False)
        own = jnp.where(inside, jnp.where(lane - at == sub, 1.0, 0.0), rows[g])
        new = tree_sum([inv[k] * sub_rep(own, k) for k in range(SUB)])
        news = [sub_rep(new, k) for k in range(SUB)]
        order = [(g + 1 + i) % count for i in range(count - 1)]
        for i in order:
            kept = jnp.where(inside, 0.0, rows[i])
            rows[i] = kept - tree_sum([lane_rep(rows[i], at + k) * news[k] for k in range(SUB)])
        rows[g] = new
    return rows


def factor_inverse(rows, width):
    rows = list(rows)
    count = width // SUB
    for g in range(count):
        at = g * SUB
        inv, low = micro_inverse([lane_rep(rows[g], at + k) for k in range(SUB)], True)
        own = rows[g]
        own_rep = [sub_rep(own, k) for k in range(SUB)]
        new = tree_sum([inv[k] * own_rep[k] for k in range(SUB)])
        news = [sub_rep(new, k) for k in range(SUB)]
        for i in range(g + 1, count):
            rows[i] = rows[i] - tree_sum(
                [lane_rep(rows[i], at + k) * news[k] for k in range(SUB)]
            )
        rows[g] = tree_sum([low[k] * own_rep[k] for k in range(SUB)])
    return rows


def as_rows(x):
    return [x[i * SUB : (i + 1) * SUB, :] for i in range(x.shape[0] // SUB)]


def inverse_kernel(
    own_rows, gathered, col_rank, tangents, inverse, solved, products, pivot, left, right
):
    size = inverse.shape[0]
    steps = size // BLOCK
    shards = gathered.shape[0]

    def copy_in(r, _):
        inverse[pl.ds(pl.multiple_of(r * own_rows, own_rows), own_rows), :] = gathered[
            r, pl.ds(0, own_rows), :
        ]
        return _

    lax.fori_loop(0, shards, copy_in, 0)

    def invert_to_pivot(block):
        pivot[...] = jnp.concatenate(block_inverse(as_rows(block)), axis=0)

    def prepare(k):
        at = pl.ds(pl.multiple_of(k * BLOCK, BLOCK), BLOCK)
        inv = pivot[...]
        column = inverse[:, at]
        row = mm(inv, inverse[at, :])
        left[...] = left_terms(column)
        right[...] = right_terms(row)
        right[:, at] = right_terms(inv)
        inverse[:, at] = jnp.zeros((size, BLOCK), F32)
        return at, row, inv

    def update(at, row, inv):
        chunk = 256
        for c in range(size // chunk):
            part = slice(c * chunk, (c + 1) * chunk)
            inverse[part, :] = inverse[part, :] - lax.dot_general(
                left[part, :], right[...], NN, preferred_element_type=F32
            )
        inverse[at, :] = row
        inverse[at, at] = inv

    invert_to_pivot(inverse[:BLOCK, :BLOCK])

    def step(k, carry):
        nxt = pl.ds(pl.multiple_of((k + 1) * BLOCK, BLOCK), BLOCK)
        block = inverse[nxt, nxt]
        at, row, inv = prepare(k)
        block = block - lax.dot_general(
            left[nxt, :], right[:, nxt], NN, preferred_element_type=F32
        )
        update(at, row, inv)
        invert_to_pivot(block)
        return carry

    lax.fori_loop(0, steps - 1, step, 0)
    update(*prepare(steps - 1))

    rank_count = solved.shape[0]
    own_ranks = rank_count // shards
    values = jnp.concatenate(
        [gathered[r, own_rows : own_rows + own_ranks, :] for r in range(shards)], axis=0
    )
    live = lax.broadcasted_iota(jnp.int32, values.shape, 0) < col_rank[0]
    values = jnp.where(live, values, 0.0)
    z = mm(values, inverse[...])
    solved[...] = z
    for t in range(3):
        products[t] = mm(z, tangents[t], NT)


def run_inverse(gathered, tangents, col_rank, own_rows):
    shards, _, size = gathered.shape
    rank_count = (gathered.shape[1] - own_rows) * shards
    vmem = pl.BlockSpec(memory_space=pltpu.VMEM)
    return pl.pallas_call(
        functools.partial(inverse_kernel, own_rows),
        out_shape=(
            jax.ShapeDtypeStruct((size, size), F32),
            jax.ShapeDtypeStruct((rank_count, size), F32),
            jax.ShapeDtypeStruct((3, rank_count, own_rows), F32),
        ),
        in_specs=[vmem, pl.BlockSpec(memory_space=pltpu.SMEM), vmem],
        out_specs=(vmem, vmem, vmem),
        scratch_shapes=[
            pltpu.VMEM((BLOCK, BLOCK), F32),
            pltpu.VMEM((size, 6 * BLOCK), BF16),
            pltpu.VMEM((6 * BLOCK, size), BF16),
        ],
        compiler_params=pltpu.CompilerParams(vmem_limit_bytes=VMEM_LIMIT),
        cost_estimate=pl.CostEstimate(
            flops=40 * 10**9, bytes_accessed=10 * 2**20, transcendentals=0
        ),
        name="inverse",
    )(gathered, col_rank, tangents)


def row_mask(shape, rank):
    return lax.broadcasted_iota(jnp.int32, shape, 0) < rank


def load_rows(own_ref, shard_refs, position, p, comp, rank):
    count = 1 + len(shard_refs)
    own = own_ref[p, comp]
    parts = [own] + [ref[p, comp] for ref in shard_refs]
    pieces = []
    for j in range(count):
        piece = parts[0]
        for s in range(1, count):
            piece = jnp.where(lax.rem(position - s + count, count) == j, parts[s], piece)
        pieces.append(piece)
    whole = jnp.concatenate(pieces, axis=1)
    return jnp.where(row_mask(whole.shape, rank), whole, 0.0)


def load_cols(ref, comp, rank):
    groups = ref.shape[0]
    whole = jnp.concatenate([ref[g, comp] for g in range(groups)], axis=0)
    return jnp.where(row_mask(whole.shape, rank), whole, 0.0)


def primal_kernel(
    tiles,
    shards,
    place,
    panel_rank,
    col_rank,
    tile_rank,
    keep_rank,
    *refs,
):
    row_refs = refs[:shards]
    cols, trailing, sketch, solved = refs[shards : shards + 4]
    basis, coeffs, mixes, factors = refs[shards + 4 :]
    rank_count, size = sketch.shape
    position = place[0]
    z = solved[...]
    u_col = load_cols(cols, 0, col_rank[0])
    s = sketch[...]
    su_all = mm(s, u_col, NT)
    keep = []
    augmented = []
    for p in range(tiles):
        live = lax.broadcasted_iota(jnp.int32, (rank_count, 1), 0) < keep_rank[p, 0]
        u_row = load_rows(row_refs[0], row_refs[1:], position, p, 0, panel_rank[p])
        v_row = load_rows(row_refs[0], row_refs[1:], position, p, 1, panel_rank[p])
        old = row_mask((rank_count, size), tile_rank[p, 0])
        u_old = jnp.where(old, trailing[p, 0, 0], 0.0)
        v_old = jnp.where(old, trailing[p, 0, 4], 0.0)
        mix = mm(v_row, z, NT)
        su = jnp.where(live, su_all, 0.0)
        sv = jnp.where(live, mm(s, v_old, NT), 0.0)
        y = mm(sv, u_old) - mm(mm(su, mix, NT), u_row)
        gram = mm(y, y, NT)
        eye = lax.broadcasted_iota(jnp.int32, gram.shape, 0) == lax.broadcasted_iota(
            jnp.int32, gram.shape, 1
        )
        gram = gram + jnp.where(eye & jnp.logical_not(live), 1.0, 0.0)
        augmented.append(jnp.concatenate([gram, jnp.where(eye, 1.0, 0.0)], axis=1))
        keep.append((y, u_row, u_old, v_old, mix))
    inverses = [factor_inverse(as_rows(a), rank_count) for a in augmented]
    for p in range(tiles):
        y, u_row, u_old, v_old, mix = keep[p]
        rinv = jnp.concatenate(inverses[p], axis=0)[:, rank_count:]
        q = mm(rinv, y)
        b = mm(mm(q, u_old, NT), v_old) - mm(mm(mm(q, u_row, NT), mix), u_col)
        basis[p] = q
        coeffs[p] = b
        mixes[p] = mix
        factors[p] = rinv


def run_primal(place, ranks, row_shards, cols, trailing, sketch, solved):
    tiles = trailing.shape[0]
    rank_count, size = sketch.shape
    vmem = pl.BlockSpec(memory_space=pltpu.VMEM)
    smem = pl.BlockSpec(memory_space=pltpu.SMEM)
    big = jax.ShapeDtypeStruct((tiles, rank_count, size), F32)
    small = jax.ShapeDtypeStruct((tiles, rank_count, rank_count), F32)
    return pl.pallas_call(
        functools.partial(primal_kernel, tiles, len(row_shards)),
        out_shape=(big, big, small, small),
        in_specs=[smem] * 5 + [vmem] * (len(row_shards) + 4),
        out_specs=(vmem,) * 4,
        compiler_params=pltpu.CompilerParams(vmem_limit_bytes=VMEM_LIMIT),
        cost_estimate=pl.CostEstimate(
            flops=5 * 10**9, bytes_accessed=8 * 2**20, transcendentals=0
        ),
        name="primal",
    )(place, *ranks, *row_shards, cols, trailing, sketch, solved)


def tangent_kernel(
    tiles,
    shards,
    place,
    panel_rank,
    col_rank,
    tile_rank,
    keep_rank,
    *refs,
):
    row_refs = refs[:shards]
    tan_refs = refs[shards : 2 * shards]
    cols, trailing, sketch, solved, inverse, products, basis, coeffs, mixes, factors = refs[
        2 * shards : 2 * shards + 10
    ]
    (out,) = refs[2 * shards + 10 :]
    rank_count, size = sketch.shape
    up_scale = math.sqrt(size)
    down_scale = 1.0 / math.sqrt(rank_count)
    position = place[0]
    z = solved[...]
    u_col = [load_cols(cols, t, col_rank[0]) for t in range(4)]
    sides = []
    for t in range(3):
        whole = jnp.concatenate([products[r, t] for r in range(products.shape[0])], axis=1)
        sides.append(load_cols(cols, 5 + t, col_rank[0]) - whole)
    dz = mm(jnp.concatenate(sides, axis=0), inverse[...])
    s = sketch[...]
    su_all = mm(s, jnp.concatenate(u_col, axis=0), NT)
    for p in range(tiles):
        live = lax.broadcasted_iota(jnp.int32, (rank_count, 1), 0) < keep_rank[p, 0]
        load = functools.partial(load_rows, position=position, p=p, rank=panel_rank[p])
        u_row = [load(row_refs[0], row_refs[1:], comp=0)]
        v_row = load(row_refs[0], row_refs[1:], comp=1)
        u_row += [load(tan_refs[0], tan_refs[1:], comp=t) for t in range(3)]
        dv_row = jnp.concatenate(
            [load(tan_refs[0], tan_refs[1:], comp=3 + t) for t in range(3)], axis=0
        )
        old = row_mask((rank_count, size), tile_rank[p, 0])
        u_old = [jnp.where(old, trailing[p, 0, t], 0.0) for t in range(4)]
        v_old = [jnp.where(old, trailing[p, 0, 4 + t], 0.0) for t in range(4)]
        q, mix, rinv = basis[p], mixes[p], factors[p]
        dv_z = mm(dv_row, z, NT)
        v_dz = mm(v_row, dz, NT)
        su_p = jnp.where(live, su_all, 0.0)
        sv_p = jnp.where(live, mm(s, jnp.concatenate(v_old, axis=0), NT), 0.0)
        part = lambda x, t: x[:, t * rank_count : (t + 1) * rank_count]
        base_v = mm(rinv, part(sv_p, 0))
        base_u = mm(rinv, mm(part(su_p, 0), mix, NT))
        q_parts = mm(q, jnp.concatenate(u_old + u_row, axis=0), NT)
        q_mix = mm(part(q_parts, 4), mix)
        out[p, 0, 0] = q * up_scale
        out[p, 0, 4] = coeffs[p] * down_scale
        for t in range(3):
            dmix = dv_z[t * rank_count : (t + 1) * rank_count] + part(v_dz, t)
            u_side = mm(part(su_p, t + 1), mix, NT) + mm(part(su_p, 0), dmix, NT)
            left = jnp.concatenate(
                [mm(rinv, part(sv_p, t + 1)), base_v, -mm(rinv, u_side), -base_u], axis=1
            )
            right = jnp.concatenate([u_old[0], u_old[t + 1], u_row[0], u_row[t + 1]], axis=0)
            e = mm(left, right)
            cross = mm(e, q, NT)
            sym = cross + mm(q, e, NT)
            i0 = lax.broadcasted_iota(jnp.int32, sym.shape, 0)
            i1 = lax.broadcasted_iota(jnp.int32, sym.shape, 1)
            phi = jnp.where(i0 > i1, sym, jnp.where(i0 == i1, 0.5 * sym, 0.0))
            dq = e - mm(phi, q)
            dq_parts = mm(dq, jnp.concatenate([u_old[0], u_row[0]], axis=0), NT)
            on_v = part(dq_parts, 0) + part(q_parts, t + 1)
            on_u = mm(part(dq_parts, 1) + part(q_parts, 5 + t), mix) + mm(part(q_parts, 4), dmix)
            left = jnp.concatenate([on_v, part(q_parts, 0), -on_u, -q_mix], axis=1)
            right = jnp.concatenate([v_old[0], v_old[t + 1], u_col[0], u_col[t + 1]], axis=0)
            out[p, 0, 1 + t] = dq * up_scale
            out[p, 0, 5 + t] = mm(left, right) * down_scale


def run_tangent(
    place, ranks, row_shards, tan_shards, cols, trailing, sketch, solved, inverse, products, primal
):
    vmem = pl.BlockSpec(memory_space=pltpu.VMEM)
    smem = pl.BlockSpec(memory_space=pltpu.SMEM)
    return pl.pallas_call(
        functools.partial(tangent_kernel, trailing.shape[0], len(row_shards)),
        out_shape=jax.ShapeDtypeStruct(trailing.shape, F32),
        in_specs=[smem] * 5 + [vmem] * (2 * len(row_shards) + 6 + len(primal)),
        out_specs=vmem,
        compiler_params=pltpu.CompilerParams(vmem_limit_bytes=VMEM_LIMIT),
        cost_estimate=pl.CostEstimate(
            flops=10 * 10**9, bytes_accessed=20 * 2**20, transcendentals=0
        ),
        name="tangent",
    )(place, *ranks, *row_shards, *tan_shards, cols, trailing, sketch, solved, inverse, products, *primal)


def on_device(
    row_count,
    col_count,
    diag,
    panel_rows,
    panel_cols,
    trailing,
    sketch,
    panel_rank,
    col_rank,
    tile_rank,
    keep_rank,
):
    own_rows = diag.shape[1]
    own_ranks = panel_cols.shape[2]
    comps = panel_cols.shape[1]
    size = sketch.shape[1]
    gathered = lax.all_gather(
        jnp.concatenate([diag[0], panel_cols[0, 4]], axis=0), "row", axis=0
    )
    first = panel_rows[:, 0::4]
    second = jnp.concatenate([panel_rows[:, 1:4], panel_rows[:, 5:8]], axis=1)
    first_shards, second_shards = [first], [second]
    for source, shards in ((first, first_shards), (second, second_shards)):
        for s in range(1, col_count):
            shards.append(
                lax.ppermute(source, "col", [(i, (i + s) % col_count) for i in range(col_count)])
            )
    late_cols, gathered = lax.optimization_barrier((panel_cols[0], gathered))
    cols = lax.all_gather(late_cols, "row", axis=0)
    if own_ranks != SUB:
        cols = cols.reshape(-1, SUB // own_ranks, comps, own_ranks, size)
        cols = cols.transpose(0, 2, 1, 3, 4).reshape(-1, comps, SUB, size)
    inverse, solved, products = run_inverse(gathered, diag[1:], col_rank, own_rows)
    all_products = lax.all_gather(products, "row", axis=0)
    place = lax.axis_index("col").astype(jnp.int32).reshape(1)
    ranks = (panel_rank, col_rank, tile_rank, keep_rank)
    primal = run_primal(place, ranks, first_shards, cols, trailing, sketch, solved)
    return run_tangent(
        place,
        ranks,
        first_shards,
        second_shards,
        cols,
        trailing,
        sketch,
        solved,
        inverse,
        all_products,
        primal,
    )


def solution(mesh):
    in_specs = (
        P(None, "row", None),
        P("row", None, None, "col"),
        P("col", None, "row", None),
        P("row", "col", None, None, None),
        P(),
        P("row"),
        P("col"),
        P("row", "col"),
        P("row", "col"),
    )
    out_specs = P("row", "col", None, None, None)
    body = functools.partial(on_device, mesh.shape["row"], mesh.shape["col"])
    return jax.shard_map(body, mesh=mesh, in_specs=in_specs, out_specs=out_specs, check_vma=False)
```

time: 675 us -> 196 us (0.29); the launches traced: 666 us -> 194 us
  other arithmetic: 295 us -> 0.92 us
  matrix products: 140 us -> 0 us
  Pallas kernels: 0 us -> 119 us
  waiting for transfers between devices: 123 us -> 27.2 us
  local copies, waits for them, and re-layouts: 75.1 us -> 10 us
  starting transfers between devices: 0.11 us -> 11.7 us
    another operation x40 -> x0, other arithmetic: 279 us -> none  [the longest x30 172 us: on_device(): lower_factor = jnp.linalg.cholesky(primal)]
    pallas_call x0 -> x3, Pallas kernels: none -> 119 us  [the longest x1 62.9 us: run_inverse(): pl.pallas_call(functools.partial(inverse_kernel, own_rows), out_shape=(ja...]
    all_gather x3 -> x2, waiting for transfers between devices: 122 us -> 27.1 us  [the longest x1 27.1 us: on_device(): lax.all_gather(jnp.concatenate([diag[0], panel_cols[0, 4]], axis=0), 'row...]
    dot_general x49 -> x0, matrix products: 75.3 us -> none  [the longest x48 71.7 us: highest_accuracy(): jnp.dot(left, right, precision=HIGHEST_PRECISION, preferred_element_type=...]
    another operation x78 -> x0, matrix products: 64.5 us -> none  [the longest x14 22.9 us: on_device(): lower_factor = jnp.linalg.cholesky(primal)]
    another operation x45 -> x0, local copies, waits for them, and re-layouts: 35.9 us -> none
    ppermute x0 -> x6, starting transfers between devices: none -> 11.6 us  [on_device(): lax.ppermute(source, 'col', [(i, (i + s) % col_count) for i in range(col_...]
    mul x3 -> x0, other arithmetic: 7.71 us -> none  [the longest x1 3.15 us: update_tile(): old_tile = old_tile * tile_mask[None, :, None]]
  transfers between devices with their start and end apart: 3 -> 8, of which waited for: 3 -> 1; matrix products, arithmetic and copies ran while one was open for 4% -> 1% of each run, Pallas kernels for 0% -> 38%
where the time goes in v1:
time: 196 us; the launch traced here: 194 us
  Pallas kernels  119 us (61%)
  waiting for transfers between devices  27.2 us (14%)
  between operations  14.4 us (7%)
  starting transfers between devices  11.7 us (6%)
  blocking collectives  11.3 us (6%)
  local copies, waits for them, and re-layouts  10 us (5%)
    pallas_call x1, Pallas kernels, run_inverse(): pl.pallas_call(functools.partial(inverse_kernel, own_rows), out_shape=(ja...  62.9 us
    pallas_call x1, Pallas kernels, run_tangent(): pl.pallas_call(functools.partial(tangent_kernel, trailing.shape[0], len(r...  45.4 us
    all_gather x1, waiting for transfers between devices, on_device(): lax.all_gather(jnp.concatenate([diag[0], panel_cols[0, 4]], axis=0), 'row...  27.1 us
    ppermute x6, starting transfers between devices, on_device(): lax.ppermute(source, 'col', [(i, (i + s) % col_count) for i in range(col_...  11.6 us
    all_gather x1, blocking collectives, on_device(): all_products = lax.all_gather(products, 'row', axis=0)  11.3 us
    pallas_call x1, Pallas kernels, run_primal(): pl.pallas_call(functools.partial(primal_kernel, tiles, len(row_shards)),...  10.6 us
    unnamed x20, local copies, waits for them, and re-layouts  5.74 us
  transfers between devices with their start and end apart: 8, of which 1 were waited for; matrix products, arithmetic and copies ran while one was open for 1% of the time, Pallas kernels for 38%

profile of v1, /device:TPU:0, one launch (start us, length us, event | category | flops | bytes accessed | tf_op | source)
XLA Modules:
  0.0 194.4 jit_solution(1433806606886203117)
XLA Ops:
  6.5 0.8 slice_bitcast_fusion.1
  7.3 1.1 slice_bitcast_fusion
  8.4 0.0 copy-start.7
  8.4 0.0 copy-start.8
  8.4 0.8 pad_maximum_fusion.1
  9.2 0.0 all-gather.6.cloned.1.call-update
  9.3 0.0 all-gather.8.cloned.1.call-start
  9.3 0.0 copy-start.6
  9.3 1.1 slice.18.refs_0_
  10.5 5.1 %collective-permute-start.2 = (f32[2,2,64,256]{3,2,1,0:T(8,128)S(1)}, f32[2,2,64,256]{3,2,1,0:T(8,128)}, u32[]{:S(2)}, u32[]{:S(2)}) collective-permute-start(f32[2,2,64,256]{3,2,1,0:T(8,128)S(1)} %slice.18.refs_0_), channel_id=1, source_target_pairs={{0,3},{1,0},{2,1},{3,2},{4,7},{5,4},{6,5},{7,6},{8,11},{9,8},{10,9... | collective-permute-start | bytes 786440 | tf_op jit(solution)/shard_map/ppermute | solution.py:449
  15.6 1.0 collective-permute-start
  16.6 1.2 fusion
  17.7 0.1 pad_maximum_fusion.refs_4_
  17.8 2.9 %collective-permute-start.5 = (f32[2,6,64,256]{3,2,1,0:T(8,128)S(1)}, f32[2,6,64,256]{3,2,1,0:T(8,128)S(1)}, u32[]{:S(2)}, u32[]{:S(2)}) collective-permute-start(f32[2,6,64,256]{3,2,1,0:T(8,128)S(1)} %pad_maximum_fusion.refs_4_), channel_id=1, source_target_pairs={{0,3},{1,0},{2,1},{3,2},{4,7},{5,4},{6,5},{7,6},{8,11},{9,8},{10,9... | collective-permute-start | bytes 2359304 | tf_op jit(solution)/shard_map/ppermute | solution.py:449
  20.7 1.1 collective-permute-start.4
  21.8 0.2 slice.23.tangents
  22.7 0.1 copy.16.tile_rank
  22.8 0.1 copy.17.keep_rank
  22.8 27.1 %all-gather.6.cloned.1.call-done = f32[1088,1024]{1,0:T(8,128)} async-done(((f32[136,1024]{1,0:T(8,128)}), f32[1088,1024]{1,0:T(8,128)}) %all-gather.6.cloned.1.call-update) | async-done | bytes 4456464 | tf_op jit(solution)/shard_map/all_gather | solution.py:440
  49.9 0.0 all-gather.8.cloned.1.call-update
  50.0 0.0 copy-start.2
  50.0 1.5 collective-permute-start.3
  51.5 62.9 %inverse.1 = (f32[1024,1024]{1,0:T(8,128)S(1)}, f32[64,1024]{1,0:T(8,128)S(1)}, f32[3,64,128]{2,1,0:T(8,128)S(1)}) custom-call(f32[8,136,1024]{2,1,0:T(8,128)} %bitcast.13, s32[1]{0:T(128)S(6)} %copy.18.col_rank, f32[3,128,1024]{2,1,0:T(8,128)S(1)} %slice.23.tangents), custom_call_target="tpu_custom_call" | custom-call | flops 40000000000 | bytes 10485760 | tf_op jit(solution)/shard_map/inverse/pallas_call | solution.py:212
  114.4 0.0 copy-start.3
  114.4 2.0 %copy-done.3 = f32[1024,1024]{1,0:T(8,128)} copy-done((f32[1024,1024]{1,0:T(8,128)}, f32[1024,1024]{1,0:T(8,128)S(1)}, u32[]{:S(2)}) %copy-start.3) | copy-done | bytes 4194328
  116.4 11.3 %all-gather.2 = f32[24,64,128]{2,1,0:T(8,128)} all-gather(f32[3,64,128]{2,1,0:T(8,128)S(1)} %get-tuple-element.18), channel_id=4, replica_groups=mesh['row'=8,'col'=4] {'row'}, dimensions={0}, use_global_device_ids=true | all-gather | bytes 884736 | tf_op jit(solution)/shard_map/all_gather | solution.py:457
  127.8 0.0 all-gather.8.cloned.1.call-done
  127.8 1.6 copy-done
  129.4 0.9 copy-done.1
  130.4 0.9 copy-done.5
  131.3 10.6 %primal.1 = (f32[2,64,1024]{2,1,0:T(8,128)S(1)}, f32[2,64,1024]{2,1,0:T(8,128)S(1)}, f32[2,64,64]{2,1,0:T(8,128)S(1)}, f32[2,64,64]{2,1,0:T(8,128)S(1)}) custom-call(s32[1]{0:T(128)} %bitcast.place, s32[2]{0:T(128)S(1)} %copy-done.2, s32[1]{0:T(128)S(6)} %copy.18.col_rank, s32[2,1]{1,0:T(2,128)S(1)} %copy.16.tile_rank, s32[2,1]{1,0:T(2,128)S(1)} %copy.17.keep_rank, ...), custom_call_target="tpu_custom_call" | custom-call | flops 5000000000 | bytes 8388608 | tf_op jit(solution)/shard_map/primal/pallas_call | solution.py:316
  142.0 45.4 %tangent.1 = f32[2,1,8,64,1024]{4,3,2,1,0:T(8,128)} custom-call(s32[1]{0:T(128)} %bitcast.place, s32[2]{0:T(128)S(1)} %copy-done.2, s32[1]{0:T(128)S(6)} %copy.18.col_rank, s32[2,1]{1,0:T(2,128)S(1)} %copy.16.tile_rank, s32[2,1]{1,0:T(2,128)S(1)} %copy.17.keep_rank, f32[2,2,64,256]{3,2,1,0:T(8,128)S(1)} %slice.18.refs_0_, ...), custom_call_target="tpu_custom_call" | custom-call | flops 10000000000 | bytes 20971520 | tf_op jit(solution)/shard_map/tangent/pallas_call | solution.py:410
  (17 shorter events, 0.0 us)
Async XLA Ops:
  6.5 43.4 %all-gather.6.cloned.1.call-start = ((), (), s32[]{:S(2)}) async-start(), calls=%async_computation | async-start | bytes 5013504 | tf_op jit(solution)/shard_map/all_gather | solution.py:440
  8.4 14.3 %copy-start.7 = (s32[2,1]{0,1:T(1,128)S(1)}, s32[2,1]{0,1:T(1,128)}, u32[]{:S(2)}) copy-start(s32[2,1]{0,1:T(1,128)} %param.16) | copy-start | bytes 28
  8.4 14.4 %copy-start.8 = (s32[2,1]{0,1:T(1,128)S(1)}, s32[2,1]{0,1:T(1,128)}, u32[]{:S(2)}) copy-start(s32[2,1]{0,1:T(1,128)} %param.17) | copy-start | bytes 28
  9.3 118.5 %all-gather.8.cloned.1.call-start = ((), (), s32[]{:S(2)}) async-start(), calls=%async_computation.1 | async-start | bytes 2359296 | tf_op jit(solution)/shard_map/all_gather | solution.py:452
  9.3 12.5 %copy-start.6 = (f32[4,128,1024]{2,1,0:T(8,128)S(1)}, f32[4,128,1024]{2,1,0:T(8,128)}, u32[]{:S(2)}) copy-start(f32[4,128,1024]{2,1,0:T(8,128)} %param.9) | copy-start | bytes 6291460
  10.5 39.5 %collective-permute-start.2 = (f32[2,2,64,256]{3,2,1,0:T(8,128)S(1)}, f32[2,2,64,256]{3,2,1,0:T(8,128)}, u32[]{:S(2)}, u32[]{:S(2)}) collective-permute-start(f32[2,2,64,256]{3,2,1,0:T(8,128)S(1)} %slice.18.refs_0_), channel_id=1, source_target_pairs={{0,3},{1,0},{2,1},{3,2},{4,7},{5,4},{6,5},{7,6},{8,11},{9,8},{10,9... | collective-permute-start | bytes 786440 | tf_op jit(solution)/shard_map/ppermute | solution.py:449
  15.6 112.2 %collective-permute-start.1 = (f32[2,2,64,256]{3,2,1,0:T(8,128)S(1)}, f32[2,2,64,256]{3,2,1,0:T(8,128)}, u32[]{:S(2)}, u32[]{:S(2)}) collective-permute-start(f32[2,2,64,256]{3,2,1,0:T(8,128)S(1)} %slice.18.refs_0_), channel_id=1, source_target_pairs={{0,2},{1,3},{2,0},{3,1},{4,6},{5,7},{6,4},{7,5},{8,10},{9,11},{10,... | collective-permute-start | bytes 786440 | tf_op jit(solution)/shard_map/ppermute | solution.py:449
  15.6 112.2 %collective-permute-start = (f32[2,2,64,256]{3,2,1,0:T(8,128)S(1)}, f32[2,2,64,256]{3,2,1,0:T(8,128)}, u32[]{:S(2)}, u32[]{:S(2)}) collective-permute-start(f32[2,2,64,256]{3,2,1,0:T(8,128)S(1)} %slice.18.refs_0_), channel_id=1, source_target_pairs={{0,1},{1,2},{2,3},{3,0},{4,5},{5,6},{6,7},{7,4},{8,9},{9,10},{10,1... | collective-permute-start | bytes 786440 | tf_op jit(solution)/shard_map/ppermute | solution.py:449
  17.8 124.1 %collective-permute-start.5 = (f32[2,6,64,256]{3,2,1,0:T(8,128)S(1)}, f32[2,6,64,256]{3,2,1,0:T(8,128)S(1)}, u32[]{:S(2)}, u32[]{:S(2)}) collective-permute-start(f32[2,6,64,256]{3,2,1,0:T(8,128)S(1)} %pad_maximum_fusion.refs_4_), channel_id=1, source_target_pairs={{0,3},{1,0},{2,1},{3,2},{4,7},{5,4},{6,5},{7,6},{8,11},{9,8},{10,9... | collective-permute-start | bytes 2359304 | tf_op jit(solution)/shard_map/ppermute | solution.py:449
  20.7 121.3 %collective-permute-start.4 = (f32[2,6,64,256]{3,2,1,0:T(8,128)S(1)}, f32[2,6,64,256]{3,2,1,0:T(8,128)}, u32[]{:S(2)}, u32[]{:S(2)}) collective-permute-start(f32[2,6,64,256]{3,2,1,0:T(8,128)S(1)} %pad_maximum_fusion.refs_4_), channel_id=1, source_target_pairs={{0,2},{1,3},{2,0},{3,1},{4,6},{5,7},{6,4},{7,5},{8,10},{9,11},{10,... | collective-permute-start | bytes 2359304 | tf_op jit(solution)/shard_map/ppermute | solution.py:449
  50.0 77.8 %copy-start.2 = (s32[2]{0:T(128)S(1)}, s32[2]{0:T(128)}, u32[]{:S(2)}) copy-start(s32[2]{0:T(128)} %panel_rank.3) | copy-start | bytes 28
  50.0 92.0 %collective-permute-start.3 = (f32[2,6,64,256]{3,2,1,0:T(8,128)S(1)}, f32[2,6,64,256]{3,2,1,0:T(8,128)}, u32[]{:S(2)}, u32[]{:S(2)}) collective-permute-start(f32[2,6,64,256]{3,2,1,0:T(8,128)S(1)} %pad_maximum_fusion.refs_4_), channel_id=1, source_target_pairs={{0,1},{1,2},{2,3},{3,0},{4,5},{5,6},{6,7},{7,4},{8,9},{9,10},{10,1... | collective-permute-start | bytes 2359304 | tf_op jit(solution)/shard_map/ppermute | solution.py:449
  114.4 2.1 %copy-start.3 = (f32[1024,1024]{1,0:T(8,128)}, f32[1024,1024]{1,0:T(8,128)S(1)}, u32[]{:S(2)}) copy-start(f32[1024,1024]{1,0:T(8,128)S(1)} %get-tuple-element.17.refs_12_) | copy-start | bytes 12582916
  116.4 11.3 %copy-start.4 = (f32[64,1024]{1,0:T(8,128)}, f32[64,1024]{1,0:T(8,128)S(1)}, u32[]{:S(2)}) copy-start(f32[64,1024]{1,0:T(8,128)S(1)} %get-tuple-element.16.refs_7_.refs_11_) | copy-start | bytes 786436
  127.8 1.6 copy-start
  129.4 0.9 copy-start.1
  130.4 0.9 copy-start.5
Sparse Core Ops, SparseCore 0:
  9.4 40.5 all-gather.5
  51.8 27.9 all-gather.7

commit v2 on v1

v2 whole, which is shorter than its diff:
```python
import functools
import math

import jax
import jax.numpy as jnp
from jax import lax
from jax.experimental import pallas as pl
from jax.experimental.pallas import tpu as pltpu
from jax.sharding import PartitionSpec as P

HIGHEST = lax.Precision.HIGHEST
F32 = jnp.float32
BF16 = jnp.bfloat16
BLOCK = 128
SUB = 8
VMEM_LIMIT = 48 * 1024 * 1024

NN = (((1,), (0,)), ((), ()))
NT = (((1,), (1,)), ((), ()))


def mm(left, right, dims=NN):
    return lax.dot_general(left, right, dims, precision=HIGHEST, preferred_element_type=F32)


def split3(x):
    hi = x.astype(BF16)
    rest = x - hi.astype(F32)
    mid = rest.astype(BF16)
    lo = (rest - mid.astype(F32)).astype(BF16)
    return hi, mid, lo


def left_terms(x):
    hi, mid, lo = split3(x)
    return jnp.concatenate([hi, hi, mid, mid, hi, lo], axis=1)


def right_terms(x):
    hi, mid, lo = split3(x)
    return jnp.concatenate([hi, mid, hi, mid, lo, hi], axis=0)


def lane_rep(x, lane):
    return jnp.broadcast_to(x[:, lane : lane + 1], (SUB, BLOCK))


def sub_rep(x, row):
    return jnp.broadcast_to(x[row : row + 1, :], (SUB, BLOCK))


def tree_sum(terms):
    while len(terms) > 1:
        terms = [
            terms[i] + terms[i + 1] if i + 1 < len(terms) else terms[i]
            for i in range(0, len(terms), 2)
        ]
    return terms[0]


def sub_index():
    return lax.broadcasted_iota(jnp.int32, (SUB, BLOCK), 0)


def lane_index():
    return lax.broadcasted_iota(jnp.int32, (SUB, BLOCK), 1)


def micro_inverse(cols):
    sub = sub_index()
    cols = list(cols)
    for j in range(0, SUB, 2):
        first, second = sub == j, sub == j + 1
        pair = first | second
        a, b, d = sub_rep(cols[j], j), sub_rep(cols[j], j + 1), sub_rep(cols[j + 1], j + 1)
        inv_det = 1.0 / (a * d - b * b)
        f0 = jnp.where(first, -1.0, jnp.where(second, 0.0, cols[j]))
        f1 = jnp.where(second, -1.0, jnp.where(first, 0.0, cols[j + 1]))
        fresh = []
        for k in range(SUB):
            if k == j:
                fresh.append((f1 * b - f0 * d) * inv_det)
            elif k == j + 1:
                fresh.append((f0 * b - f1 * a) * inv_det)
            else:
                x0, x1 = sub_rep(cols[k], j), sub_rep(cols[k], j + 1)
                change = f0 * (d * x0 - b * x1) + f1 * (a * x1 - b * x0)
                fresh.append(jnp.where(pair, 0.0, cols[k]) - change * inv_det)
        cols = fresh
    return cols


def micro_factor(cols):
    sub = sub_index()
    cols = list(cols)
    low = [jnp.where(sub == k, 1.0, 0.0) for k in range(SUB)]
    pivots = jnp.zeros((SUB, BLOCK), F32)
    for j in range(SUB):
        here = sub == j
        piv = sub_rep(cols[j], j)
        inv_piv = 1.0 / piv
        factor = jnp.where(here, -1.0, cols[j])
        pivots = jnp.where(here, piv, pivots)
        below = jnp.where(sub > j, cols[j], 0.0)
        for k in range(j + 1):
            low[k] = low[k] - below * sub_rep(low[k], j) * inv_piv
        cols = [
            -factor * inv_piv
            if k == j
            else jnp.where(here, 0.0, cols[k]) - factor * (sub_rep(cols[k], j) * inv_piv)
            for k in range(SUB)
        ]
    scale = lax.rsqrt(pivots)
    return cols, [scale * c for c in low]


def block_inverse(rows):
    rows = list(rows)
    count = len(rows)
    sub, lane = sub_index(), lane_index()
    for g in range(count):
        at = g * SUB
        inside = (lane >= at) & (lane < at + SUB)
        inv = micro_inverse([lane_rep(rows[g], at + k) for k in range(SUB)])
        own = jnp.where(inside, jnp.where(lane - at == sub, 1.0, 0.0), rows[g])
        new = tree_sum([inv[k] * sub_rep(own, k) for k in range(SUB)])
        news = [sub_rep(new, k) for k in range(SUB)]
        order = [(g + 1 + i) % count for i in range(count - 1)]
        for i in order:
            kept = jnp.where(inside, 0.0, rows[i])
            rows[i] = kept - tree_sum([lane_rep(rows[i], at + k) * news[k] for k in range(SUB)])
        rows[g] = new
    return rows


def factor_inverse(rows, width):
    rows = list(rows)
    count = width // SUB
    for g in range(count):
        at = g * SUB
        inv, low = micro_factor([lane_rep(rows[g], at + k) for k in range(SUB)])
        own = rows[g]
        own_rep = [sub_rep(own, k) for k in range(SUB)]
        new = tree_sum([inv[k] * own_rep[k] for k in range(SUB)])
        news = [sub_rep(new, k) for k in range(SUB)]
        for i in range(g + 1, count):
            rows[i] = rows[i] - tree_sum(
                [lane_rep(rows[i], at + k) * news[k] for k in range(SUB)]
            )
        rows[g] = tree_sum([low[k] * own_rep[k] for k in range(SUB)])
    return rows


def as_rows(x):
    return [x[i * SUB : (i + 1) * SUB, :] for i in range(x.shape[0] // SUB)]


def inverse_kernel(
    own_rows,
    gathered,
    col_rank,
    tangents,
    inverse,
    solved,
    products,
    pivot,
    left,
    right,
    scale_row,
    scale_col,
):
    size = inverse.shape[0]
    steps = size // BLOCK
    shards = gathered.shape[0]

    def copy_in(r, _):
        inverse[pl.ds(pl.multiple_of(r * own_rows, own_rows), own_rows), :] = gathered[
            r, pl.ds(0, own_rows), :
        ]
        return _

    lax.fori_loop(0, shards, copy_in, 0)

    eye = lax.broadcasted_iota(jnp.int32, (BLOCK, BLOCK), 0) == lax.broadcasted_iota(
        jnp.int32, (BLOCK, BLOCK), 1
    )
    for c in range(steps):
        part = slice(c * BLOCK, (c + 1) * BLOCK)
        own = jnp.where(eye, inverse[part, part], 0.0)
        scale_row[:, part] = lax.rsqrt(jnp.sum(own, axis=0, keepdims=True))
        scale_col[part, :] = jnp.broadcast_to(
            lax.rsqrt(jnp.sum(own, axis=1, keepdims=True)), (BLOCK, BLOCK)
        )

    def rescale():
        for c in range(steps):
            part = slice(c * BLOCK, (c + 1) * BLOCK)
            col = scale_col[part, :]
            for e in range(steps):
                other = slice(e * BLOCK, (e + 1) * BLOCK)
                inverse[part, other] = inverse[part, other] * col * scale_row[:, other]

    rescale()

    def invert_to_pivot(block):
        pivot[...] = jnp.concatenate(block_inverse(as_rows(block)), axis=0)

    def prepare(k):
        at = pl.ds(pl.multiple_of(k * BLOCK, BLOCK), BLOCK)
        inv = pivot[...]
        column = inverse[:, at]
        row = mm(inv, inverse[at, :])
        left[...] = left_terms(column)
        right[...] = right_terms(row)
        right[:, at] = right_terms(inv)
        inverse[:, at] = jnp.zeros((size, BLOCK), F32)
        return at, row, inv

    def update(at, row, inv):
        chunk = 256
        for c in range(size // chunk):
            part = slice(c * chunk, (c + 1) * chunk)
            inverse[part, :] = inverse[part, :] - lax.dot_general(
                left[part, :], right[...], NN, preferred_element_type=F32
            )
        inverse[at, :] = row
        inverse[at, at] = inv

    invert_to_pivot(inverse[:BLOCK, :BLOCK])

    def step(k, carry):
        nxt = pl.ds(pl.multiple_of((k + 1) * BLOCK, BLOCK), BLOCK)
        block = inverse[nxt, nxt]
        at, row, inv = prepare(k)
        block = block - lax.dot_general(
            left[nxt, :], right[:, nxt], NN, preferred_element_type=F32
        )
        update(at, row, inv)
        invert_to_pivot(block)
        return carry

    lax.fori_loop(0, steps - 1, step, 0)
    update(*prepare(steps - 1))
    rescale()

    rank_count = solved.shape[0]
    own_ranks = rank_count // shards
    values = jnp.concatenate(
        [gathered[r, own_rows : own_rows + own_ranks, :] for r in range(shards)], axis=0
    )
    live = lax.broadcasted_iota(jnp.int32, values.shape, 0) < col_rank[0]
    values = jnp.where(live, values, 0.0)
    z = mm(values, inverse[...])
    solved[...] = z
    for t in range(3):
        products[t] = mm(z, tangents[t], NT)


def run_inverse(gathered, tangents, col_rank, own_rows):
    shards, _, size = gathered.shape
    rank_count = (gathered.shape[1] - own_rows) * shards
    vmem = pl.BlockSpec(memory_space=pltpu.VMEM)
    return pl.pallas_call(
        functools.partial(inverse_kernel, own_rows),
        out_shape=(
            jax.ShapeDtypeStruct((size, size), F32),
            jax.ShapeDtypeStruct((rank_count, size), F32),
            jax.ShapeDtypeStruct((3, rank_count, own_rows), F32),
        ),
        in_specs=[vmem, pl.BlockSpec(memory_space=pltpu.SMEM), vmem],
        out_specs=(vmem, vmem, vmem),
        scratch_shapes=[
            pltpu.VMEM((BLOCK, BLOCK), F32),
            pltpu.VMEM((size, 6 * BLOCK), BF16),
            pltpu.VMEM((6 * BLOCK, size), BF16),
            pltpu.VMEM((1, size), F32),
            pltpu.VMEM((size, BLOCK), F32),
        ],
        compiler_params=pltpu.CompilerParams(vmem_limit_bytes=VMEM_LIMIT),
        cost_estimate=pl.CostEstimate(
            flops=40 * 10**9, bytes_accessed=10 * 2**20, transcendentals=0
        ),
        name="inverse",
    )(gathered, col_rank, tangents)


def split2(x):
    hi = x.astype(BF16)
    return hi, (x - hi.astype(F32)).astype(BF16)


def dot_split(left, right, dims=NN):
    left_hi, left_lo = left
    right_hi, right_lo = right
    rows = left_hi.shape[0]
    both = lax.dot_general(
        jnp.concatenate([left_hi, left_lo], axis=0), right_hi, dims, preferred_element_type=F32
    )
    cross = lax.dot_general(left_hi, right_lo, dims, preferred_element_type=F32)
    return both[:rows] + (both[rows:] + cross)


def keep_rows(x, rank):
    return jnp.where(lax.broadcasted_iota(jnp.int32, x.shape, 0) < rank, x, 0.0)


def put(refs, at, x):
    hi, lo = split2(x)
    refs[0][at] = hi
    refs[1][at] = lo


def put_shards(refs, slot, sources, position, p, comp, rank):
    count = len(sources)
    width = sources[0].shape[-1]
    rank_count = sources[0].shape[-2]
    for s, ref in enumerate(sources):
        owner = lax.rem(position - s + count, count)
        at = pl.ds(pl.multiple_of(owner * width, width), width)
        put(refs, (p, pl.ds(slot * rank_count, rank_count), at), keep_rows(ref[p, comp], rank))


def col_component(ref, comp, rank):
    whole = jnp.concatenate([ref[g, comp] for g in range(ref.shape[0])], axis=0)
    return keep_rows(whole, rank)


def recompress_kernel(
    tiles, shards, place, panel_rank, col_rank, tile_rank, keep_rank, *refs
):
    first = refs[:shards]
    second = refs[shards : 2 * shards]
    cols, trailing, sketch, solved, inverse, products, out = refs[2 * shards : 2 * shards + 7]
    left_hi, left_lo, right_hi, right_lo, panel_hi, panel_lo = refs[2 * shards + 7 :]
    lefts, rights, panels = (left_hi, left_lo), (right_hi, right_lo), (panel_hi, panel_lo)
    rank_count, size = sketch.shape
    up_scale = math.sqrt(size)
    down_scale = 1.0 / math.sqrt(rank_count)
    position = place[0]
    block = lambda x, i: x[:, i * rank_count : (i + 1) * rank_count]
    band = lambda x, i: x[i * rank_count : (i + 1) * rank_count]
    slot = lambda p, i, n=1: (p, slice(i * rank_count, (i + n) * rank_count), slice(None))
    take = lambda pair, at: (pair[0][at], pair[1][at])

    for t in range(4):
        u_col = col_component(cols, t, col_rank[0])
        for p in range(tiles):
            put(rights, slot(p, 1 if t == 0 else 4 + t), u_col)
    for p in range(tiles):
        for t in range(4):
            rank = tile_rank[p, 0]
            put(lefts, slot(p, 0 if t == 0 else 1 + t), keep_rows(trailing[p, 0, t], rank))
            put(rights, slot(p, 0 if t == 0 else 1 + t), keep_rows(trailing[p, 0, 4 + t], rank))
        put_shards(lefts, 1, first, position, p, 0, panel_rank[p])
        put_shards(panels, 0, first, position, p, 1, panel_rank[p])
        for t in range(3):
            put_shards(lefts, 5 + t, second, position, p, t, panel_rank[p])
            put_shards(panels, 1 + t, second, position, p, 3 + t, panel_rank[p])

    sides = []
    for t in range(3):
        whole = jnp.concatenate([products[r, t] for r in range(products.shape[0])], axis=1)
        sides.append(col_component(cols, 5 + t, col_rank[0]) - whole)
    dz = dot_split(split2(jnp.concatenate(sides, axis=0)), split2(inverse[...]))
    z_hi, z_lo = split2(solved[...])
    dz_hi, dz_lo = split2(dz)
    zz = (jnp.concatenate([z_hi, dz_hi], axis=0), jnp.concatenate([z_lo, dz_lo], axis=0))
    s = split2(sketch[...])

    state = []
    for p in range(tiles):
        live = lax.broadcasted_iota(jnp.int32, (rank_count, 1), 0) < keep_rank[p, 0]
        mixes = dot_split(take(panels, slot(p, 0, 4)), zz, NT)
        sketched = jnp.where(live, dot_split(s, take(rights, slot(p, 0, 8)), NT), 0.0)
        mix = mixes[:rank_count, :rank_count]
        base_u = -mm(block(sketched, 1), mix, NT)
        pair = jnp.concatenate([block(sketched, 0), base_u], axis=1)
        bases = take(lefts, slot(p, 0, 2))
        y = dot_split(split2(pair), bases)
        y_split = split2(y)
        gram = dot_split(y_split, y_split, NT)
        eye = lax.broadcasted_iota(jnp.int32, gram.shape, 0) == lax.broadcasted_iota(
            jnp.int32, gram.shape, 1
        )
        gram = gram + jnp.where(eye & jnp.logical_not(live), 1.0, 0.0)
        augmented = jnp.concatenate([gram, jnp.where(eye, 1.0, 0.0)], axis=1)
        cross = dot_split(bases, take(lefts, slot(p, 0, 8)), NT)
        state.append((mixes, sketched, pair, cross, augmented))

    factors = [factor_inverse(as_rows(entry[-1]), rank_count) for entry in state]

    for p in range(tiles):
        mixes, sketched, pair, cross, _ = state[p]
        rinv = jnp.concatenate(factors[p], axis=0)[:, rank_count:]
        mix = mixes[:rank_count, :rank_count]
        dmix = [band(block(mixes, 0), 1 + t) + band(block(mixes, 1 + t), 0) for t in range(3)]
        su = [block(sketched, 1)] + [block(sketched, 5 + t) for t in range(3)]
        u_mix = mm(jnp.concatenate(su[1:], axis=0), mix, NT)
        u_dmix = mm(su[0], jnp.concatenate(dmix, axis=0), NT)
        u_sides = [-(band(u_mix, t) + block(u_dmix, t)) for t in range(3)]
        sv = [block(sketched, 2 + t) for t in range(3)]
        coefs = mm(rinv, jnp.concatenate([pair] + sv + u_sides, axis=1))
        q_coef = coefs[:, : 2 * rank_count]
        q_parts = mm(q_coef, cross)
        phis = []
        for t in range(3):
            e_coef = jnp.concatenate(
                [block(coefs, 2 + t), block(coefs, 5 + t), q_coef], axis=1
            )
            q_side = jnp.concatenate(
                [block(q_parts, 0), block(q_parts, 1), block(q_parts, 2 + t), block(q_parts, 5 + t)],
                axis=1,
            )
            half = mm(e_coef, q_side, NT)
            sym = half + half.T
            i0 = lax.broadcasted_iota(jnp.int32, sym.shape, 0)
            i1 = lax.broadcasted_iota(jnp.int32, sym.shape, 1)
            phis.append(jnp.where(i0 > i1, sym, jnp.where(i0 == i1, 0.5 * sym, 0.0)))
        turned = mm(jnp.concatenate(phis, axis=0), q_coef)
        none = jnp.zeros((rank_count, rank_count), F32)
        rows = [jnp.concatenate([q_coef] + [none] * 6, axis=1)]
        for t in range(3):
            head = jnp.concatenate([block(coefs, 2 + t), block(coefs, 5 + t)], axis=1)
            tail = [none] * 6
            tail[t], tail[3 + t] = block(q_coef, 0), block(q_coef, 1)
            rows.append(jnp.concatenate([head - band(turned, t)] + tail, axis=1))
        basis_coef = jnp.concatenate(rows, axis=0)
        basis = dot_split(split2(basis_coef), take(lefts, slot(p, 0, 8))) * up_scale
        for t in range(4):
            out[p, 0, t] = band(basis, t)
        dq_parts = mm(basis_coef[rank_count:], cross, NT)
        on_u = mm(
            block(dq_parts, 1)
            + jnp.concatenate([block(q_parts, 5 + t) for t in range(3)], axis=0),
            mix,
        )
        on_dmix = mm(block(q_parts, 1), jnp.concatenate(dmix, axis=1))
        q_mix = mm(block(q_parts, 1), mix)
        rows = [jnp.concatenate([block(q_parts, 0), -q_mix] + [none] * 6, axis=1)]
        for t in range(3):
            on_v = band(block(dq_parts, 0), t) + block(q_parts, 2 + t)
            tail = [none] * 6
            tail[t], tail[3 + t] = block(q_parts, 0), -q_mix
            rows.append(
                jnp.concatenate([on_v, -(band(on_u, t) + block(on_dmix, t))] + tail, axis=1)
            )
        coeff = dot_split(
            split2(jnp.concatenate(rows, axis=0) * down_scale), take(rights, slot(p, 0, 8))
        )
        for t in range(4):
            out[p, 0, 4 + t] = band(coeff, t)


def run_recompress(
    place, ranks, first, second, cols, trailing, sketch, solved, inverse, products
):
    tiles = trailing.shape[0]
    rank_count, size = sketch.shape
    vmem = pl.BlockSpec(memory_space=pltpu.VMEM)
    smem = pl.BlockSpec(memory_space=pltpu.SMEM)
    return pl.pallas_call(
        functools.partial(recompress_kernel, tiles, len(first)),
        out_shape=jax.ShapeDtypeStruct(trailing.shape, F32),
        in_specs=[smem] * 5 + [vmem] * (2 * len(first) + 6),
        out_specs=vmem,
        scratch_shapes=[pltpu.VMEM((tiles, 8 * rank_count, size), BF16)] * 4
        + [pltpu.VMEM((tiles, 4 * rank_count, size), BF16)] * 2,
        compiler_params=pltpu.CompilerParams(vmem_limit_bytes=VMEM_LIMIT),
        cost_estimate=pl.CostEstimate(
            flops=10 * 10**9, bytes_accessed=20 * 2**20, transcendentals=0
        ),
        name="recompress",
    )(place, *ranks, *first, *second, cols, trailing, sketch, solved, inverse, products)


def on_device(
    row_count,
    col_count,
    diag,
    panel_rows,
    panel_cols,
    trailing,
    sketch,
    panel_rank,
    col_rank,
    tile_rank,
    keep_rank,
):
    own_rows = diag.shape[1]
    own_ranks = panel_cols.shape[2]
    comps = panel_cols.shape[1]
    size = sketch.shape[1]
    gathered = lax.all_gather(
        jnp.concatenate([diag[0], panel_cols[0, 4]], axis=0), "row", axis=0
    )
    first = panel_rows[:, 0::4]
    second = jnp.concatenate([panel_rows[:, 1:4], panel_rows[:, 5:8]], axis=1)
    first_shards, second_shards = [first], [second]
    for source, shards in ((first, first_shards), (second, second_shards)):
        for s in range(1, col_count):
            shards.append(
                lax.ppermute(source, "col", [(i, (i + s) % col_count) for i in range(col_count)])
            )
    late_cols, gathered = lax.optimization_barrier((panel_cols[0], gathered))
    cols = lax.all_gather(late_cols, "row", axis=0)
    if own_ranks != SUB:
        cols = cols.reshape(-1, SUB // own_ranks, comps, own_ranks, size)
        cols = cols.transpose(0, 2, 1, 3, 4).reshape(-1, comps, SUB, size)
    inverse, solved, products = run_inverse(gathered, diag[1:], col_rank, own_rows)
    all_products = lax.all_gather(products, "row", axis=0)
    place = lax.axis_index("col").astype(jnp.int32).reshape(1)
    ranks = (panel_rank, col_rank, tile_rank, keep_rank)
    return run_recompress(
        place,
        ranks,
        first_shards,
        second_shards,
        cols,
        trailing,
        sketch,
        solved,
        inverse,
        all_products,
    )


def solution(mesh):
    in_specs = (
        P(None, "row", None),
        P("row", None, None, "col"),
        P("col", None, "row", None),
        P("row", "col", None, None, None),
        P(),
        P("row"),
        P("col"),
        P("row", "col"),
        P("row", "col"),
    )
    out_specs = P("row", "col", None, None, None)
    body = functools.partial(on_device, mesh.shape["row"], mesh.shape["col"])
    return jax.shard_map(body, mesh=mesh, in_specs=in_specs, out_specs=out_specs, check_vma=False)
```

time: 196 us -> 167 us (0.85)
  Pallas kernels: 119 us -> 90.2 us
    pallas_call x2 -> x1, Pallas kernels: 56 us -> 23.8 us  [run_recompress(): pl.pallas_call(functools.partial(recompress_kernel, tiles, len(first)), o...]
    pallas_call x1, Pallas kernels: 62.9 us -> 66.3 us  [run_inverse(): pl.pallas_call(functools.partial(inverse_kernel, own_rows), out_shape=(ja...]
    unnamed x20 -> x22, local copies, waits for them, and re-layouts: 5.74 us -> 5.71 us
  transfers between devices with their start and end apart: 8 -> 8, of which waited for: 1 -> 1; matrix products, arithmetic and copies ran while one was open for 1% -> 2% of each run, Pallas kernels for 38% -> 40%
where the time goes in v2:
time: 167 us; the launch traced here: 166 us
  Pallas kernels  90.2 us (54%)
  waiting for transfers between devices  28.3 us (17%)
  between operations  14.2 us (9%)
  starting transfers between devices  12.4 us (7%)
  blocking collectives  10.4 us (6%)
  local copies, waits for them, and re-layouts  10 us (6%)
    pallas_call x1, Pallas kernels, run_inverse(): pl.pallas_call(functools.partial(inverse_kernel, own_rows), out_shape=(ja...  66.3 us
    all_gather x1, waiting for transfers between devices, on_device(): lax.all_gather(jnp.concatenate([diag[0], panel_cols[0, 4]], axis=0), 'row...  28.2 us
    pallas_call x1, Pallas kernels, run_recompress(): pl.pallas_call(functools.partial(recompress_kernel, tiles, len(first)), o...  23.8 us
    ppermute x6, starting transfers between devices, on_device(): lax.ppermute(source, 'col', [(i, (i + s) % col_count) for i in range(col_...  12.4 us
    all_gather x1, blocking collectives, on_device(): all_products = lax.all_gather(products, 'row', axis=0)  10.4 us
    unnamed x22, local copies, waits for them, and re-layouts  5.71 us
  transfers between devices with their start and end apart: 8, of which 1 were waited for; matrix products, arithmetic and copies ran while one was open for 2% of the time, Pallas kernels for 40%

profile of v2, /device:TPU:0, one launch (start us, length us, event | category | flops | bytes accessed | tf_op | source)
XLA Modules:
  0.0 166.3 jit_solution(6597061164411645674)
XLA Ops:
  6.5 1.1 slice_bitcast_fusion
  7.6 0.8 slice_bitcast_fusion.1
  8.4 0.8 pad_maximum_fusion.1
  9.2 0.0 all-gather.6.cloned.1.call-update
  9.3 0.0 all-gather.8.cloned.1.call-start
  9.3 0.0 copy-start.7
  9.3 1.1 slice.18.refs_0_
  10.4 3.1 %collective-permute-start = (f32[2,2,64,256]{3,2,1,0:T(8,128)S(1)}, f32[2,2,64,256]{3,2,1,0:T(8,128)}, u32[]{:S(2)}, u32[]{:S(2)}) collective-permute-start(f32[2,2,64,256]{3,2,1,0:T(8,128)S(1)} %slice.18.refs_0_), channel_id=1, source_target_pairs={{0,1},{1,2},{2,3},{3,0},{4,5},{5,6},{6,7},{7,4},{8,9},{9,10},{10,1... | collective-permute-start | bytes 786440 | tf_op jit(solution)/shard_map/ppermute | solution.py:502
  13.5 1.2 fusion
  14.7 0.1 pad_maximum_fusion.refs_4_
  14.8 1.6 collective-permute-start.3
  16.4 1.1 collective-permute-start.4
  17.5 2.8 %collective-permute-start.5 = (f32[2,6,64,256]{3,2,1,0:T(8,128)S(1)}, f32[2,6,64,256]{3,2,1,0:T(8,128)}, u32[]{:S(2)}, u32[]{:S(2)}) collective-permute-start(f32[2,6,64,256]{3,2,1,0:T(8,128)S(1)} %pad_maximum_fusion.refs_4_), channel_id=1, source_target_pairs={{0,3},{1,0},{2,1},{3,2},{4,7},{5,4},{6,5},{7,6},{8,11},{9,8},{10,9... | collective-permute-start | bytes 2359304 | tf_op jit(solution)/shard_map/ppermute | solution.py:502
  20.3 0.3 collective-permute-start.1
  20.7 0.2 slice.23.tangents
  21.5 0.1 copy.12.tile_rank
  21.6 0.1 copy.13.keep_rank
  21.7 28.2 %all-gather.6.cloned.1.call-done = f32[1088,1024]{1,0:T(8,128)} async-done(((f32[136,1024]{1,0:T(8,128)}), f32[1088,1024]{1,0:T(8,128)}) %all-gather.6.cloned.1.call-update) | async-done | bytes 4456464 | tf_op jit(solution)/shard_map/all_gather | solution.py:493
  49.9 0.0 all-gather.8.cloned.1.call-update
  49.9 0.0 copy-start.3
  50.0 3.4 %collective-permute-start.2 = (f32[2,2,64,256]{3,2,1,0:T(8,128)S(1)}, f32[2,2,64,256]{3,2,1,0:T(8,128)S(1)}, u32[]{:S(2)}, u32[]{:S(2)}) collective-permute-start(f32[2,2,64,256]{3,2,1,0:T(8,128)S(1)} %slice.18.refs_0_), channel_id=1, source_target_pairs={{0,3},{1,0},{2,1},{3,2},{4,7},{5,4},{6,5},{7,6},{8,11},{9,8},{10,9... | collective-permute-start | bytes 786440 | tf_op jit(solution)/shard_map/ppermute | solution.py:502
  53.4 66.3 %inverse.1 = (f32[1024,1024]{1,0:T(8,128)S(1)}, f32[64,1024]{1,0:T(8,128)S(1)}, f32[3,64,128]{2,1,0:T(8,128)S(1)}) custom-call(f32[8,136,1024]{2,1,0:T(8,128)} %bitcast.11, s32[1]{0:T(128)S(6)} %copy.14.col_rank, f32[3,128,1024]{2,1,0:T(8,128)S(1)} %slice.23.tangents), custom_call_target="tpu_custom_call" | custom-call | flops 40000000000 | bytes 10485760 | tf_op jit(solution)/shard_map/inverse/pallas_call | solution.py:263
  119.7 0.0 copy-start.4
  119.7 1.9 %copy-done.4 = f32[1024,1024]{1,0:T(8,128)} copy-done((f32[1024,1024]{1,0:T(8,128)}, f32[1024,1024]{1,0:T(8,128)S(1)}, u32[]{:S(2)}) %copy-start.4) | copy-done | bytes 4194328
  121.6 10.4 %all-gather.2 = f32[24,64,128]{2,1,0:T(8,128)S(1)} all-gather(f32[3,64,128]{2,1,0:T(8,128)S(1)} %get-tuple-element.14), channel_id=4, replica_groups=mesh['row'=8,'col'=4] {'row'}, dimensions={0}, use_global_device_ids=true | all-gather | bytes 884736 | tf_op jit(solution)/shard_map/all_gather | solution.py:510
  132.0 0.7 copy-done.1
  132.7 0.0 all-gather.8.cloned.1.call-done
  132.8 0.0 copy-start
  132.8 0.9 copy-done
  133.7 0.9 copy-done.2
  134.7 0.9 copy-done.6
  135.6 23.8 %recompress.1 = f32[2,1,8,64,1024]{4,3,2,1,0:T(8,128)} custom-call(s32[1]{0:T(128)} %bitcast.place, s32[2]{0:T(128)S(1)} %copy-done.3, s32[1]{0:T(128)S(6)} %copy.14.col_rank, s32[2,1]{1,0:T(2,128)S(1)} %copy.12.tile_rank, s32[2,1]{1,0:T(2,128)S(1)} %copy.13.keep_rank, f32[2,2,64,256]{3,2,1,0:T(8,128)S(1)} %slice.18.refs_0_, ...), custom_call_target="tpu_custom_call" | custom-call | flops 10000000000 | bytes 20971520 | tf_op jit(solution)/shard_map/recompress/pallas_call | solution.py:461
  (18 shorter events, 0.0 us)
Async XLA Ops:
  6.5 43.4 %all-gather.6.cloned.1.call-start = ((), (), s32[]{:S(2)}) async-start(), calls=%async_computation | async-start | bytes 5013504 | tf_op jit(solution)/shard_map/all_gather | solution.py:493
  8.4 13.1 %copy-start.8 = (s32[2,1]{0,1:T(1,128)S(1)}, s32[2,1]{0,1:T(1,128)}, u32[]{:S(2)}) copy-start(s32[2,1]{0,1:T(1,128)} %param.16) | copy-start | bytes 28
  8.4 13.2 %copy-start.9 = (s32[2,1]{0,1:T(1,128)S(1)}, s32[2,1]{0,1:T(1,128)}, u32[]{:S(2)}) copy-start(s32[2,1]{0,1:T(1,128)} %param.17) | copy-start | bytes 28
  9.3 123.5 %all-gather.8.cloned.1.call-start = ((), (), s32[]{:S(2)}) async-start(), calls=%async_computation.1 | async-start | bytes 2359296 | tf_op jit(solution)/shard_map/all_gather | solution.py:505
  9.3 11.4 %copy-start.7 = (f32[4,128,1024]{2,1,0:T(8,128)S(1)}, f32[4,128,1024]{2,1,0:T(8,128)}, u32[]{:S(2)}) copy-start(f32[4,128,1024]{2,1,0:T(8,128)} %param.9) | copy-start | bytes 6291460
  10.4 39.5 %collective-permute-start = (f32[2,2,64,256]{3,2,1,0:T(8,128)S(1)}, f32[2,2,64,256]{3,2,1,0:T(8,128)}, u32[]{:S(2)}, u32[]{:S(2)}) collective-permute-start(f32[2,2,64,256]{3,2,1,0:T(8,128)S(1)} %slice.18.refs_0_), channel_id=1, source_target_pairs={{0,1},{1,2},{2,3},{3,0},{4,5},{5,6},{6,7},{7,4},{8,9},{9,10},{10,1... | collective-permute-start | bytes 786440 | tf_op jit(solution)/shard_map/ppermute | solution.py:502
  14.8 117.9 %collective-permute-start.3 = (f32[2,6,64,256]{3,2,1,0:T(8,128)S(1)}, f32[2,6,64,256]{3,2,1,0:T(8,128)S(1)}, u32[]{:S(2)}, u32[]{:S(2)}) collective-permute-start(f32[2,6,64,256]{3,2,1,0:T(8,128)S(1)} %pad_maximum_fusion.refs_4_), channel_id=1, source_target_pairs={{0,1},{1,2},{2,3},{3,0},{4,5},{5,6},{6,7},{7,4},{8,9},{9,10},{10,1... | collective-permute-start | bytes 2359304 | tf_op jit(solution)/shard_map/ppermute | solution.py:502
  16.4 116.3 %collective-permute-start.4 = (f32[2,6,64,256]{3,2,1,0:T(8,128)S(1)}, f32[2,6,64,256]{3,2,1,0:T(8,128)}, u32[]{:S(2)}, u32[]{:S(2)}) collective-permute-start(f32[2,6,64,256]{3,2,1,0:T(8,128)S(1)} %pad_maximum_fusion.refs_4_), channel_id=1, source_target_pairs={{0,2},{1,3},{2,0},{3,1},{4,6},{5,7},{6,4},{7,5},{8,10},{9,11},{10,... | collective-permute-start | bytes 2359304 | tf_op jit(solution)/shard_map/ppermute | solution.py:502
  17.5 115.2 %collective-permute-start.5 = (f32[2,6,64,256]{3,2,1,0:T(8,128)S(1)}, f32[2,6,64,256]{3,2,1,0:T(8,128)}, u32[]{:S(2)}, u32[]{:S(2)}) collective-permute-start(f32[2,6,64,256]{3,2,1,0:T(8,128)S(1)} %pad_maximum_fusion.refs_4_), channel_id=1, source_target_pairs={{0,3},{1,0},{2,1},{3,2},{4,7},{5,4},{6,5},{7,6},{8,11},{9,8},{10,9... | collective-permute-start | bytes 2359304 | tf_op jit(solution)/shard_map/ppermute | solution.py:502
  20.3 111.7 %collective-permute-start.1 = (f32[2,2,64,256]{3,2,1,0:T(8,128)S(1)}, f32[2,2,64,256]{3,2,1,0:T(8,128)}, u32[]{:S(2)}, u32[]{:S(2)}) collective-permute-start(f32[2,2,64,256]{3,2,1,0:T(8,128)S(1)} %slice.18.refs_0_), channel_id=1, source_target_pairs={{0,2},{1,3},{2,0},{3,1},{4,6},{5,7},{6,4},{7,5},{8,10},{9,11},{10,... | collective-permute-start | bytes 786440 | tf_op jit(solution)/shard_map/ppermute | solution.py:502
  49.9 82.8 %copy-start.3 = (s32[2]{0:T(128)S(1)}, s32[2]{0:T(128)}, u32[]{:S(2)}) copy-start(s32[2]{0:T(128)} %panel_rank.1) | copy-start | bytes 28
  50.0 82.0 %collective-permute-start.2 = (f32[2,2,64,256]{3,2,1,0:T(8,128)S(1)}, f32[2,2,64,256]{3,2,1,0:T(8,128)S(1)}, u32[]{:S(2)}, u32[]{:S(2)}) collective-permute-start(f32[2,2,64,256]{3,2,1,0:T(8,128)S(1)} %slice.18.refs_0_), channel_id=1, source_target_pairs={{0,3},{1,0},{2,1},{3,2},{4,7},{5,4},{6,5},{7,6},{8,11},{9,8},{10,9... | collective-permute-start | bytes 786440 | tf_op jit(solution)/shard_map/ppermute | solution.py:502
  119.7 2.0 %copy-start.4 = (f32[1024,1024]{1,0:T(8,128)}, f32[1024,1024]{1,0:T(8,128)S(1)}, u32[]{:S(2)}) copy-start(f32[1024,1024]{1,0:T(8,128)S(1)} %get-tuple-element.13.refs_12_) | copy-start | bytes 12582916
  121.6 11.1 %copy-start.5 = (f32[64,1024]{1,0:T(8,128)}, f32[64,1024]{1,0:T(8,128)S(1)}, u32[]{:S(2)}) copy-start(f32[64,1024]{1,0:T(8,128)S(1)} %get-tuple-element.12.refs_11_) | copy-start | bytes 786436
  132.0 0.7 copy-start.1
  132.8 1.0 copy-start
  133.7 0.9 copy-start.2
  134.7 0.9 copy-start.6
Sparse Core Ops, SparseCore 0:
  9.4 40.5 all-gather.5
  51.8 27.8 all-gather.7

commit v3 on v2

--- a/solution.py
+++ b/solution.py
@@ -13,7 +13,8 @@
 BF16 = jnp.bfloat16
 BLOCK = 128
 SUB = 8
-VMEM_LIMIT = 48 * 1024 * 1024
+INVERSE_VMEM = 28 * 1024 * 1024
+RECOMPRESS_VMEM = 40 * 1024 * 1024
 
 NN = (((1,), (0,)), ((), ()))
 NT = (((1,), (1,)), ((), ()))
@@ -114,7 +115,7 @@
     return cols, [scale * c for c in low]
 
 
-def block_inverse(rows):
+def block_inverse(rows, work):
     rows = list(rows)
     count = len(rows)
     sub, lane = sub_index(), lane_index()
@@ -130,6 +131,8 @@
             kept = jnp.where(inside, 0.0, rows[i])
             rows[i] = kept - tree_sum([lane_rep(rows[i], at + k) * news[k] for k in range(SUB)])
         rows[g] = new
+        for piece in work[g * len(work) // count : (g + 1) * len(work) // count]:
+            piece()
     return rows
 
 
@@ -163,102 +166,114 @@
     inverse,
     solved,
     products,
+    scale_row,
     pivot,
     left,
     right,
-    scale_row,
     scale_col,
 ):
     size = inverse.shape[0]
     steps = size // BLOCK
-    shards = gathered.shape[0]
-
-    def copy_in(r, _):
-        inverse[pl.ds(pl.multiple_of(r * own_rows, own_rows), own_rows), :] = gathered[
-            r, pl.ds(0, own_rows), :
-        ]
-        return _
-
-    lax.fori_loop(0, shards, copy_in, 0)
-
+    shards, height, width = gathered.shape
     eye = lax.broadcasted_iota(jnp.int32, (BLOCK, BLOCK), 0) == lax.broadcasted_iota(
         jnp.int32, (BLOCK, BLOCK), 1
     )
-    for c in range(steps):
-        part = slice(c * BLOCK, (c + 1) * BLOCK)
-        own = jnp.where(eye, inverse[part, part], 0.0)
-        scale_row[:, part] = lax.rsqrt(jnp.sum(own, axis=0, keepdims=True))
-        scale_col[part, :] = jnp.broadcast_to(
+    part = lambda c, n=BLOCK: slice(c * n, (c + 1) * n)
+
+    def set_scale(c, block):
+        own = jnp.where(eye, block, 0.0)
+        scale_row[:, part(c)] = lax.rsqrt(jnp.sum(own, axis=0, keepdims=True))
+        scale_col[part(c), :] = jnp.broadcast_to(
             lax.rsqrt(jnp.sum(own, axis=1, keepdims=True)), (BLOCK, BLOCK)
         )
 
-    def rescale():
+    if width < size:
         for c in range(steps):
-            part = slice(c * BLOCK, (c + 1) * BLOCK)
-            col = scale_col[part, :]
-            for e in range(steps):
-                other = slice(e * BLOCK, (e + 1) * BLOCK)
-                inverse[part, other] = inverse[part, other] * col * scale_row[:, other]
-
-    rescale()
-
-    def invert_to_pivot(block):
-        pivot[...] = jnp.concatenate(block_inverse(as_rows(block)), axis=0)
-
-    def prepare(k):
+            set_scale(c, gathered[c, :BLOCK, :BLOCK])
+        for r in range(steps):
+            for o in range(width // BLOCK):
+                c = (r + o) % steps
+                block = gathered[r, :BLOCK, part(o)] * scale_col[part(r), :] * scale_row[:, part(c)]
+                inverse[part(r), part(c)] = block
+                if 0 < o and 2 * o < steps:
+                    inverse[part(c), part(r)] = block.T
+    else:
+        for r in range(shards):
+            inverse[part(r, own_rows), :] = gathered[r, :own_rows, :]
+        for c in range(steps):
+            set_scale(c, inverse[part(c), part(c)])
+        for r in range(steps):
+            for c in range(steps):
+                inverse[part(r), part(c)] = (
+                    inverse[part(r), part(c)] * scale_col[part(r), :] * scale_row[:, part(c)]
+                )
+
+    def eliminate(k, at, inv):
+        chunk = 2 * BLOCK
+        chunks = size // chunk
+        twice = jnp.concatenate([inv, inv], axis=1)
+
+        def fill_left(c):
+            column = inverse[part(c, chunk), at]
+            owner = 2 * c + lax.broadcasted_iota(jnp.int32, column.shape, 0) // BLOCK
+            left[part(c, chunk), :] = left_terms(jnp.where(owner == k, 0.0, column))
+            inverse[part(c, chunk), at] = jnp.zeros((chunk, BLOCK), F32)
+
+        def fill_right(c):
+            row = mm(inv, inverse[at, part(c, chunk)])
+            owner = 2 * c + lax.broadcasted_iota(jnp.int32, row.shape, 1) // BLOCK
+            row = jnp.where(owner == k, twice, row)
+            right[:, part(c, chunk)] = right_terms(row)
+            inverse[at, part(c, chunk)] = row
+
+        def update(r, c):
+            here = (part(r, chunk), part(c, chunk))
+            inverse[here] = inverse[here] - lax.dot_general(
+                left[here[0], :], right[:, here[1]], NN, preferred_element_type=F32
+            )
+
+        work = [functools.partial(fill_left, c) for c in range(chunks)]
+        for c in range(chunks):
+            work.append(functools.partial(fill_right, c))
+            work += [functools.partial(update, r, c) for r in range(chunks)]
+        return work
+
+    def invert_to_pivot(block, work):
+        pivot[...] = jnp.concatenate(block_inverse(as_rows(block), work), axis=0)
+
+    invert_to_pivot(inverse[:BLOCK, :BLOCK], [])
+
+    def step(k, carry):
         at = pl.ds(pl.multiple_of(k * BLOCK, BLOCK), BLOCK)
+        nxt = pl.ds(pl.multiple_of((k + 1) * BLOCK, BLOCK), BLOCK)
         inv = pivot[...]
-        column = inverse[:, at]
-        row = mm(inv, inverse[at, :])
-        left[...] = left_terms(column)
-        right[...] = right_terms(row)
-        right[:, at] = right_terms(inv)
-        inverse[:, at] = jnp.zeros((size, BLOCK), F32)
-        return at, row, inv
-
-    def update(at, row, inv):
-        chunk = 256
-        for c in range(size // chunk):
-            part = slice(c * chunk, (c + 1) * chunk)
-            inverse[part, :] = inverse[part, :] - lax.dot_general(
-                left[part, :], right[...], NN, preferred_element_type=F32
-            )
-        inverse[at, :] = row
-        inverse[at, at] = inv
-
-    invert_to_pivot(inverse[:BLOCK, :BLOCK])
-
-    def step(k, carry):
-        nxt = pl.ds(pl.multiple_of((k + 1) * BLOCK, BLOCK), BLOCK)
-        block = inverse[nxt, nxt]
-        at, row, inv = prepare(k)
-        block = block - lax.dot_general(
-            left[nxt, :], right[:, nxt], NN, preferred_element_type=F32
-        )
-        update(at, row, inv)
-        invert_to_pivot(block)
+        block = inverse[nxt, nxt] - mm(inverse[nxt, at], mm(inv, inverse[at, nxt]))
+        invert_to_pivot(block, eliminate(k, at, inv))
         return carry
 
     lax.fori_loop(0, steps - 1, step, 0)
-    update(*prepare(steps - 1))
-    rescale()
+    for piece in eliminate(steps - 1, slice(size - BLOCK, size), pivot[...]):
+        piece()
 
     rank_count = solved.shape[0]
     own_ranks = rank_count // shards
-    values = jnp.concatenate(
-        [gathered[r, own_rows : own_rows + own_ranks, :] for r in range(shards)], axis=0
-    )
-    live = lax.broadcasted_iota(jnp.int32, values.shape, 0) < col_rank[0]
-    values = jnp.where(live, values, 0.0)
-    z = mm(values, inverse[...])
+    values = []
+    for r in range(shards):
+        pieces = []
+        for at in range(own_rows, height, own_ranks):
+            pieces.append(gathered[r, at : at + own_ranks, :])
+        values.append(jnp.concatenate(pieces, axis=1)[:, :size])
+    values = keep_rows(jnp.concatenate(values, axis=0), col_rank[0])
+    z = mm(values * scale_row[...], inverse[...]) * scale_row[...]
     solved[...] = z
     for t in range(3):
         products[t] = mm(z, tangents[t], NT)
 
 
-def run_inverse(gathered, tangents, col_rank, own_rows):
-    shards, _, size = gathered.shape
-    rank_count = (gathered.shape[1] - own_rows) * shards
+def run_inverse(gathered, tangents, col_rank, own_rows, own_ranks):
+    shards = gathered.shape[0]
+    size = tangents.shape[2]
+    rank_count = own_ranks * shards
     vmem = pl.BlockSpec(memory_space=pltpu.VMEM)
     return pl.pallas_call(
         functools.partial(inverse_kernel, own_rows),
@@ -266,17 +281,17 @@
             jax.ShapeDtypeStruct((size, size), F32),
             jax.ShapeDtypeStruct((rank_count, size), F32),
             jax.ShapeDtypeStruct((3, rank_count, own_rows), F32),
+            jax.ShapeDtypeStruct((1, size), F32),
         ),
         in_specs=[vmem, pl.BlockSpec(memory_space=pltpu.SMEM), vmem],
-        out_specs=(vmem, vmem, vmem),
+        out_specs=(vmem,) * 4,
         scratch_shapes=[
             pltpu.VMEM((BLOCK, BLOCK), F32),
             pltpu.VMEM((size, 6 * BLOCK), BF16),
             pltpu.VMEM((6 * BLOCK, size), BF16),
-            pltpu.VMEM((1, size), F32),
             pltpu.VMEM((size, BLOCK), F32),
         ],
-        compiler_params=pltpu.CompilerParams(vmem_limit_bytes=VMEM_LIMIT),
+        compiler_params=pltpu.CompilerParams(vmem_limit_bytes=INVERSE_VMEM),
         cost_estimate=pl.CostEstimate(
             flops=40 * 10**9, bytes_accessed=10 * 2**20, transcendentals=0
         ),
@@ -330,8 +345,10 @@
 ):
     first = refs[:shards]
     second = refs[shards : 2 * shards]
-    cols, trailing, sketch, solved, inverse, products, out = refs[2 * shards : 2 * shards + 7]
-    left_hi, left_lo, right_hi, right_lo, panel_hi, panel_lo = refs[2 * shards + 7 :]
+    cols, trailing, sketch, solved, inverse, scale, products, out = refs[
+        2 * shards : 2 * shards + 8
+    ]
+    left_hi, left_lo, right_hi, right_lo, panel_hi, panel_lo = refs[2 * shards + 8 :]
     lefts, rights, panels = (left_hi, left_lo), (right_hi, right_lo), (panel_hi, panel_lo)
     rank_count, size = sketch.shape
     up_scale = math.sqrt(size)
@@ -361,7 +378,8 @@
     for t in range(3):
         whole = jnp.concatenate([products[r, t] for r in range(products.shape[0])], axis=1)
         sides.append(col_component(cols, 5 + t, col_rank[0]) - whole)
-    dz = dot_split(split2(jnp.concatenate(sides, axis=0)), split2(inverse[...]))
+    sides = jnp.concatenate(sides, axis=0) * scale[...]
+    dz = dot_split(split2(sides), split2(inverse[...])) * scale[...]
     z_hi, z_lo = split2(solved[...])
     dz_hi, dz_lo = split2(dz)
     zz = (jnp.concatenate([z_hi, dz_hi], axis=0), jnp.concatenate([z_lo, dz_lo], axis=0))
@@ -452,7 +470,7 @@
 
 
 def run_recompress(
-    place, ranks, first, second, cols, trailing, sketch, solved, inverse, products
+    place, ranks, first, second, cols, trailing, sketch, solved, inverse, scale, products
 ):
     tiles = trailing.shape[0]
     rank_count, size = sketch.shape
@@ -461,16 +479,16 @@
     return pl.pallas_call(
         functools.partial(recompress_kernel, tiles, len(first)),
         out_shape=jax.ShapeDtypeStruct(trailing.shape, F32),
-        in_specs=[smem] * 5 + [vmem] * (2 * len(first) + 6),
+        in_specs=[smem] * 5 + [vmem] * (2 * len(first) + 7),
         out_specs=vmem,
         scratch_shapes=[pltpu.VMEM((tiles, 8 * rank_count, size), BF16)] * 4
         + [pltpu.VMEM((tiles, 4 * rank_count, size), BF16)] * 2,
-        compiler_params=pltpu.CompilerParams(vmem_limit_bytes=VMEM_LIMIT),
+        compiler_params=pltpu.CompilerParams(vmem_limit_bytes=RECOMPRESS_VMEM),
         cost_estimate=pl.CostEstimate(
             flops=10 * 10**9, bytes_accessed=20 * 2**20, transcendentals=0
         ),
         name="recompress",
-    )(place, *ranks, *first, *second, cols, trailing, sketch, solved, inverse, products)
+    )(place, *ranks, *first, *second, cols, trailing, sketch, solved, inverse, scale, products)
 
 
 def on_device(
@@ -490,9 +508,20 @@
     own_ranks = panel_cols.shape[2]
     comps = panel_cols.shape[1]
     size = sketch.shape[1]
-    gathered = lax.all_gather(
-        jnp.concatenate([diag[0], panel_cols[0, 4]], axis=0), "row", axis=0
-    )
+    values = panel_cols[0, 4]
+    own = diag[0]
+    if own_rows == BLOCK and row_count > 2:
+        width = (row_count // 2 + 1) * BLOCK
+        own = lax.dynamic_slice(
+            jnp.concatenate([own, own[:, : width - BLOCK]], axis=1),
+            (0, lax.axis_index("row") * BLOCK),
+            (BLOCK, width),
+        )
+        values = jnp.pad(values, ((0, 0), (0, -size % width)))
+        values = jnp.concatenate(
+            [values[:, i : i + width] for i in range(0, values.shape[1], width)], axis=0
+        )
+    gathered = lax.all_gather(jnp.concatenate([own, values], axis=0), "row", axis=0)
     first = panel_rows[:, 0::4]
     second = jnp.concatenate([panel_rows[:, 1:4], panel_rows[:, 5:8]], axis=1)
     first_shards, second_shards = [first], [second]
@@ -506,7 +535,9 @@
     if own_ranks != SUB:
         cols = cols.reshape(-1, SUB // own_ranks, comps, own_ranks, size)
         cols = cols.transpose(0, 2, 1, 3, 4).reshape(-1, comps, SUB, size)
-    inverse, solved, products = run_inverse(gathered, diag[1:], col_rank, own_rows)
+    inverse, solved, products, scale = run_inverse(
+        gathered, diag[1:], col_rank, own_rows, own_ranks
+    )
     all_products = lax.all_gather(products, "row", axis=0)
     place = lax.axis_index("col").astype(jnp.int32).reshape(1)
     ranks = (panel_rank, col_rank, tile_rank, keep_rank)
@@ -520,6 +551,7 @@
         sketch,
         solved,
         inverse,
+        scale,
         all_products,
     )
 

time: 167 us -> 153 us (0.916)
  Pallas kernels: 90.2 us -> 78.1 us
  waiting for transfers between devices: 28.3 us -> 21.5 us
  local copies, waits for them, and re-layouts: 10 us -> 15.4 us
    pallas_call x1, Pallas kernels: 66.3 us -> 56.3 us  [run_inverse(): pl.pallas_call(functools.partial(inverse_kernel, own_rows), out_shape=(ja...]
    all_gather x1, waiting for transfers between devices: 28.2 us -> 21.4 us  [on_device(): lax.all_gather(jnp.concatenate([own, values], axis=0), 'row', axis=0)]
    unnamed x22 -> x28, local copies, waits for them, and re-layouts: 5.71 us -> 11.7 us
    pallas_call x1, Pallas kernels: 23.8 us -> 21.8 us  [run_recompress(): pl.pallas_call(functools.partial(recompress_kernel, tiles, len(first)), o...]
  transfers between devices with their start and end apart: 8 -> 8, of which waited for: 1 -> 1; matrix products, arithmetic and copies ran while one was open for 2% -> 1% of each run, Pallas kernels for 40% -> 37%
where the time goes in v3:
time: 153 us; the launch traced here: 152 us
  Pallas kernels  78.1 us (51%)
  waiting for transfers between devices  21.5 us (14%)
  local copies, waits for them, and re-layouts  15.4 us (10%)
  between operations  14.2 us (9%)
  starting transfers between devices  11.7 us (8%)
  blocking collectives  10.6 us (7%)
    pallas_call x1, Pallas kernels, run_inverse(): pl.pallas_call(functools.partial(inverse_kernel, own_rows), out_shape=(ja...  56.3 us
    pallas_call x1, Pallas kernels, run_recompress(): pl.pallas_call(functools.partial(recompress_kernel, tiles, len(first)), o...  21.8 us
    all_gather x1, waiting for transfers between devices, on_device(): lax.all_gather(jnp.concatenate([own, values], axis=0), 'row', axis=0)  21.4 us
    unnamed x28, local copies, waits for them, and re-layouts  11.7 us
    ppermute x6, starting transfers between devices, on_device(): lax.ppermute(source, 'col', [(i, (i + s) % col_count) for i in range(col_...  11.6 us
    all_gather x1, blocking collectives, on_device(): all_products = lax.all_gather(products, 'row', axis=0)  10.6 us
  transfers between devices with their start and end apart: 8, of which 1 were waited for; matrix products, arithmetic and copies ran while one was open for 1% of the time, Pallas kernels for 37%

profile of v3, /device:TPU:0, one launch (start us, length us, event | category | flops | bytes accessed | tf_op | source)
XLA Modules:
  0.0 152.4 jit_solution(14621540509271411555)
XLA Ops:
  6.5 0.8 slice_bitcast_fusion.1
  7.4 1.1 slice_bitcast_fusion
  8.5 0.1 fusion
  8.6 0.8 pad_maximum_fusion.1
  9.3 0.0 all-gather.6.cloned.1.call-update
  9.4 0.0 all-gather.8.cloned.1.call-start
  9.5 0.0 copy-start.11
  9.5 0.0 copy-start.12
  9.5 5.1 %collective-permute-start.2 = (f32[2,2,64,256]{3,2,1,0:T(8,128)S(1)}, f32[2,2,64,256]{3,2,1,0:T(8,128)}, u32[]{:S(2)}, u32[]{:S(2)}) collective-permute-start(f32[2,2,64,256]{3,2,1,0:T(8,128)S(1)} %slice.28.refs_0_), channel_id=1, source_target_pairs={{0,3},{1,0},{2,1},{3,2},{4,7},{5,4},{6,5},{7,6},{8,11},{9,8},{10,9... | collective-permute-start | bytes 786440 | tf_op jit(solution)/shard_map/ppermute | solution.py:531
  14.6 1.0 collective-permute-start
  15.6 0.1 fusion.1
  15.7 0.1 pad_maximum_fusion.refs_4_
  15.8 2.9 %collective-permute-start.5 = (f32[2,6,64,256]{3,2,1,0:T(8,128)S(1)}, f32[2,6,64,256]{3,2,1,0:T(8,128)S(1)}, u32[]{:S(2)}, u32[]{:S(2)}) collective-permute-start(f32[2,6,64,256]{3,2,1,0:T(8,128)S(1)} %pad_maximum_fusion.refs_4_), channel_id=1, source_target_pairs={{0,3},{1,0},{2,1},{3,2},{4,7},{5,4},{6,5},{7,6},{8,11},{9,8},{10,9... | collective-permute-start | bytes 2359304 | tf_op jit(solution)/shard_map/ppermute | solution.py:531
  18.6 1.1 collective-permute-start.4
  19.8 1.7 %slice.36.tangents = f32[3,128,1024]{2,1,0:T(8,128)S(1)} slice(f32[4,128,1024]{2,1,0:T(8,128)} %param.9), slice={[1:4], [0:128], [0:1024]} | slice | bytes 3145728 | tf_op jit(solution)/shard_map/slice | solution.py:539
  22.1 0.1 copy.12.tile_rank
  22.2 0.1 copy.13.keep_rank
  22.3 21.4 %all-gather.6.cloned.1.call-done = f32[1152,640]{1,0:T(8,128)} async-done(((f32[144,640]{1,0:T(8,128)}), f32[1152,640]{1,0:T(8,128)}) %all-gather.6.cloned.1.call-update) | async-done | bytes 2949136 | tf_op jit(solution)/shard_map/all_gather | solution.py:524
  43.7 0.0 all-gather.8.cloned.1.call-update
  43.8 1.5 %collective-permute-start.3 = (f32[2,6,64,256]{3,2,1,0:T(8,128)S(1)}, f32[2,6,64,256]{3,2,1,0:T(8,128)S(1)}, u32[]{:S(2)}, u32[]{:S(2)}) collective-permute-start(f32[2,6,64,256]{3,2,1,0:T(8,128)S(1)} %pad_maximum_fusion.refs_4_), channel_id=1, source_target_pairs={{0,1},{1,2},{2,3},{3,0},{4,5},{5,6},{6,7},{7,4},{8,9},{9,10},{10,1... | collective-permute-start | bytes 2359304 | tf_op jit(solution)/shard_map/ppermute | solution.py:531
  45.3 1.8 %copy-done.1 = f32[1152,640]{1,0:T(8,128)S(1)} copy-done((f32[1152,640]{1,0:T(8,128)S(1)}, f32[1152,640]{1,0:T(8,128)}, u32[]{:S(2)}) %copy-start.1) | copy-done | bytes 2949144
  47.1 56.3 %inverse.1 = (f32[1024,1024]{1,0:T(8,128)S(1)}, f32[64,1024]{1,0:T(8,128)S(1)}, f32[3,64,128]{2,1,0:T(8,128)S(1)}, f32[1,1024]{1,0:T(1,128)S(1)}) custom-call(f32[8,144,640]{2,1,0:T(8,128)S(1)} %bitcast.10, s32[1]{0:T(128)S(6)} %copy.14.col_rank, f32[3,128,1024]{2,1,0:T(8,128)S(1)} %slice.36.tangents), custom_call_target="tpu_custom_call" | custom-call | flops 40000000000 | bytes 10485760 | tf_op jit(solution)/shard_map/inverse/pallas_call | solution.py:278
  103.5 0.0 copy-start.7
  103.5 2.0 %copy-done.7 = f32[1024,1024]{1,0:T(8,128)} copy-done((f32[1024,1024]{1,0:T(8,128)}, f32[1024,1024]{1,0:T(8,128)S(1)}, u32[]{:S(2)}) %copy-start.7) | copy-done | bytes 4194328
  105.4 10.6 %all-gather.2 = f32[24,64,128]{2,1,0:T(8,128)S(1)} all-gather(f32[3,64,128]{2,1,0:T(8,128)S(1)} %get-tuple-element.16), channel_id=4, replica_groups=mesh['row'=8,'col'=4] {'row'}, dimensions={0}, use_global_device_ids=true | all-gather | bytes 884736 | tf_op jit(solution)/shard_map/all_gather | solution.py:541
  116.1 0.9 copy-done.3
  116.9 2.2 %copy-done = f32[2,1,8,64,1024]{4,3,2,1,0:T(8,128)S(1)} copy-done((f32[2,1,8,64,1024]{4,3,2,1,0:T(8,128)S(1)}, f32[2,1,8,64,1024]{4,3,2,1,0:T(8,128)}, u32[]{:S(2)}) %copy-start) | copy-done | bytes 4194328
  119.1 1.6 %copy-done.2 = f32[64,8,1024]{2,1,0:T(8,128)S(1)} copy-done((f32[64,8,1024]{2,1,0:T(8,128)S(1)}, f32[64,8,1024]{2,1,0:T(8,128)}, u32[]{:S(2)}) %copy-start.2) | copy-done | bytes 2097176
  120.7 1.1 copy-done.4
  121.8 0.9 copy-done.5
  122.8 0.9 copy-done.9
  123.7 21.8 %recompress.1 = f32[2,1,8,64,1024]{4,3,2,1,0:T(8,128)} custom-call(s32[1]{0:T(128)} %bitcast.place, s32[2]{0:T(128)S(1)} %copy-done.6, s32[1]{0:T(128)S(6)} %copy.14.col_rank, s32[2,1]{1,0:T(2,128)S(1)} %copy.12.tile_rank, s32[2,1]{1,0:T(2,128)S(1)} %copy.13.keep_rank, f32[2,2,64,256]{3,2,1,0:T(8,128)S(1)} %slice.28.refs_0_, ...), custom_call_target="tpu_custom_call" | custom-call | flops 10000000000 | bytes 20971520 | tf_op jit(solution)/shard_map/recompress/pallas_call | solution.py:479
  (27 shorter events, 0.1 us)
Async XLA Ops:
  6.5 2.9 %copy-start.10 = (f32[2,8,64,256]{3,2,1,0:T(8,128)S(1)}, f32[2,8,64,256]{3,2,1,0:T(8,128)}, u32[]{:S(2)}) copy-start(f32[2,8,64,256]{3,2,1,0:T(8,128)} %param.10) | copy-start | bytes 3145732
  6.5 37.2 %all-gather.6.cloned.1.call-start = ((), (), s32[]{:S(2)}) async-start(), calls=%async_computation | async-start | bytes 3317760 | tf_op jit(solution)/shard_map/all_gather | solution.py:524
  9.4 107.6 %all-gather.8.cloned.1.call-start = ((), (), s32[]{:S(2)}) async-start(), calls=%async_computation.1 | async-start | bytes 2359296 | tf_op jit(solution)/shard_map/all_gather | solution.py:534
  9.5 12.6 %copy-start.11 = (s32[2,1]{0,1:T(1,128)S(1)}, s32[2,1]{0,1:T(1,128)}, u32[]{:S(2)}) copy-start(s32[2,1]{0,1:T(1,128)} %param.16) | copy-start | bytes 28
  9.5 12.7 %copy-start.12 = (s32[2,1]{0,1:T(1,128)S(1)}, s32[2,1]{0,1:T(1,128)}, u32[]{:S(2)}) copy-start(s32[2,1]{0,1:T(1,128)} %param.17) | copy-start | bytes 28
  9.5 34.3 %collective-permute-start.2 = (f32[2,2,64,256]{3,2,1,0:T(8,128)S(1)}, f32[2,2,64,256]{3,2,1,0:T(8,128)}, u32[]{:S(2)}, u32[]{:S(2)}) collective-permute-start(f32[2,2,64,256]{3,2,1,0:T(8,128)S(1)} %slice.28.refs_0_), channel_id=1, source_target_pairs={{0,3},{1,0},{2,1},{3,2},{4,7},{5,4},{6,5},{7,6},{8,11},{9,8},{10,9... | collective-permute-start | bytes 786440 | tf_op jit(solution)/shard_map/ppermute | solution.py:531
  14.6 101.4 %collective-permute-start.1 = (f32[2,2,64,256]{3,2,1,0:T(8,128)S(1)}, f32[2,2,64,256]{3,2,1,0:T(8,128)}, u32[]{:S(2)}, u32[]{:S(2)}) collective-permute-start(f32[2,2,64,256]{3,2,1,0:T(8,128)S(1)} %slice.28.refs_0_), channel_id=1, source_target_pairs={{0,2},{1,3},{2,0},{3,1},{4,6},{5,7},{6,4},{7,5},{8,10},{9,11},{10,... | collective-permute-start | bytes 786440 | tf_op jit(solution)/shard_map/ppermute | solution.py:531
  14.6 101.4 %collective-permute-start = (f32[2,2,64,256]{3,2,1,0:T(8,128)S(1)}, f32[2,2,64,256]{3,2,1,0:T(8,128)}, u32[]{:S(2)}, u32[]{:S(2)}) collective-permute-start(f32[2,2,64,256]{3,2,1,0:T(8,128)S(1)} %slice.28.refs_0_), channel_id=1, source_target_pairs={{0,1},{1,2},{2,3},{3,0},{4,5},{5,6},{6,7},{7,4},{8,9},{9,10},{10,1... | collective-permute-start | bytes 786440 | tf_op jit(solution)/shard_map/ppermute | solution.py:531
  15.8 100.2 %collective-permute-start.5 = (f32[2,6,64,256]{3,2,1,0:T(8,128)S(1)}, f32[2,6,64,256]{3,2,1,0:T(8,128)S(1)}, u32[]{:S(2)}, u32[]{:S(2)}) collective-permute-start(f32[2,6,64,256]{3,2,1,0:T(8,128)S(1)} %pad_maximum_fusion.refs_4_), channel_id=1, source_target_pairs={{0,3},{1,0},{2,1},{3,2},{4,7},{5,4},{6,5},{7,6},{8,11},{9,8},{10,9... | collective-permute-start | bytes 2359304 | tf_op jit(solution)/shard_map/ppermute | solution.py:531
  18.6 97.4 %collective-permute-start.4 = (f32[2,6,64,256]{3,2,1,0:T(8,128)S(1)}, f32[2,6,64,256]{3,2,1,0:T(8,128)}, u32[]{:S(2)}, u32[]{:S(2)}) collective-permute-start(f32[2,6,64,256]{3,2,1,0:T(8,128)S(1)} %pad_maximum_fusion.refs_4_), channel_id=1, source_target_pairs={{0,2},{1,3},{2,0},{3,1},{4,6},{5,7},{6,4},{7,5},{8,10},{9,11},{10,... | collective-permute-start | bytes 2359304 | tf_op jit(solution)/shard_map/ppermute | solution.py:531
  43.7 73.2 %copy-start.6 = (s32[2]{0:T(128)S(1)}, s32[2]{0:T(128)}, u32[]{:S(2)}) copy-start(s32[2]{0:T(128)} %panel_rank.1) | copy-start | bytes 28
  43.8 72.3 %collective-permute-start.3 = (f32[2,6,64,256]{3,2,1,0:T(8,128)S(1)}, f32[2,6,64,256]{3,2,1,0:T(8,128)S(1)}, u32[]{:S(2)}, u32[]{:S(2)}) collective-permute-start(f32[2,6,64,256]{3,2,1,0:T(8,128)S(1)} %pad_maximum_fusion.refs_4_), channel_id=1, source_target_pairs={{0,1},{1,2},{2,3},{3,0},{4,5},{5,6},{6,7},{7,4},{8,9},{9,10},{10,1... | collective-permute-start | bytes 2359304 | tf_op jit(solution)/shard_map/ppermute | solution.py:531
  45.3 1.8 %copy-start.1 = (f32[1152,640]{1,0:T(8,128)S(1)}, f32[1152,640]{1,0:T(8,128)}, u32[]{:S(2)}) copy-start(f32[1152,640]{1,0:T(8,128)} %all-gather.6.cloned.1.call-done) | copy-start | bytes 8847364
  103.5 2.0 %copy-start.7 = (f32[1024,1024]{1,0:T(8,128)}, f32[1024,1024]{1,0:T(8,128)S(1)}, u32[]{:S(2)}) copy-start(f32[1024,1024]{1,0:T(8,128)S(1)} %get-tuple-element.14.refs_12_) | copy-start | bytes 12582916
  105.4 10.6 %copy-start.8 = (f32[64,1024]{1,0:T(8,128)}, f32[64,1024]{1,0:T(8,128)S(1)}, u32[]{:S(2)}) copy-start(f32[64,1024]{1,0:T(8,128)S(1)} %get-tuple-element.13.refs_11_) | copy-start | bytes 786436
  116.0 0.9 copy-start.3
  116.9 2.2 %copy-start = (f32[2,1,8,64,1024]{4,3,2,1,0:T(8,128)S(1)}, f32[2,1,8,64,1024]{4,3,2,1,0:T(8,128)}, u32[]{:S(2)}) copy-start(f32[2,1,8,64,1024]{4,3,2,1,0:T(8,128)} %refs_9_.1) | copy-start | bytes 12582916
  119.1 1.6 %copy-start.2 = (f32[64,8,1024]{2,1,0:T(8,128)S(1)}, f32[64,8,1024]{2,1,0:T(8,128)}, u32[]{:S(2)}) copy-start(f32[64,8,1024]{2,1,0:T(8,128)} %all-gather.8.cloned.1.call-done) | copy-start | bytes 6291460
  120.7 1.1 copy-start.4
  121.8 0.9 copy-start.5
  122.8 0.9 copy-start.9
Sparse Core Ops, SparseCore 0:
  9.5 34.1 all-gather.5
  45.6 27.9 all-gather.7

commit v4 on v3

--- a/solution.py
+++ b/solution.py
@@ -13,8 +13,9 @@
 BF16 = jnp.bfloat16
 BLOCK = 128
 SUB = 8
+BAND = 4
 INVERSE_VMEM = 28 * 1024 * 1024
-RECOMPRESS_VMEM = 40 * 1024 * 1024
+RECOMPRESS_VMEM = 46 * 1024 * 1024
 
 NN = (((1,), (0,)), ((), ()))
 NT = (((1,), (1,)), ((), ()))
@@ -119,20 +120,30 @@
     rows = list(rows)
     count = len(rows)
     sub, lane = sub_index(), lane_index()
-    for g in range(count):
-        at = g * SUB
-        inside = (lane >= at) & (lane < at + SUB)
-        inv = micro_inverse([lane_rep(rows[g], at + k) for k in range(SUB)])
-        own = jnp.where(inside, jnp.where(lane - at == sub, 1.0, 0.0), rows[g])
-        new = tree_sum([inv[k] * sub_rep(own, k) for k in range(SUB)])
-        news = [sub_rep(new, k) for k in range(SUB)]
-        order = [(g + 1 + i) % count for i in range(count - 1)]
-        for i in order:
-            kept = jnp.where(inside, 0.0, rows[i])
-            rows[i] = kept - tree_sum([lane_rep(rows[i], at + k) * news[k] for k in range(SUB)])
-        rows[g] = new
-        for piece in work[g * len(work) // count : (g + 1) * len(work) // count]:
-            piece()
+    for first in range(0, count, BAND):
+        band = range(first, first + BAND)
+        for g in band:
+            at = g * SUB
+            inside = (lane >= at) & (lane < at + SUB)
+            inv = micro_inverse([lane_rep(rows[g], at + k) for k in range(SUB)])
+            own = jnp.where(inside, jnp.where(lane - at == sub, 1.0, 0.0), rows[g])
+            new = tree_sum([inv[k] * sub_rep(own, k) for k in range(SUB)])
+            news = [sub_rep(new, k) for k in range(SUB)]
+            for i in [first + (g - first + 1 + i) % BAND for i in range(BAND - 1)]:
+                kept = jnp.where(inside, 0.0, rows[i])
+                rows[i] = kept - tree_sum(
+                    [lane_rep(rows[i], at + k) * news[k] for k in range(SUB)]
+                )
+            rows[g] = new
+            for piece in work[g * len(work) // count : (g + 1) * len(work) // count]:
+                piece()
+        inside = (lane >= first * SUB) & (lane < (first + BAND) * SUB)
+        others = [(first + BAND + i) % count for i in range(count - BAND)]
+        none = jnp.zeros((SUB, BLOCK), F32)
+        padded = jnp.concatenate([rows[i] if i in band else none for i in range(count)], axis=0)
+        change = as_rows(mm(jnp.concatenate([rows[i] for i in others], axis=0), padded))
+        for i, delta in zip(others, change):
+            rows[i] = jnp.where(inside, 0.0, rows[i]) - delta
     return rows
 
 
@@ -162,19 +173,24 @@
     own_rows,
     gathered,
     col_rank,
-    tangents,
-    inverse,
+    diag,
+    inverse_out,
     solved,
     products,
     scale_row,
+    inverse,
+    tangents,
     pivot,
     left,
     right,
     scale_col,
+    sems,
 ):
     size = inverse.shape[0]
     steps = size // BLOCK
     shards, height, width = gathered.shape
+    fetch = pltpu.make_async_copy(diag.at[pl.ds(1, 3)], tangents, sems.at[0])
+    fetch.start()
     eye = lax.broadcasted_iota(jnp.int32, (BLOCK, BLOCK), 0) == lax.broadcasted_iota(
         jnp.int32, (BLOCK, BLOCK), 1
     )
@@ -254,6 +270,8 @@
     lax.fori_loop(0, steps - 1, step, 0)
     for piece in eliminate(steps - 1, slice(size - BLOCK, size), pivot[...]):
         piece()
+    store = pltpu.make_async_copy(inverse, inverse_out, sems.at[1])
+    store.start()
 
     rank_count = solved.shape[0]
     own_ranks = rank_count // shards
@@ -266,13 +284,15 @@
     values = keep_rows(jnp.concatenate(values, axis=0), col_rank[0])
     z = mm(values * scale_row[...], inverse[...]) * scale_row[...]
     solved[...] = z
+    fetch.wait()
     for t in range(3):
         products[t] = mm(z, tangents[t], NT)
-
-
-def run_inverse(gathered, tangents, col_rank, own_rows, own_ranks):
+    store.wait()
+
+
+def run_inverse(gathered, diag, col_rank, own_ranks):
     shards = gathered.shape[0]
-    size = tangents.shape[2]
+    _, own_rows, size = diag.shape
     rank_count = own_ranks * shards
     vmem = pl.BlockSpec(memory_space=pltpu.VMEM)
     return pl.pallas_call(
@@ -283,20 +303,27 @@
             jax.ShapeDtypeStruct((3, rank_count, own_rows), F32),
             jax.ShapeDtypeStruct((1, size), F32),
         ),
-        in_specs=[vmem, pl.BlockSpec(memory_space=pltpu.SMEM), vmem],
-        out_specs=(vmem,) * 4,
+        in_specs=[
+            vmem,
+            pl.BlockSpec(memory_space=pltpu.SMEM),
+            pl.BlockSpec(memory_space=pl.ANY),
+        ],
+        out_specs=(pl.BlockSpec(memory_space=pl.ANY), vmem, vmem, vmem),
         scratch_shapes=[
+            pltpu.VMEM((size, size), F32),
+            pltpu.VMEM((3, own_rows, size), F32),
             pltpu.VMEM((BLOCK, BLOCK), F32),
             pltpu.VMEM((size, 6 * BLOCK), BF16),
             pltpu.VMEM((6 * BLOCK, size), BF16),
             pltpu.VMEM((size, BLOCK), F32),
+            pltpu.SemaphoreType.DMA((2,)),
         ],
         compiler_params=pltpu.CompilerParams(vmem_limit_bytes=INVERSE_VMEM),
         cost_estimate=pl.CostEstimate(
             flops=40 * 10**9, bytes_accessed=10 * 2**20, transcendentals=0
         ),
         name="inverse",
-    )(gathered, col_rank, tangents)
+    )(gathered, col_rank, diag)
 
 
 def split2(x):
@@ -343,12 +370,53 @@
 def recompress_kernel(
     tiles, shards, place, panel_rank, col_rank, tile_rank, keep_rank, *refs
 ):
-    first = refs[:shards]
-    second = refs[shards : 2 * shards]
-    cols, trailing, sketch, solved, inverse, scale, products, out = refs[
-        2 * shards : 2 * shards + 8
+    first_any = refs[:shards]
+    second_any = refs[shards : 2 * shards]
+    (
+        cols_any,
+        trailing_any,
+        sketch,
+        solved,
+        inverse_any,
+        scale,
+        products,
+        out_any,
+        left_hi,
+        left_lo,
+        right_hi,
+        right_lo,
+        panel_hi,
+        panel_lo,
+        cols,
+        trailing,
+        first_all,
+        second_all,
+        inverse,
+        out,
+        sems,
+    ) = refs[2 * shards :]
+    first = [first_all.at[i] for i in range(shards)]
+    second = [second_all.at[i] for i in range(shards)]
+    pairs = [(cols_any, cols)]
+    pairs += [(trailing_any.at[p], trailing.at[p]) for p in range(tiles)]
+    pairs += list(zip(first_any, first)) + list(zip(second_any, second))
+    pairs.append((inverse_any, inverse))
+    copies = [
+        pltpu.make_async_copy(source, target, sems.at[i])
+        for i, (source, target) in enumerate(pairs)
     ]
-    left_hi, left_lo, right_hi, right_lo, panel_hi, panel_lo = refs[2 * shards + 8 :]
+    for copy in copies:
+        copy.start()
+    stores = []
+
+    def store(p, begin):
+        part = pl.ds(begin, 4)
+        copy = pltpu.make_async_copy(
+            out.at[p, 0, part], out_any.at[p, 0, part], sems.at[len(pairs) + len(stores)]
+        )
+        copy.start()
+        stores.append(copy)
+
     lefts, rights, panels = (left_hi, left_lo), (right_hi, right_lo), (panel_hi, panel_lo)
     rank_count, size = sketch.shape
     up_scale = math.sqrt(size)
@@ -359,15 +427,20 @@
     slot = lambda p, i, n=1: (p, slice(i * rank_count, (i + n) * rank_count), slice(None))
     take = lambda pair, at: (pair[0][at], pair[1][at])
 
+    copies[0].wait()
     for t in range(4):
         u_col = col_component(cols, t, col_rank[0])
         for p in range(tiles):
             put(rights, slot(p, 1 if t == 0 else 4 + t), u_col)
     for p in range(tiles):
+        copies[1 + p].wait()
         for t in range(4):
             rank = tile_rank[p, 0]
             put(lefts, slot(p, 0 if t == 0 else 1 + t), keep_rows(trailing[p, 0, t], rank))
             put(rights, slot(p, 0 if t == 0 else 1 + t), keep_rows(trailing[p, 0, 4 + t], rank))
+    for copy in copies[1 + tiles : -1]:
+        copy.wait()
+    for p in range(tiles):
         put_shards(lefts, 1, first, position, p, 0, panel_rank[p])
         put_shards(panels, 0, first, position, p, 1, panel_rank[p])
         for t in range(3):
@@ -379,6 +452,7 @@
         whole = jnp.concatenate([products[r, t] for r in range(products.shape[0])], axis=1)
         sides.append(col_component(cols, 5 + t, col_rank[0]) - whole)
     sides = jnp.concatenate(sides, axis=0) * scale[...]
+    copies[-1].wait()
     dz = dot_split(split2(sides), split2(inverse[...])) * scale[...]
     z_hi, z_lo = split2(solved[...])
     dz_hi, dz_lo = split2(dz)
@@ -446,6 +520,7 @@
         basis = dot_split(split2(basis_coef), take(lefts, slot(p, 0, 8))) * up_scale
         for t in range(4):
             out[p, 0, t] = band(basis, t)
+        store(p, 0)
         dq_parts = mm(basis_coef[rank_count:], cross, NT)
         on_u = mm(
             block(dq_parts, 1)
@@ -467,6 +542,9 @@
         )
         for t in range(4):
             out[p, 0, 4 + t] = band(coeff, t)
+        store(p, 4)
+    for copy in stores:
+        copy.wait()
 
 
 def run_recompress(
@@ -476,13 +554,27 @@
     rank_count, size = sketch.shape
     vmem = pl.BlockSpec(memory_space=pltpu.VMEM)
     smem = pl.BlockSpec(memory_space=pltpu.SMEM)
+    hbm = pl.BlockSpec(memory_space=pl.ANY)
     return pl.pallas_call(
         functools.partial(recompress_kernel, tiles, len(first)),
         out_shape=jax.ShapeDtypeStruct(trailing.shape, F32),
-        in_specs=[smem] * 5 + [vmem] * (2 * len(first) + 7),
-        out_specs=vmem,
+        in_specs=[smem] * 5
+        + [hbm] * (2 * len(first) + 2)
+        + [vmem] * 2
+        + [hbm]
+        + [vmem] * 2,
+        out_specs=hbm,
         scratch_shapes=[pltpu.VMEM((tiles, 8 * rank_count, size), BF16)] * 4
-        + [pltpu.VMEM((tiles, 4 * rank_count, size), BF16)] * 2,
+        + [pltpu.VMEM((tiles, 4 * rank_count, size), BF16)] * 2
+        + [
+            pltpu.VMEM(cols.shape, F32),
+            pltpu.VMEM(trailing.shape, F32),
+            pltpu.VMEM((len(first),) + first[0].shape, F32),
+            pltpu.VMEM((len(second),) + second[0].shape, F32),
+            pltpu.VMEM(inverse.shape, F32),
+            pltpu.VMEM(trailing.shape, F32),
+            pltpu.SemaphoreType.DMA((2 + tiles + 2 * len(first) + 2 * tiles,)),
+        ],
         compiler_params=pltpu.CompilerParams(vmem_limit_bytes=RECOMPRESS_VMEM),
         cost_estimate=pl.CostEstimate(
             flops=10 * 10**9, bytes_accessed=20 * 2**20, transcendentals=0
@@ -536,7 +628,7 @@
         cols = cols.reshape(-1, SUB // own_ranks, comps, own_ranks, size)
         cols = cols.transpose(0, 2, 1, 3, 4).reshape(-1, comps, SUB, size)
     inverse, solved, products, scale = run_inverse(
-        gathered, diag[1:], col_rank, own_rows, own_ranks
+        gathered, diag, col_rank, own_ranks
     )
     all_products = lax.all_gather(products, "row", axis=0)
     place = lax.axis_index("col").astype(jnp.int32).reshape(1)

time: 153 us -> 146 us (0.954)
  Pallas kernels: 78.1 us -> 71.5 us
  waiting for transfers between devices: 21.5 us -> 23.2 us
    pallas_call x1, Pallas kernels: 56.3 us -> 49.5 us  [run_inverse(): pl.pallas_call(functools.partial(inverse_kernel, own_rows), out_shape=(ja...]
    all_gather x1, waiting for transfers between devices: 21.4 us -> 23.2 us  [on_device(): lax.all_gather(jnp.concatenate([own, values], axis=0), 'row', axis=0)]
    slice x1 -> x0, local copies, waits for them, and re-layouts: 1.68 us -> none  [on_device(): diag[1:]]
    unnamed x28 -> x32, local copies, waits for them, and re-layouts: 11.7 us -> 12 us
  transfers between devices with their start and end apart: 8 -> 8, of which waited for: 1 -> 1; matrix products, arithmetic and copies ran while one was open for 1% -> 0% of each run, Pallas kernels for 37% -> 34%
where the time goes in v4:
time: 146 us
  Pallas kernels  71.5 us (49%)
  waiting for transfers between devices  23.2 us (16%)
  between operations  14.2 us (10%)
  local copies, waits for them, and re-layouts  14.1 us (10%)
  starting transfers between devices  11.7 us (8%)
  blocking collectives  10.3 us (7%)
    pallas_call x1, Pallas kernels, run_inverse(): pl.pallas_call(functools.partial(inverse_kernel, own_rows), out_shape=(ja...  49.5 us
    all_gather x1, waiting for transfers between devices, on_device(): lax.all_gather(jnp.concatenate([own, values], axis=0), 'row', axis=0)  23.2 us
    pallas_call x1, Pallas kernels, run_recompress(): pl.pallas_call(functools.partial(recompress_kernel, tiles, len(first)), o...  22 us
    unnamed x32, local copies, waits for them, and re-layouts  12 us
    ppermute x6, starting transfers between devices, on_device(): lax.ppermute(source, 'col', [(i, (i + s) % col_count) for i in range(col_...  11.6 us
    all_gather x1, blocking collectives, on_device(): all_products = lax.all_gather(products, 'row', axis=0)  10.3 us
  transfers between devices with their start and end apart: 8, of which 1 were waited for; matrix products, arithmetic and copies ran while one was open for 0% of the time, Pallas kernels for 34%

profile of v4, /device:TPU:0, one launch (start us, length us, event | category | flops | bytes accessed | tf_op | source)
XLA Modules:
  0.0 146.0 jit_solution(4871658867438934506)
XLA Ops:
  6.5 0.8 slice_bitcast_fusion.1
  7.4 1.1 slice_bitcast_fusion
  8.5 0.0 copy-start.13
  8.5 0.0 copy-start.14
  8.5 0.1 fusion
  8.6 0.8 pad_maximum_fusion.1
  9.4 0.0 all-gather.6.cloned.1.call-update
  9.4 0.0 all-gather.8.cloned.1.call-start
  9.5 5.1 %collective-permute-start.2 = (f32[2,2,64,256]{3,2,1,0:T(8,128)S(1)}, f32[2,2,64,256]{3,2,1,0:T(8,128)S(1)}, u32[]{:S(2)}, u32[]{:S(2)}) collective-permute-start(f32[2,2,64,256]{3,2,1,0:T(8,128)S(1)} %slice.25.refs_0_), channel_id=1, source_target_pairs={{0,3},{1,0},{2,1},{3,2},{4,7},{5,4},{6,5},{7,6},{8,11},{9,8},{10,9... | collective-permute-start | bytes 786440 | tf_op jit(solution)/shard_map/ppermute | solution.py:623
  14.6 1.0 collective-permute-start
  15.6 0.1 fusion.1
  15.7 0.1 pad_maximum_fusion.refs_4_
  15.7 2.9 %collective-permute-start.5 = (f32[2,6,64,256]{3,2,1,0:T(8,128)S(1)}, f32[2,6,64,256]{3,2,1,0:T(8,128)S(1)}, u32[]{:S(2)}, u32[]{:S(2)}) collective-permute-start(f32[2,6,64,256]{3,2,1,0:T(8,128)S(1)} %pad_maximum_fusion.refs_4_), channel_id=1, source_target_pairs={{0,3},{1,0},{2,1},{3,2},{4,7},{5,4},{6,5},{7,6},{8,11},{9,8},{10,9... | collective-permute-start | bytes 2359304 | tf_op jit(solution)/shard_map/ppermute | solution.py:623
  18.6 1.1 collective-permute-start.4
  20.4 0.1 copy.12.tile_rank
  20.5 0.1 copy.13.keep_rank
  20.6 23.2 %all-gather.6.cloned.1.call-done = f32[1152,640]{1,0:T(8,128)} async-done(((f32[144,640]{1,0:T(8,128)}), f32[1152,640]{1,0:T(8,128)}) %all-gather.6.cloned.1.call-update) | async-done | bytes 2949136 | tf_op jit(solution)/shard_map/all_gather | solution.py:616
  43.7 0.0 all-gather.8.cloned.1.call-update
  43.8 1.5 %collective-permute-start.3 = (f32[2,6,64,256]{3,2,1,0:T(8,128)S(1)}, f32[2,6,64,256]{3,2,1,0:T(8,128)S(1)}, u32[]{:S(2)}, u32[]{:S(2)}) collective-permute-start(f32[2,6,64,256]{3,2,1,0:T(8,128)S(1)} %pad_maximum_fusion.refs_4_), channel_id=1, source_target_pairs={{0,1},{1,2},{2,3},{3,0},{4,5},{5,6},{6,7},{7,4},{8,9},{9,10},{10,1... | collective-permute-start | bytes 2359304 | tf_op jit(solution)/shard_map/ppermute | solution.py:623
  45.3 1.6 %copy-done = f32[4,128,1024]{2,1,0:T(8,128)S(1)} copy-done((f32[4,128,1024]{2,1,0:T(8,128)S(1)}, f32[4,128,1024]{2,1,0:T(8,128)}, u32[]{:S(2)}) %copy-start) | copy-done | bytes 2097176
  46.9 1.8 %copy-done.1 = f32[1152,640]{1,0:T(8,128)S(1)} copy-done((f32[1152,640]{1,0:T(8,128)S(1)}, f32[1152,640]{1,0:T(8,128)}, u32[]{:S(2)}) %copy-start.1) | copy-done | bytes 2949144
  48.8 49.5 %inverse.1 = (f32[1024,1024]{1,0:T(8,128)S(1)}, f32[64,1024]{1,0:T(8,128)S(1)}, f32[3,64,128]{2,1,0:T(8,128)S(1)}, f32[1,1024]{1,0:T(1,128)S(1)}) custom-call(f32[8,144,640]{2,1,0:T(8,128)S(1)} %bitcast.10, s32[1]{0:T(128)S(6)} %copy.14.col_rank, f32[4,128,1024]{2,1,0:T(8,128)S(1)} %copy-done), custom_call_target="tpu_custom_call" | custom-call | flops 40000000000 | bytes 10485760 | tf_op jit(solution)/shard_map/inverse/pallas_call | solution.py:298
  98.3 1.9 %copy-done.9 = f32[1024,1024]{1,0:T(8,128)} copy-done((f32[1024,1024]{1,0:T(8,128)}, f32[1024,1024]{1,0:T(8,128)S(1)}, u32[]{:S(2)}) %copy-start.9) | copy-done | bytes 4194328
  100.3 10.3 %all-gather.2 = f32[24,64,128]{2,1,0:T(8,128)S(1)} all-gather(f32[3,64,128]{2,1,0:T(8,128)S(1)} %get-tuple-element.16), channel_id=4, replica_groups=mesh['row'=8,'col'=4] {'row'}, dimensions={0}, use_global_device_ids=true | all-gather | bytes 884736 | tf_op jit(solution)/shard_map/all_gather | solution.py:633
  110.6 0.0 copy-start.3
  110.7 0.9 copy-done.3
  111.5 1.6 %copy-done.2 = f32[64,8,1024]{2,1,0:T(8,128)S(1)} copy-done((f32[64,8,1024]{2,1,0:T(8,128)S(1)}, f32[64,8,1024]{2,1,0:T(8,128)}, u32[]{:S(2)}) %copy-start.2) | copy-done | bytes 2097176
  113.1 1.1 copy-done.4
  114.3 0.9 copy-done.5
  115.2 0.9 copy-done.7
  116.2 0.9 copy-done.11
  117.1 22.0 %recompress.1 = f32[2,1,8,64,1024]{4,3,2,1,0:T(8,128)} custom-call(s32[1]{0:T(128)} %bitcast.place, s32[2]{0:T(128)S(1)} %copy-done.8, s32[1]{0:T(128)S(6)} %copy.14.col_rank, s32[2,1]{1,0:T(2,128)S(1)} %copy.12.tile_rank, s32[2,1]{1,0:T(2,128)S(1)} %copy.13.keep_rank, f32[2,2,64,256]{3,2,1,0:T(8,128)S(1)} %slice.25.refs_0_, ...), custom_call_target="tpu_custom_call" | custom-call | flops 10000000000 | bytes 20971520 | tf_op jit(solution)/shard_map/recompress/pallas_call | solution.py:558
  (30 shorter events, 0.1 us)
Async XLA Ops:
  6.5 2.9 %copy-start.12 = (f32[2,8,64,256]{3,2,1,0:T(8,128)S(1)}, f32[2,8,64,256]{3,2,1,0:T(8,128)}, u32[]{:S(2)}) copy-start(f32[2,8,64,256]{3,2,1,0:T(8,128)} %param.10) | copy-start | bytes 3145732
  6.5 37.2 %all-gather.6.cloned.1.call-start = ((), (), s32[]{:S(2)}) async-start(), calls=%async_computation | async-start | bytes 3317760 | tf_op jit(solution)/shard_map/all_gather | solution.py:616
  8.5 11.9 %copy-start.13 = (s32[2,1]{0,1:T(1,128)S(1)}, s32[2,1]{0,1:T(1,128)}, u32[]{:S(2)}) copy-start(s32[2,1]{0,1:T(1,128)} %param.16) | copy-start | bytes 28
  8.5 12.0 %copy-start.14 = (s32[2,1]{0,1:T(1,128)S(1)}, s32[2,1]{0,1:T(1,128)}, u32[]{:S(2)}) copy-start(s32[2,1]{0,1:T(1,128)} %param.17) | copy-start | bytes 28
  9.4 102.1 %all-gather.8.cloned.1.call-start = ((), (), s32[]{:S(2)}) async-start(), calls=%async_computation.1 | async-start | bytes 2359296 | tf_op jit(solution)/shard_map/all_gather | solution.py:626
  9.5 34.3 %collective-permute-start.2 = (f32[2,2,64,256]{3,2,1,0:T(8,128)S(1)}, f32[2,2,64,256]{3,2,1,0:T(8,128)S(1)}, u32[]{:S(2)}, u32[]{:S(2)}) collective-permute-start(f32[2,2,64,256]{3,2,1,0:T(8,128)S(1)} %slice.25.refs_0_), channel_id=1, source_target_pairs={{0,3},{1,0},{2,1},{3,2},{4,7},{5,4},{6,5},{7,6},{8,11},{9,8},{10,9... | collective-permute-start | bytes 786440 | tf_op jit(solution)/shard_map/ppermute | solution.py:623
  14.6 96.0 %collective-permute-start.1 = (f32[2,2,64,256]{3,2,1,0:T(8,128)S(1)}, f32[2,2,64,256]{3,2,1,0:T(8,128)}, u32[]{:S(2)}, u32[]{:S(2)}) collective-permute-start(f32[2,2,64,256]{3,2,1,0:T(8,128)S(1)} %slice.25.refs_0_), channel_id=1, source_target_pairs={{0,2},{1,3},{2,0},{3,1},{4,6},{5,7},{6,4},{7,5},{8,10},{9,11},{10,... | collective-permute-start | bytes 786440 | tf_op jit(solution)/shard_map/ppermute | solution.py:623
  14.6 96.0 %collective-permute-start = (f32[2,2,64,256]{3,2,1,0:T(8,128)S(1)}, f32[2,2,64,256]{3,2,1,0:T(8,128)}, u32[]{:S(2)}, u32[]{:S(2)}) collective-permute-start(f32[2,2,64,256]{3,2,1,0:T(8,128)S(1)} %slice.25.refs_0_), channel_id=1, source_target_pairs={{0,1},{1,2},{2,3},{3,0},{4,5},{5,6},{6,7},{7,4},{8,9},{9,10},{10,1... | collective-permute-start | bytes 786440 | tf_op jit(solution)/shard_map/ppermute | solution.py:623
  15.7 94.9 %collective-permute-start.5 = (f32[2,6,64,256]{3,2,1,0:T(8,128)S(1)}, f32[2,6,64,256]{3,2,1,0:T(8,128)S(1)}, u32[]{:S(2)}, u32[]{:S(2)}) collective-permute-start(f32[2,6,64,256]{3,2,1,0:T(8,128)S(1)} %pad_maximum_fusion.refs_4_), channel_id=1, source_target_pairs={{0,3},{1,0},{2,1},{3,2},{4,7},{5,4},{6,5},{7,6},{8,11},{9,8},{10,9... | collective-permute-start | bytes 2359304 | tf_op jit(solution)/shard_map/ppermute | solution.py:623
  18.6 92.0 %collective-permute-start.4 = (f32[2,6,64,256]{3,2,1,0:T(8,128)S(1)}, f32[2,6,64,256]{3,2,1,0:T(8,128)S(1)}, u32[]{:S(2)}, u32[]{:S(2)}) collective-permute-start(f32[2,6,64,256]{3,2,1,0:T(8,128)S(1)} %pad_maximum_fusion.refs_4_), channel_id=1, source_target_pairs={{0,2},{1,3},{2,0},{3,1},{4,6},{5,7},{6,4},{7,5},{8,10},{9,11},{10,... | collective-permute-start | bytes 2359304 | tf_op jit(solution)/shard_map/ppermute | solution.py:623
  43.7 67.8 %copy-start.8 = (s32[2]{0:T(128)S(1)}, s32[2]{0:T(128)}, u32[]{:S(2)}) copy-start(s32[2]{0:T(128)} %panel_rank.1) | copy-start | bytes 28
  43.8 54.5 %copy-start.6 = (f32[2,2,64,256]{3,2,1,0:T(8,128)}, f32[2,2,64,256]{3,2,1,0:T(8,128)S(1)}, u32[]{:S(2)}) copy-start(f32[2,2,64,256]{3,2,1,0:T(8,128)S(1)} %collective-permute-done.2.refs_3_) | copy-start | bytes 786436
  43.8 66.8 %collective-permute-start.3 = (f32[2,6,64,256]{3,2,1,0:T(8,128)S(1)}, f32[2,6,64,256]{3,2,1,0:T(8,128)S(1)}, u32[]{:S(2)}, u32[]{:S(2)}) collective-permute-start(f32[2,6,64,256]{3,2,1,0:T(8,128)S(1)} %pad_maximum_fusion.refs_4_), channel_id=1, source_target_pairs={{0,1},{1,2},{2,3},{3,0},{4,5},{5,6},{6,7},{7,4},{8,9},{9,10},{10,1... | collective-permute-start | bytes 2359304 | tf_op jit(solution)/shard_map/ppermute | solution.py:623
  45.3 1.6 %copy-start = (f32[4,128,1024]{2,1,0:T(8,128)S(1)}, f32[4,128,1024]{2,1,0:T(8,128)}, u32[]{:S(2)}) copy-start(f32[4,128,1024]{2,1,0:T(8,128)} %diag.1) | copy-start | bytes 6291460
  46.9 1.8 %copy-start.1 = (f32[1152,640]{1,0:T(8,128)S(1)}, f32[1152,640]{1,0:T(8,128)}, u32[]{:S(2)}) copy-start(f32[1152,640]{1,0:T(8,128)} %all-gather.6.cloned.1.call-done) | copy-start | bytes 8847364
  98.3 2.0 %copy-start.9 = (f32[1024,1024]{1,0:T(8,128)}, f32[1024,1024]{1,0:T(8,128)S(1)}, u32[]{:S(2)}) copy-start(f32[1024,1024]{1,0:T(8,128)S(1)} %get-tuple-element.14.refs_12_) | copy-start | bytes 12582916
  100.3 10.4 %copy-start.10 = (f32[64,1024]{1,0:T(8,128)}, f32[64,1024]{1,0:T(8,128)S(1)}, u32[]{:S(2)}) copy-start(f32[64,1024]{1,0:T(8,128)S(1)} %get-tuple-element.13.refs_11_) | copy-start | bytes 786436
  110.6 0.9 copy-start.3
  111.5 1.6 %copy-start.2 = (f32[64,8,1024]{2,1,0:T(8,128)S(1)}, f32[64,8,1024]{2,1,0:T(8,128)}, u32[]{:S(2)}) copy-start(f32[64,8,1024]{2,1,0:T(8,128)} %all-gather.8.cloned.1.call-done) | copy-start | bytes 6291460
  113.1 1.1 copy-start.4
  114.3 0.9 copy-start.5
  115.2 0.9 copy-start.7
  116.2 0.9 copy-start.11
Sparse Core Ops, SparseCore 0:
  9.5 34.1 all-gather.5
  45.6 27.9 all-gather.7

commit v5 on v4

--- a/solution.py
+++ b/solution.py
@@ -116,12 +116,42 @@
     return cols, [scale * c for c in low]
 
 
-def block_inverse(rows, work):
-    rows = list(rows)
+def band_left(x, band):
+    lanes = BAND * SUB
+    hi = x.astype(BF16).astype(F32)
+    rest = x - hi
+    mid = rest.astype(BF16).astype(F32)
+    lo = rest - mid
+    place = lax.rem(
+        lax.broadcasted_iota(jnp.int32, x.shape, 1) // lanes - band + BLOCK // lanes, BLOCK // lanes
+    )
+    hi_next = pltpu.roll(hi, lanes, 1)
+    mid_two = pltpu.roll(mid, 2 * lanes, 1)
+    mid_three = pltpu.roll(mid, 3 * lanes, 1)
+    one = jnp.where(
+        place == 0, hi, jnp.where(place == 1, hi_next, jnp.where(place == 2, mid_two, mid_three))
+    )
+    two = jnp.where(place == 0, lo, jnp.where(place == 1, hi_next, 0.0))
+    return jnp.concatenate([one, two], axis=1).astype(BF16)
+
+
+def band_right(x, band):
+    hi, mid, lo = split3(x)
+    none = jnp.zeros(x.shape, BF16)
+    turn = lambda parts: [parts[(i - band) % len(parts)] for i in range(len(parts))]
+    return jnp.concatenate(turn([hi, mid, hi, mid]) + turn([hi, lo, none, none]), axis=0)
+
+
+def block_inverse(rows, ahead, below, below_ahead, work):
+    rows, ahead, below, below_ahead = list(rows), list(ahead), list(below), list(below_ahead)
     count = len(rows)
     sub, lane = sub_index(), lane_index()
     for first in range(0, count, BAND):
         band = range(first, first + BAND)
+        others = [(first + BAND + i) % count for i in range(count - BAND)]
+        left = band_left(
+            jnp.concatenate([rows[i] for i in others] + below, axis=0), first // BAND
+        )
         for g in band:
             at = g * SUB
             inside = (lane >= at) & (lane < at + SUB)
@@ -129,22 +159,31 @@
             own = jnp.where(inside, jnp.where(lane - at == sub, 1.0, 0.0), rows[g])
             new = tree_sum([inv[k] * sub_rep(own, k) for k in range(SUB)])
             news = [sub_rep(new, k) for k in range(SUB)]
+            new_ahead = tree_sum([inv[k] * sub_rep(ahead[g], k) for k in range(SUB)])
+            news_ahead = [sub_rep(new_ahead, k) for k in range(SUB)]
             for i in [first + (g - first + 1 + i) % BAND for i in range(BAND - 1)]:
+                factors = [lane_rep(rows[i], at + k) for k in range(SUB)]
                 kept = jnp.where(inside, 0.0, rows[i])
-                rows[i] = kept - tree_sum(
-                    [lane_rep(rows[i], at + k) * news[k] for k in range(SUB)]
-                )
-            rows[g] = new
+                rows[i] = kept - tree_sum([factors[k] * news[k] for k in range(SUB)])
+                ahead[i] = ahead[i] - tree_sum([factors[k] * news_ahead[k] for k in range(SUB)])
+            rows[g], ahead[g] = new, new_ahead
             for piece in work[g * len(work) // count : (g + 1) * len(work) // count]:
                 piece()
         inside = (lane >= first * SUB) & (lane < (first + BAND) * SUB)
-        others = [(first + BAND + i) % count for i in range(count - BAND)]
-        none = jnp.zeros((SUB, BLOCK), F32)
-        padded = jnp.concatenate([rows[i] if i in band else none for i in range(count)], axis=0)
-        change = as_rows(mm(jnp.concatenate([rows[i] for i in others], axis=0), padded))
-        for i, delta in zip(others, change):
-            rows[i] = jnp.where(inside, 0.0, rows[i]) - delta
-    return rows
+        top = jnp.concatenate(
+            [jnp.concatenate([x[i] for i in band], axis=0) for x in (rows, ahead)], axis=1
+        )
+        change = lax.dot_general(
+            left, band_right(top, first // BAND), NN, preferred_element_type=F32
+        )
+        here, there = as_rows(change[:, :BLOCK]), as_rows(change[:, BLOCK:])
+        for j, i in enumerate(others):
+            rows[i] = jnp.where(inside, 0.0, rows[i]) - here[j]
+            ahead[i] = ahead[i] - there[j]
+        for j in range(count):
+            below[j] = below[j] - here[len(others) + j]
+            below_ahead[j] = below_ahead[j] - there[len(others) + j]
+    return rows, below_ahead
 
 
 def factor_inverse(rows, width):
@@ -171,7 +210,7 @@
 
 def inverse_kernel(
     own_rows,
-    gathered,
+    gathered_hbm,
     col_rank,
     diag,
     inverse_out,
@@ -180,7 +219,9 @@
     scale_row,
     inverse,
     tangents,
+    gathered,
     pivot,
+    upcoming,
     left,
     right,
     scale_col,
@@ -190,7 +231,10 @@
     steps = size // BLOCK
     shards, height, width = gathered.shape
     fetch = pltpu.make_async_copy(diag.at[pl.ds(1, 3)], tangents, sems.at[0])
+    receive = pltpu.make_async_copy(gathered_hbm, gathered, sems.at[2])
+    receive.start()
     fetch.start()
+    receive.wait()
     eye = lax.broadcasted_iota(jnp.int32, (BLOCK, BLOCK), 0) == lax.broadcasted_iota(
         jnp.int32, (BLOCK, BLOCK), 1
     )
@@ -254,17 +298,26 @@
             work += [functools.partial(update, r, c) for r in range(chunks)]
         return work
 
-    def invert_to_pivot(block, work):
-        pivot[...] = jnp.concatenate(block_inverse(as_rows(block), work), axis=0)
-
-    invert_to_pivot(inverse[:BLOCK, :BLOCK], [])
+    def invert_to_pivot(blocks, work):
+        inv, following = block_inverse(*[as_rows(block) for block in blocks], work)
+        pivot[...] = jnp.concatenate(inv, axis=0)
+        upcoming[...] = jnp.concatenate(following, axis=0)
+
+    one, two = part(0), part(1)
+    invert_to_pivot([inverse[one, one], inverse[one, two], inverse[two, one], inverse[two, two]], [])
 
     def step(k, carry):
         at = pl.ds(pl.multiple_of(k * BLOCK, BLOCK), BLOCK)
-        nxt = pl.ds(pl.multiple_of((k + 1) * BLOCK, BLOCK), BLOCK)
+        one = pl.ds(pl.multiple_of((k + 1) * BLOCK, BLOCK), BLOCK)
+        two = pl.ds(pl.multiple_of(lax.min(k + 2, steps - 1) * BLOCK, BLOCK), BLOCK)
         inv = pivot[...]
-        block = inverse[nxt, nxt] - mm(inverse[nxt, at], mm(inv, inverse[at, nxt]))
-        invert_to_pivot(block, eliminate(k, at, inv))
+        block = upcoming[...]
+        row = mm(inv, jnp.concatenate([inverse[at, one], inverse[at, two]], axis=1))
+        ahead = inverse[one, two] - mm(inverse[one, at], row[:, BLOCK:])
+        change = mm(inverse[two, at], row)
+        below = inverse[two, one] - change[:, :BLOCK]
+        below_ahead = inverse[two, two] - change[:, BLOCK:]
+        invert_to_pivot([block, ahead, below, below_ahead], eliminate(k, at, inv))
         return carry
 
     lax.fori_loop(0, steps - 1, step, 0)
@@ -295,6 +348,7 @@
     _, own_rows, size = diag.shape
     rank_count = own_ranks * shards
     vmem = pl.BlockSpec(memory_space=pltpu.VMEM)
+    hbm = pl.BlockSpec(memory_space=pltpu.HBM)
     return pl.pallas_call(
         functools.partial(inverse_kernel, own_rows),
         out_shape=(
@@ -303,20 +357,18 @@
             jax.ShapeDtypeStruct((3, rank_count, own_rows), F32),
             jax.ShapeDtypeStruct((1, size), F32),
         ),
-        in_specs=[
-            vmem,
-            pl.BlockSpec(memory_space=pltpu.SMEM),
-            pl.BlockSpec(memory_space=pl.ANY),
-        ],
-        out_specs=(pl.BlockSpec(memory_space=pl.ANY), vmem, vmem, vmem),
+        in_specs=[hbm, pl.BlockSpec(memory_space=pltpu.SMEM), hbm],
+        out_specs=(hbm, vmem, vmem, vmem),
         scratch_shapes=[
             pltpu.VMEM((size, size), F32),
             pltpu.VMEM((3, own_rows, size), F32),
+            pltpu.VMEM(gathered.shape, F32),
+            pltpu.VMEM((BLOCK, BLOCK), F32),
             pltpu.VMEM((BLOCK, BLOCK), F32),
             pltpu.VMEM((size, 6 * BLOCK), BF16),
             pltpu.VMEM((6 * BLOCK, size), BF16),
             pltpu.VMEM((size, BLOCK), F32),
-            pltpu.SemaphoreType.DMA((2,)),
+            pltpu.SemaphoreType.DMA((3,)),
         ],
         compiler_params=pltpu.CompilerParams(vmem_limit_bytes=INVERSE_VMEM),
         cost_estimate=pl.CostEstimate(
@@ -375,11 +427,11 @@
     (
         cols_any,
         trailing_any,
-        sketch,
-        solved,
+        sketch_any,
+        solved_any,
         inverse_any,
         scale,
-        products,
+        products_any,
         out_any,
         left_hi,
         left_lo,
@@ -392,6 +444,9 @@
         first_all,
         second_all,
         inverse,
+        sketch,
+        solved,
+        products,
         out,
         sems,
     ) = refs[2 * shards :]
@@ -400,6 +455,7 @@
     pairs = [(cols_any, cols)]
     pairs += [(trailing_any.at[p], trailing.at[p]) for p in range(tiles)]
     pairs += list(zip(first_any, first)) + list(zip(second_any, second))
+    pairs += [(sketch_any, sketch), (solved_any, solved), (products_any, products)]
     pairs.append((inverse_any, inverse))
     copies = [
         pltpu.make_async_copy(source, target, sems.at[i])
@@ -554,15 +610,13 @@
     rank_count, size = sketch.shape
     vmem = pl.BlockSpec(memory_space=pltpu.VMEM)
     smem = pl.BlockSpec(memory_space=pltpu.SMEM)
-    hbm = pl.BlockSpec(memory_space=pl.ANY)
+    hbm = pl.BlockSpec(memory_space=pltpu.HBM)
     return pl.pallas_call(
         functools.partial(recompress_kernel, tiles, len(first)),
         out_shape=jax.ShapeDtypeStruct(trailing.shape, F32),
         in_specs=[smem] * 5
-        + [hbm] * (2 * len(first) + 2)
-        + [vmem] * 2
-        + [hbm]
-        + [vmem] * 2,
+        + [hbm] * (2 * len(first) + 5)
+        + [vmem, hbm],
         out_specs=hbm,
         scratch_shapes=[pltpu.VMEM((tiles, 8 * rank_count, size), BF16)] * 4
         + [pltpu.VMEM((tiles, 4 * rank_count, size), BF16)] * 2
@@ -572,8 +626,11 @@
             pltpu.VMEM((len(first),) + first[0].shape, F32),
             pltpu.VMEM((len(second),) + second[0].shape, F32),
             pltpu.VMEM(inverse.shape, F32),
+            pltpu.VMEM(sketch.shape, F32),
+            pltpu.VMEM(solved.shape, F32),
+            pltpu.VMEM(products.shape, F32),
             pltpu.VMEM(trailing.shape, F32),
-            pltpu.SemaphoreType.DMA((2 + tiles + 2 * len(first) + 2 * tiles,)),
+            pltpu.SemaphoreType.DMA((5 + tiles + 2 * len(first) + 2 * tiles,)),
         ],
         compiler_params=pltpu.CompilerParams(vmem_limit_bytes=RECOMPRESS_VMEM),
         cost_estimate=pl.CostEstimate(

time: 146 us -> 146 us (level)
  no operation moved by 1% of the time
where the time goes in v5:
time: 146 us; the launch traced here: 145 us
  Pallas kernels  71 us (49%)
  waiting for transfers between devices  23.2 us (16%)
  between operations  14.2 us (10%)
  local copies, waits for them, and re-layouts  14.1 us (10%)
  starting transfers between devices  11.7 us (8%)
  blocking collectives  10.3 us (7%)
    pallas_call x1, Pallas kernels, run_inverse(): pl.pallas_call(functools.partial(inverse_kernel, own_rows), out_shape=(ja...  49 us
    all_gather x1, waiting for transfers between devices, on_device(): lax.all_gather(jnp.concatenate([own, values], axis=0), 'row', axis=0)  23.2 us
    pallas_call x1, Pallas kernels, run_recompress(): pl.pallas_call(functools.partial(recompress_kernel, tiles, len(first)), o...  22 us
    unnamed x32, local copies, waits for them, and re-layouts  12 us
    ppermute x6, starting transfers between devices, on_device(): lax.ppermute(source, 'col', [(i, (i + s) % col_count) for i in range(col_...  11.6 us
    all_gather x1, blocking collectives, on_device(): all_products = lax.all_gather(products, 'row', axis=0)  10.3 us
  transfers between devices with their start and end apart: 8, of which 1 were waited for; matrix products, arithmetic and copies ran while one was open for 0% of the time, Pallas kernels for 34%

profile of v5, /device:TPU:0, one launch (start us, length us, event | category | flops | bytes accessed | tf_op | source)
XLA Modules:
  0.0 145.4 jit_solution(17148796299431041889)
XLA Ops:
  6.5 0.8 slice_bitcast_fusion.1
  7.4 1.1 slice_bitcast_fusion
  8.5 0.0 copy-start.13
  8.5 0.0 copy-start.14
  8.5 0.1 fusion
  8.6 0.8 pad_maximum_fusion.1
  9.4 0.0 all-gather.6.cloned.1.call-update
  9.4 0.0 all-gather.8.cloned.1.call-start
  9.5 5.1 %collective-permute-start.2 = (f32[2,2,64,256]{3,2,1,0:T(8,128)S(1)}, f32[2,2,64,256]{3,2,1,0:T(8,128)S(1)}, u32[]{:S(2)}, u32[]{:S(2)}) collective-permute-start(f32[2,2,64,256]{3,2,1,0:T(8,128)S(1)} %slice.25.refs_0_), channel_id=1, source_target_pairs={{0,3},{1,0},{2,1},{3,2},{4,7},{5,4},{6,5},{7,6},{8,11},{9,8},{10,9... | collective-permute-start | bytes 786440 | tf_op jit(solution)/shard_map/ppermute | solution.py:680
  14.6 1.0 collective-permute-start
  15.6 0.1 fusion.1
  15.7 0.1 pad_maximum_fusion.refs_4_
  15.7 2.9 %collective-permute-start.5 = (f32[2,6,64,256]{3,2,1,0:T(8,128)S(1)}, f32[2,6,64,256]{3,2,1,0:T(8,128)S(1)}, u32[]{:S(2)}, u32[]{:S(2)}) collective-permute-start(f32[2,6,64,256]{3,2,1,0:T(8,128)S(1)} %pad_maximum_fusion.refs_4_), channel_id=1, source_target_pairs={{0,3},{1,0},{2,1},{3,2},{4,7},{5,4},{6,5},{7,6},{8,11},{9,8},{10,9... | collective-permute-start | bytes 2359304 | tf_op jit(solution)/shard_map/ppermute | solution.py:680
  18.6 1.1 collective-permute-start.4
  20.4 0.1 copy.12.tile_rank
  20.5 0.1 copy.13.keep_rank
  20.6 23.2 %all-gather.6.cloned.1.call-done = f32[1152,640]{1,0:T(8,128)} async-done(((f32[144,640]{1,0:T(8,128)}), f32[1152,640]{1,0:T(8,128)}) %all-gather.6.cloned.1.call-update) | async-done | bytes 2949136 | tf_op jit(solution)/shard_map/all_gather | solution.py:673
  43.7 0.0 all-gather.8.cloned.1.call-update
  43.8 1.5 %collective-permute-start.3 = (f32[2,6,64,256]{3,2,1,0:T(8,128)S(1)}, f32[2,6,64,256]{3,2,1,0:T(8,128)S(1)}, u32[]{:S(2)}, u32[]{:S(2)}) collective-permute-start(f32[2,6,64,256]{3,2,1,0:T(8,128)S(1)} %pad_maximum_fusion.refs_4_), channel_id=1, source_target_pairs={{0,1},{1,2},{2,3},{3,0},{4,5},{5,6},{6,7},{7,4},{8,9},{9,10},{10,1... | collective-permute-start | bytes 2359304 | tf_op jit(solution)/shard_map/ppermute | solution.py:680
  45.3 1.6 %copy-done = f32[4,128,1024]{2,1,0:T(8,128)S(1)} copy-done((f32[4,128,1024]{2,1,0:T(8,128)S(1)}, f32[4,128,1024]{2,1,0:T(8,128)}, u32[]{:S(2)}) %copy-start) | copy-done | bytes 2097176
  46.9 1.8 %copy-done.1 = f32[1152,640]{1,0:T(8,128)S(1)} copy-done((f32[1152,640]{1,0:T(8,128)S(1)}, f32[1152,640]{1,0:T(8,128)}, u32[]{:S(2)}) %copy-start.1) | copy-done | bytes 2949144
  48.8 49.0 %inverse.1 = (f32[1024,1024]{1,0:T(8,128)S(1)}, f32[64,1024]{1,0:T(8,128)S(1)}, f32[3,64,128]{2,1,0:T(8,128)S(1)}, f32[1,1024]{1,0:T(1,128)S(1)}) custom-call(f32[8,144,640]{2,1,0:T(8,128)S(1)} %bitcast.10, s32[1]{0:T(128)S(6)} %copy.14.col_rank, f32[4,128,1024]{2,1,0:T(8,128)S(1)} %copy-done), custom_call_target="tpu_custom_call" | custom-call | flops 40000000000 | bytes 10485760 | tf_op jit(solution)/shard_map/inverse/pallas_call | solution.py:352
  97.7 1.9 %copy-done.9 = f32[1024,1024]{1,0:T(8,128)} copy-done((f32[1024,1024]{1,0:T(8,128)}, f32[1024,1024]{1,0:T(8,128)S(1)}, u32[]{:S(2)}) %copy-start.9) | copy-done | bytes 4194328
  99.7 10.3 %all-gather.2 = f32[24,64,128]{2,1,0:T(8,128)S(1)} all-gather(f32[3,64,128]{2,1,0:T(8,128)S(1)} %get-tuple-element.16), channel_id=4, replica_groups=mesh['row'=8,'col'=4] {'row'}, dimensions={0}, use_global_device_ids=true | all-gather | bytes 884736 | tf_op jit(solution)/shard_map/all_gather | solution.py:690
  110.1 0.0 copy-start.3
  110.1 0.9 copy-done.3
  111.0 1.6 %copy-done.2 = f32[64,8,1024]{2,1,0:T(8,128)S(1)} copy-done((f32[64,8,1024]{2,1,0:T(8,128)S(1)}, f32[64,8,1024]{2,1,0:T(8,128)}, u32[]{:S(2)}) %copy-start.2) | copy-done | bytes 2097176
  112.6 1.1 copy-done.4
  113.7 0.9 copy-done.5
  114.7 0.9 copy-done.7
  115.6 0.9 copy-done.11
  116.5 22.0 %recompress.1 = f32[2,1,8,64,1024]{4,3,2,1,0:T(8,128)} custom-call(s32[1]{0:T(128)} %bitcast.place, s32[2]{0:T(128)S(1)} %copy-done.8, s32[1]{0:T(128)S(6)} %copy.14.col_rank, s32[2,1]{1,0:T(2,128)S(1)} %copy.12.tile_rank, s32[2,1]{1,0:T(2,128)S(1)} %copy.13.keep_rank, f32[2,2,64,256]{3,2,1,0:T(8,128)S(1)} %slice.25.refs_0_, ...), custom_call_target="tpu_custom_call" | custom-call | flops 10000000000 | bytes 20971520 | tf_op jit(solution)/shard_map/recompress/pallas_call | solution.py:614
  (30 shorter events, 0.1 us)
Async XLA Ops:
  6.5 2.9 %copy-start.12 = (f32[2,8,64,256]{3,2,1,0:T(8,128)S(1)}, f32[2,8,64,256]{3,2,1,0:T(8,128)}, u32[]{:S(2)}) copy-start(f32[2,8,64,256]{3,2,1,0:T(8,128)} %param.10) | copy-start | bytes 3145732
  6.5 37.2 %all-gather.6.cloned.1.call-start = ((), (), s32[]{:S(2)}) async-start(), calls=%async_computation | async-start | bytes 3317760 | tf_op jit(solution)/shard_map/all_gather | solution.py:673
  8.5 11.9 %copy-start.13 = (s32[2,1]{0,1:T(1,128)S(1)}, s32[2,1]{0,1:T(1,128)}, u32[]{:S(2)}) copy-start(s32[2,1]{0,1:T(1,128)} %param.16) | copy-start | bytes 28
  8.5 12.0 %copy-start.14 = (s32[2,1]{0,1:T(1,128)S(1)}, s32[2,1]{0,1:T(1,128)}, u32[]{:S(2)}) copy-start(s32[2,1]{0,1:T(1,128)} %param.17) | copy-start | bytes 28
  9.4 101.6 %all-gather.8.cloned.1.call-start = ((), (), s32[]{:S(2)}) async-start(), calls=%async_computation.1 | async-start | bytes 2359296 | tf_op jit(solution)/shard_map/all_gather | solution.py:683
  9.5 34.3 %collective-permute-start.2 = (f32[2,2,64,256]{3,2,1,0:T(8,128)S(1)}, f32[2,2,64,256]{3,2,1,0:T(8,128)S(1)}, u32[]{:S(2)}, u32[]{:S(2)}) collective-permute-start(f32[2,2,64,256]{3,2,1,0:T(8,128)S(1)} %slice.25.refs_0_), channel_id=1, source_target_pairs={{0,3},{1,0},{2,1},{3,2},{4,7},{5,4},{6,5},{7,6},{8,11},{9,8},{10,9... | collective-permute-start | bytes 786440 | tf_op jit(solution)/shard_map/ppermute | solution.py:680
  14.6 95.5 %collective-permute-start.1 = (f32[2,2,64,256]{3,2,1,0:T(8,128)S(1)}, f32[2,2,64,256]{3,2,1,0:T(8,128)}, u32[]{:S(2)}, u32[]{:S(2)}) collective-permute-start(f32[2,2,64,256]{3,2,1,0:T(8,128)S(1)} %slice.25.refs_0_), channel_id=1, source_target_pairs={{0,2},{1,3},{2,0},{3,1},{4,6},{5,7},{6,4},{7,5},{8,10},{9,11},{10,... | collective-permute-start | bytes 786440 | tf_op jit(solution)/shard_map/ppermute | solution.py:680
  14.6 95.5 %collective-permute-start = (f32[2,2,64,256]{3,2,1,0:T(8,128)S(1)}, f32[2,2,64,256]{3,2,1,0:T(8,128)}, u32[]{:S(2)}, u32[]{:S(2)}) collective-permute-start(f32[2,2,64,256]{3,2,1,0:T(8,128)S(1)} %slice.25.refs_0_), channel_id=1, source_target_pairs={{0,1},{1,2},{2,3},{3,0},{4,5},{5,6},{6,7},{7,4},{8,9},{9,10},{10,1... | collective-permute-start | bytes 786440 | tf_op jit(solution)/shard_map/ppermute | solution.py:680
  15.7 94.3 %collective-permute-start.5 = (f32[2,6,64,256]{3,2,1,0:T(8,128)S(1)}, f32[2,6,64,256]{3,2,1,0:T(8,128)S(1)}, u32[]{:S(2)}, u32[]{:S(2)}) collective-permute-start(f32[2,6,64,256]{3,2,1,0:T(8,128)S(1)} %pad_maximum_fusion.refs_4_), channel_id=1, source_target_pairs={{0,3},{1,0},{2,1},{3,2},{4,7},{5,4},{6,5},{7,6},{8,11},{9,8},{10,9... | collective-permute-start | bytes 2359304 | tf_op jit(solution)/shard_map/ppermute | solution.py:680
  18.6 91.5 %collective-permute-start.4 = (f32[2,6,64,256]{3,2,1,0:T(8,128)S(1)}, f32[2,6,64,256]{3,2,1,0:T(8,128)S(1)}, u32[]{:S(2)}, u32[]{:S(2)}) collective-permute-start(f32[2,6,64,256]{3,2,1,0:T(8,128)S(1)} %pad_maximum_fusion.refs_4_), channel_id=1, source_target_pairs={{0,2},{1,3},{2,0},{3,1},{4,6},{5,7},{6,4},{7,5},{8,10},{9,11},{10,... | collective-permute-start | bytes 2359304 | tf_op jit(solution)/shard_map/ppermute | solution.py:680
  43.7 67.2 %copy-start.8 = (s32[2]{0:T(128)S(1)}, s32[2]{0:T(128)}, u32[]{:S(2)}) copy-start(s32[2]{0:T(128)} %panel_rank.1) | copy-start | bytes 28
  43.8 53.9 %copy-start.6 = (f32[2,2,64,256]{3,2,1,0:T(8,128)}, f32[2,2,64,256]{3,2,1,0:T(8,128)S(1)}, u32[]{:S(2)}) copy-start(f32[2,2,64,256]{3,2,1,0:T(8,128)S(1)} %collective-permute-done.2.refs_3_) | copy-start | bytes 786436
  43.8 66.3 %collective-permute-start.3 = (f32[2,6,64,256]{3,2,1,0:T(8,128)S(1)}, f32[2,6,64,256]{3,2,1,0:T(8,128)S(1)}, u32[]{:S(2)}, u32[]{:S(2)}) collective-permute-start(f32[2,6,64,256]{3,2,1,0:T(8,128)S(1)} %pad_maximum_fusion.refs_4_), channel_id=1, source_target_pairs={{0,1},{1,2},{2,3},{3,0},{4,5},{5,6},{6,7},{7,4},{8,9},{9,10},{10,1... | collective-permute-start | bytes 2359304 | tf_op jit(solution)/shard_map/ppermute | solution.py:680
  45.3 1.6 %copy-start = (f32[4,128,1024]{2,1,0:T(8,128)S(1)}, f32[4,128,1024]{2,1,0:T(8,128)}, u32[]{:S(2)}) copy-start(f32[4,128,1024]{2,1,0:T(8,128)} %diag.1) | copy-start | bytes 6291460
  46.9 1.8 %copy-start.1 = (f32[1152,640]{1,0:T(8,128)S(1)}, f32[1152,640]{1,0:T(8,128)}, u32[]{:S(2)}) copy-start(f32[1152,640]{1,0:T(8,128)} %all-gather.6.cloned.1.call-done) | copy-start | bytes 8847364
  97.7 2.0 %copy-start.9 = (f32[1024,1024]{1,0:T(8,128)}, f32[1024,1024]{1,0:T(8,128)S(1)}, u32[]{:S(2)}) copy-start(f32[1024,1024]{1,0:T(8,128)S(1)} %get-tuple-element.14.refs_12_) | copy-start | bytes 12582916
  99.7 10.4 %copy-start.10 = (f32[64,1024]{1,0:T(8,128)}, f32[64,1024]{1,0:T(8,128)S(1)}, u32[]{:S(2)}) copy-start(f32[64,1024]{1,0:T(8,128)S(1)} %get-tuple-element.13.refs_11_) | copy-start | bytes 786436
  110.1 0.9 copy-start.3
  111.0 1.6 %copy-start.2 = (f32[64,8,1024]{2,1,0:T(8,128)S(1)}, f32[64,8,1024]{2,1,0:T(8,128)}, u32[]{:S(2)}) copy-start(f32[64,8,1024]{2,1,0:T(8,128)} %all-gather.8.cloned.1.call-done) | copy-start | bytes 6291460
  112.6 1.1 copy-start.4
  113.7 0.9 copy-start.5
  114.6 0.9 copy-start.7
  115.6 0.9 copy-start.11
Sparse Core Ops, SparseCore 0:
  9.5 34.1 all-gather.5
  45.6 27.8 all-gather.7

commit v6 on v5

--- a/solution.py
+++ b/solution.py
@@ -33,14 +33,19 @@
     return hi, mid, lo
 
 
+def split2(x):
+    hi = x.astype(BF16)
+    return hi, (x - hi.astype(F32)).astype(BF16)
+
+
 def left_terms(x):
-    hi, mid, lo = split3(x)
-    return jnp.concatenate([hi, hi, mid, mid, hi, lo], axis=1)
+    hi, lo = split2(x)
+    return jnp.concatenate([hi, hi, lo, lo], axis=1)
 
 
 def right_terms(x):
-    hi, mid, lo = split3(x)
-    return jnp.concatenate([hi, mid, hi, mid, lo, hi], axis=0)
+    hi, lo = split2(x)
+    return jnp.concatenate([hi, lo, hi, lo], axis=0)
 
 
 def lane_rep(x, lane):
@@ -287,7 +292,7 @@
             inverse[at, part(c, chunk)] = row
 
         def update(r, c):
-            here = (part(r, chunk), part(c, chunk))
+            here = (part(r, 2 * chunk), part(c, chunk))
             inverse[here] = inverse[here] - lax.dot_general(
                 left[here[0], :], right[:, here[1]], NN, preferred_element_type=F32
             )
@@ -295,7 +300,7 @@
         work = [functools.partial(fill_left, c) for c in range(chunks)]
         for c in range(chunks):
             work.append(functools.partial(fill_right, c))
-            work += [functools.partial(update, r, c) for r in range(chunks)]
+            work += [functools.partial(update, r, c) for r in range(chunks // 2)]
         return work
 
     def invert_to_pivot(blocks, work):
@@ -343,16 +348,21 @@
     store.wait()
 
 
+def in_hbm(*arrays):
+    return [pltpu.with_memory_space_constraint(x, pltpu.HBM) for x in arrays]
+
+
 def run_inverse(gathered, diag, col_rank, own_ranks):
     shards = gathered.shape[0]
     _, own_rows, size = diag.shape
     rank_count = own_ranks * shards
     vmem = pl.BlockSpec(memory_space=pltpu.VMEM)
     hbm = pl.BlockSpec(memory_space=pltpu.HBM)
+    gathered, diag = in_hbm(gathered, diag)
     return pl.pallas_call(
         functools.partial(inverse_kernel, own_rows),
         out_shape=(
-            jax.ShapeDtypeStruct((size, size), F32),
+            pltpu.HBM((size, size), F32),
             jax.ShapeDtypeStruct((rank_count, size), F32),
             jax.ShapeDtypeStruct((3, rank_count, own_rows), F32),
             jax.ShapeDtypeStruct((1, size), F32),
@@ -365,8 +375,8 @@
             pltpu.VMEM(gathered.shape, F32),
             pltpu.VMEM((BLOCK, BLOCK), F32),
             pltpu.VMEM((BLOCK, BLOCK), F32),
-            pltpu.VMEM((size, 6 * BLOCK), BF16),
-            pltpu.VMEM((6 * BLOCK, size), BF16),
+            pltpu.VMEM((size, 4 * BLOCK), BF16),
+            pltpu.VMEM((4 * BLOCK, size), BF16),
             pltpu.VMEM((size, BLOCK), F32),
             pltpu.SemaphoreType.DMA((3,)),
         ],
@@ -376,11 +386,6 @@
         ),
         name="inverse",
     )(gathered, col_rank, diag)
-
-
-def split2(x):
-    hi = x.astype(BF16)
-    return hi, (x - hi.astype(F32)).astype(BF16)
 
 
 def dot_split(left, right, dims=NN):
@@ -611,11 +616,15 @@
     vmem = pl.BlockSpec(memory_space=pltpu.VMEM)
     smem = pl.BlockSpec(memory_space=pltpu.SMEM)
     hbm = pl.BlockSpec(memory_space=pltpu.HBM)
+    cols, trailing, sketch, solved, inverse, products = in_hbm(
+        cols, trailing, sketch, solved, inverse, products
+    )
     return pl.pallas_call(
         functools.partial(recompress_kernel, tiles, len(first)),
         out_shape=jax.ShapeDtypeStruct(trailing.shape, F32),
         in_specs=[smem] * 5
-        + [hbm] * (2 * len(first) + 5)
+        + [pl.BlockSpec(memory_space=pl.ANY)] * (2 * len(first))
+        + [hbm] * 5
         + [vmem, hbm],
         out_specs=hbm,
         scratch_shapes=[pltpu.VMEM((tiles, 8 * rank_count, size), BF16)] * 4

time: 146 us -> 136 us (0.932)
  local copies, waits for them, and re-layouts: 14.1 us -> 5.87 us
  Pallas kernels: 71 us -> 69 us
    unnamed x32 -> x14, local copies, waits for them, and re-layouts: 12 us -> 1.85 us
    pallas_call x1, Pallas kernels: 49 us -> 46.1 us  [run_inverse(): pl.pallas_call(functools.partial(inverse_kernel, own_rows), out_shape=(pl...]
    all_gather x1, waiting for transfers between devices: 23.2 us -> 21.1 us  [on_device(): lax.all_gather(jnp.concatenate([own, values], axis=0), 'row', axis=0)]
    ppermute x6, waiting for transfers between devices: 0.02 us -> 1.8 us  [on_device(): lax.ppermute(source, 'col', [(i, (i + s) % col_count) for i in range(col_...]
  transfers between devices with their start and end apart: 8 -> 8, of which waited for: 1 -> 2; matrix products, arithmetic and copies ran while one was open for 0% -> 2% of each run, Pallas kernels for 34% -> 34%
where the time goes in v6:
time: 136 us
  Pallas kernels  69 us (51%)
  waiting for transfers between devices  22.9 us (17%)
  between operations  14.2 us (10%)
  starting transfers between devices  11.6 us (9%)
  blocking collectives  11.3 us (8%)
  local copies, waits for them, and re-layouts  5.87 us (4%)
    pallas_call x1, Pallas kernels, run_inverse(): pl.pallas_call(functools.partial(inverse_kernel, own_rows), out_shape=(pl...  46.1 us
    pallas_call x1, Pallas kernels, run_recompress(): pl.pallas_call(functools.partial(recompress_kernel, tiles, len(first)), o...  22.9 us
    all_gather x1, waiting for transfers between devices, on_device(): lax.all_gather(jnp.concatenate([own, values], axis=0), 'row', axis=0)  21.1 us
    ppermute x6, starting transfers between devices, on_device(): lax.ppermute(source, 'col', [(i, (i + s) % col_count) for i in range(col_...  11.6 us
    all_gather x1, blocking collectives, on_device(): all_products = lax.all_gather(products, 'row', axis=0)  11.3 us
  transfers between devices with their start and end apart: 8, of which 2 were waited for; matrix products, arithmetic and copies ran while one was open for 2% of the time, Pallas kernels for 34%

profile of v6, /device:TPU:0, one launch (start us, length us, event | category | flops | bytes accessed | tf_op | source)
XLA Modules:
  0.0 135.9 jit_solution(8112916327755158487)
XLA Ops:
  6.5 0.8 slice_bitcast_fusion.1
  7.3 1.1 slice_bitcast_fusion
  8.4 0.0 copy-start.4
  8.4 0.0 copy-start.5
  8.4 0.1 fusion
  8.5 0.8 pad_maximum_fusion.1
  9.3 0.0 all-gather.6.cloned.1.call-update
  9.3 0.0 all-gather.8.cloned.1.call-start
  9.4 1.0 slice.25.refs_0_
  10.3 5.1 %collective-permute-start.2 = (f32[2,2,64,256]{3,2,1,0:T(8,128)S(1)}, f32[2,2,64,256]{3,2,1,0:T(8,128)S(1)}, u32[]{:S(2)}, u32[]{:S(2)}) collective-permute-start(f32[2,2,64,256]{3,2,1,0:T(8,128)S(1)} %slice.25.refs_0_), channel_id=1, source_target_pairs={{0,3},{1,0},{2,1},{3,2},{4,7},{5,4},{6,5},{7,6},{8,11},{9,8},{10,9... | collective-permute-start | bytes 786440 | tf_op jit(solution)/shard_map/ppermute | solution.py:689
  15.4 0.0 collective-permute-start.1
  15.4 1.0 collective-permute-start
  16.4 1.2 fusion.1
  17.6 0.1 pad_maximum_fusion.refs_4_
  17.7 2.9 %collective-permute-start.5 = (f32[2,6,64,256]{3,2,1,0:T(8,128)S(1)}, f32[2,6,64,256]{3,2,1,0:T(8,128)S(1)}, u32[]{:S(2)}, u32[]{:S(2)}) collective-permute-start(f32[2,6,64,256]{3,2,1,0:T(8,128)S(1)} %pad_maximum_fusion.refs_4_), channel_id=1, source_target_pairs={{0,3},{1,0},{2,1},{3,2},{4,7},{5,4},{6,5},{7,6},{8,11},{9,8},{10,9... | collective-permute-start | bytes 2359304 | tf_op jit(solution)/shard_map/ppermute | solution.py:689
  20.6 1.1 collective-permute-start.4
  22.4 0.1 copy.12.tile_rank
  22.5 0.1 copy.13.keep_rank
  22.5 21.1 %all-gather.6.cloned.1.call-done = f32[1152,640]{1,0:T(8,128)} async-done(((f32[144,640]{1,0:T(8,128)}), f32[1152,640]{1,0:T(8,128)}) %all-gather.6.cloned.1.call-update) | async-done | bytes 2949136 | tf_op jit(solution)/shard_map/all_gather | solution.py:682
  43.7 0.0 all-gather.8.cloned.1.call-update
  43.7 0.0 copy-start.2
  43.7 0.0 collective-permute-done.2.refs_3_
  43.7 0.0 copy-start
  43.7 0.7 copy-done
  44.4 1.5 %collective-permute-start.3 = (f32[2,6,64,256]{3,2,1,0:T(8,128)S(1)}, f32[2,6,64,256]{3,2,1,0:T(8,128)S(1)}, u32[]{:S(2)}, u32[]{:S(2)}) collective-permute-start(f32[2,6,64,256]{3,2,1,0:T(8,128)S(1)} %pad_maximum_fusion.refs_4_), channel_id=1, source_target_pairs={{0,1},{1,2},{2,3},{3,0},{4,5},{5,6},{6,7},{7,4},{8,9},{9,10},{10,1... | collective-permute-start | bytes 2359304 | tf_op jit(solution)/shard_map/ppermute | solution.py:689
  45.9 46.1 %inverse.1 = (f32[1024,1024]{1,0:T(8,128)}, f32[64,1024]{1,0:T(8,128)S(1)}, f32[3,64,128]{2,1,0:T(8,128)S(1)}, f32[1,1024]{1,0:T(1,128)S(1)}) custom-call(f32[8,144,640]{2,1,0:T(8,128)} %bitcast.11, s32[1]{0:T(128)S(6)} %copy.14.col_rank, f32[4,128,1024]{2,1,0:T(8,128)} %diag.1), custom_call_target="tpu_custom_call" | custom-call | flops 40000000000 | bytes 10485760 | tf_op jit(solution)/shard_map/inverse/pallas_call | solution.py:362
  92.1 11.3 %all-gather.2 = f32[24,64,128]{2,1,0:T(8,128)} all-gather(f32[3,64,128]{2,1,0:T(8,128)S(1)} %get-tuple-element.16), channel_id=4, replica_groups=mesh['row'=8,'col'=4] {'row'}, dimensions={0}, use_global_device_ids=true | all-gather | bytes 884736 | tf_op jit(solution)/shard_map/all_gather | solution.py:699
  103.4 0.0 collective-permute-done.1.refs_2_
  103.4 1.8 %collective-permute-done.4.refs_6_ = f32[2,6,64,256]{3,2,1,0:T(8,128)S(1)} collective-permute-done((f32[2,6,64,256]{3,2,1,0:T(8,128)S(1)}, f32[2,6,64,256]{3,2,1,0:T(8,128)S(1)}, u32[]{:S(2)}, u32[]{:S(2)}) %collective-permute-start.4) | collective-permute-done | bytes 786464 | tf_op jit(solution)/shard_map/ppermute | solution.py:689
  105.2 0.0 copy-start.1
  105.2 0.9 copy-done.1
  106.2 22.9 %recompress.1 = f32[2,1,8,64,1024]{4,3,2,1,0:T(8,128)} custom-call(s32[1]{0:T(128)} %bitcast.place, s32[2]{0:T(128)S(1)} %copy-done.2, s32[1]{0:T(128)S(6)} %copy.14.col_rank, s32[2,1]{1,0:T(2,128)S(1)} %copy.12.tile_rank, s32[2,1]{1,0:T(2,128)S(1)} %copy.13.keep_rank, f32[2,2,64,256]{3,2,1,0:T(8,128)S(1)} %slice.25.refs_0_, ...), custom_call_target="tpu_custom_call" | custom-call | flops 10000000000 | bytes 20971520 | tf_op jit(solution)/shard_map/recompress/pallas_call | solution.py:622
  (12 shorter events, 0.0 us)
Async XLA Ops:
  6.5 37.1 %all-gather.6.cloned.1.call-start = ((), (), s32[]{:S(2)}) async-start(), calls=%async_computation | async-start | bytes 3317760 | tf_op jit(solution)/shard_map/all_gather | solution.py:682
  8.4 13.9 %copy-start.4 = (s32[2,1]{0,1:T(1,128)S(1)}, s32[2,1]{0,1:T(1,128)}, u32[]{:S(2)}) copy-start(s32[2,1]{0,1:T(1,128)} %param.16) | copy-start | bytes 28
  8.4 14.0 %copy-start.5 = (s32[2,1]{0,1:T(1,128)S(1)}, s32[2,1]{0,1:T(1,128)}, u32[]{:S(2)}) copy-start(s32[2,1]{0,1:T(1,128)} %param.17) | copy-start | bytes 28
  9.3 95.9 %all-gather.8.cloned.1.call-start = ((), (), s32[]{:S(2)}) async-start(), calls=%async_computation.1 | async-start | bytes 2359296 | tf_op jit(solution)/shard_map/all_gather | solution.py:692
  10.3 33.4 %collective-permute-start.2 = (f32[2,2,64,256]{3,2,1,0:T(8,128)S(1)}, f32[2,2,64,256]{3,2,1,0:T(8,128)S(1)}, u32[]{:S(2)}, u32[]{:S(2)}) collective-permute-start(f32[2,2,64,256]{3,2,1,0:T(8,128)S(1)} %slice.25.refs_0_), channel_id=1, source_target_pairs={{0,3},{1,0},{2,1},{3,2},{4,7},{5,4},{6,5},{7,6},{8,11},{9,8},{10,9... | collective-permute-start | bytes 786440 | tf_op jit(solution)/shard_map/ppermute | solution.py:689
  15.4 88.0 %collective-permute-start.1 = (f32[2,2,64,256]{3,2,1,0:T(8,128)S(1)}, f32[2,2,64,256]{3,2,1,0:T(8,128)}, u32[]{:S(2)}, u32[]{:S(2)}) collective-permute-start(f32[2,2,64,256]{3,2,1,0:T(8,128)S(1)} %slice.25.refs_0_), channel_id=1, source_target_pairs={{0,2},{1,3},{2,0},{3,1},{4,6},{5,7},{6,4},{7,5},{8,10},{9,11},{10,... | collective-permute-start | bytes 786440 | tf_op jit(solution)/shard_map/ppermute | solution.py:689
  15.4 88.0 %collective-permute-start = (f32[2,2,64,256]{3,2,1,0:T(8,128)S(1)}, f32[2,2,64,256]{3,2,1,0:T(8,128)}, u32[]{:S(2)}, u32[]{:S(2)}) collective-permute-start(f32[2,2,64,256]{3,2,1,0:T(8,128)S(1)} %slice.25.refs_0_), channel_id=1, source_target_pairs={{0,1},{1,2},{2,3},{3,0},{4,5},{5,6},{6,7},{7,4},{8,9},{9,10},{10,1... | collective-permute-start | bytes 786440 | tf_op jit(solution)/shard_map/ppermute | solution.py:689
  17.7 85.7 %collective-permute-start.5 = (f32[2,6,64,256]{3,2,1,0:T(8,128)S(1)}, f32[2,6,64,256]{3,2,1,0:T(8,128)S(1)}, u32[]{:S(2)}, u32[]{:S(2)}) collective-permute-start(f32[2,6,64,256]{3,2,1,0:T(8,128)S(1)} %pad_maximum_fusion.refs_4_), channel_id=1, source_target_pairs={{0,3},{1,0},{2,1},{3,2},{4,7},{5,4},{6,5},{7,6},{8,11},{9,8},{10,9... | collective-permute-start | bytes 2359304 | tf_op jit(solution)/shard_map/ppermute | solution.py:689
  20.6 84.6 %collective-permute-start.4 = (f32[2,6,64,256]{3,2,1,0:T(8,128)S(1)}, f32[2,6,64,256]{3,2,1,0:T(8,128)S(1)}, u32[]{:S(2)}, u32[]{:S(2)}) collective-permute-start(f32[2,6,64,256]{3,2,1,0:T(8,128)S(1)} %pad_maximum_fusion.refs_4_), channel_id=1, source_target_pairs={{0,2},{1,3},{2,0},{3,1},{4,6},{5,7},{6,4},{7,5},{8,10},{9,11},{10,... | collective-permute-start | bytes 2359304 | tf_op jit(solution)/shard_map/ppermute | solution.py:689
  43.7 61.5 %copy-start.2 = (s32[2]{0:T(128)S(1)}, s32[2]{0:T(128)}, u32[]{:S(2)}) copy-start(s32[2]{0:T(128)} %panel_rank.1) | copy-start | bytes 28
  43.7 0.7 copy-start
  44.4 60.8 %collective-permute-start.3 = (f32[2,6,64,256]{3,2,1,0:T(8,128)S(1)}, f32[2,6,64,256]{3,2,1,0:T(8,128)S(1)}, u32[]{:S(2)}, u32[]{:S(2)}) collective-permute-start(f32[2,6,64,256]{3,2,1,0:T(8,128)S(1)} %pad_maximum_fusion.refs_4_), channel_id=1, source_target_pairs={{0,1},{1,2},{2,3},{3,0},{4,5},{5,6},{6,7},{7,4},{8,9},{9,10},{10,1... | collective-permute-start | bytes 2359304 | tf_op jit(solution)/shard_map/ppermute | solution.py:689
  92.0 13.2 %copy-start.3 = (f32[64,1024]{1,0:T(8,128)}, f32[64,1024]{1,0:T(8,128)S(1)}, u32[]{:S(2)}) copy-start(f32[64,1024]{1,0:T(8,128)S(1)} %get-tuple-element.13.refs_11_) | copy-start | bytes 786436
  105.2 1.0 copy-start.1
Sparse Core Ops, SparseCore 0:
  9.4 34.1 all-gather.5
  45.5 27.9 all-gather.7

commit v7 on v6

--- a/solution.py
+++ b/solution.py
@@ -73,52 +73,63 @@
     return lax.broadcasted_iota(jnp.int32, (SUB, BLOCK), 1)
 
 
-def micro_inverse(cols):
+def spread_entries(x, at):
+    cols = [lane_rep(x, at + k) for k in range(SUB)]
+    return [[sub_rep(cols[k], i) for k in range(i + 1)] for i in range(SUB)]
+
+
+def merge_rows(rows):
     sub = sub_index()
-    cols = list(cols)
-    for j in range(0, SUB, 2):
-        first, second = sub == j, sub == j + 1
-        pair = first | second
-        a, b, d = sub_rep(cols[j], j), sub_rep(cols[j], j + 1), sub_rep(cols[j + 1], j + 1)
+    step = SUB // 2
+    while step:
+        rows = [
+            jnp.where((sub & step) == 0, rows[i], rows[i + step]) for i in range(step)
+        ]
+        step //= 2
+    return rows[0]
+
+
+def micro_inverse(entries):
+    m = {(i, k): entries[i][k] for i in range(SUB) for k in range(i + 1)}
+    key = lambda i, k: (i, k) if i >= k else (k, i)
+    for p in range(0, SUB, 2):
+        q = p + 1
+        a, b, d = m[p, p], m[q, p], m[q, q]
         inv_det = 1.0 / (a * d - b * b)
-        f0 = jnp.where(first, -1.0, jnp.where(second, 0.0, cols[j]))
-        f1 = jnp.where(second, -1.0, jnp.where(first, 0.0, cols[j + 1]))
-        fresh = []
-        for k in range(SUB):
-            if k == j:
-                fresh.append((f1 * b - f0 * d) * inv_det)
-            elif k == j + 1:
-                fresh.append((f0 * b - f1 * a) * inv_det)
-            else:
-                x0, x1 = sub_rep(cols[k], j), sub_rep(cols[k], j + 1)
-                change = f0 * (d * x0 - b * x1) + f1 * (a * x1 - b * x0)
-                fresh.append(jnp.where(pair, 0.0, cols[k]) - change * inv_det)
-        cols = fresh
-    return cols
-
-
-def micro_factor(cols):
-    sub = sub_index()
-    cols = list(cols)
-    low = [jnp.where(sub == k, 1.0, 0.0) for k in range(SUB)]
-    pivots = jnp.zeros((SUB, BLOCK), F32)
+        rest = [i for i in range(SUB) if i not in (p, q)]
+        x0 = {i: m[key(i, p)] for i in rest}
+        x1 = {i: m[key(i, q)] for i in rest}
+        n0 = {i: d * x0[i] - b * x1[i] for i in rest}
+        n1 = {i: a * x1[i] - b * x0[i] for i in rest}
+        for i in rest:
+            for k in rest:
+                if k <= i:
+                    m[i, k] = m[i, k] - (x0[i] * n0[k] + x1[i] * n1[k]) * inv_det
+        for i in rest:
+            m[key(i, p)] = n0[i] * inv_det
+            m[key(i, q)] = n1[i] * inv_det
+        m[p, p], m[q, p], m[q, q] = -d * inv_det, b * inv_det, -a * inv_det
+    return [[m[key(i, k)] for k in range(SUB)] for i in range(SUB)]
+
+
+def micro_factor(entries):
+    m = [list(row) for row in entries]
+    low = [[None] * SUB for _ in range(SUB)]
+    scale = []
     for j in range(SUB):
-        here = sub == j
-        piv = sub_rep(cols[j], j)
-        inv_piv = 1.0 / piv
-        factor = jnp.where(here, -1.0, cols[j])
-        pivots = jnp.where(here, piv, pivots)
-        below = jnp.where(sub > j, cols[j], 0.0)
-        for k in range(j + 1):
-            low[k] = low[k] - below * sub_rep(low[k], j) * inv_piv
-        cols = [
-            -factor * inv_piv
-            if k == j
-            else jnp.where(here, 0.0, cols[k]) - factor * (sub_rep(cols[k], j) * inv_piv)
-            for k in range(SUB)
-        ]
-    scale = lax.rsqrt(pivots)
-    return cols, [scale * c for c in low]
+        inv_piv = 1.0 / m[j][j]
+        scale.append(lax.rsqrt(m[j][j]))
+        for i in range(j + 1, SUB):
+            factor = m[i][j] * inv_piv
+            for k in range(j + 1, i + 1):
+                m[i][k] = m[i][k] - factor * m[k][j]
+            for k in range(j):
+                change = factor * low[j][k]
+                low[i][k] = -change if low[i][k] is None else low[i][k] - change
+            low[i][j] = -factor if low[i][j] is None else low[i][j] - factor
+    return [
+        [scale[i] if k == i else scale[i] * low[i][k] for k in range(i + 1)] for i in range(SUB)
+    ]
 
 
 def band_left(x, band):
@@ -160,18 +171,20 @@
         for g in band:
             at = g * SUB
             inside = (lane >= at) & (lane < at + SUB)
-            inv = micro_inverse([lane_rep(rows[g], at + k) for k in range(SUB)])
-            own = jnp.where(inside, jnp.where(lane - at == sub, 1.0, 0.0), rows[g])
-            new = tree_sum([inv[k] * sub_rep(own, k) for k in range(SUB)])
-            news = [sub_rep(new, k) for k in range(SUB)]
-            new_ahead = tree_sum([inv[k] * sub_rep(ahead[g], k) for k in range(SUB)])
-            news_ahead = [sub_rep(new_ahead, k) for k in range(SUB)]
+            negative = micro_inverse(spread_entries(rows[g], at))
+            own = jnp.where(inside, jnp.where(lane - at == sub, -1.0, 0.0), -rows[g])
+            owns = [sub_rep(own, k) for k in range(SUB)]
+            owns_ahead = [sub_rep(-ahead[g], k) for k in range(SUB)]
+            news = [tree_sum([row[k] * owns[k] for k in range(SUB)]) for row in negative]
+            news_ahead = [
+                tree_sum([row[k] * owns_ahead[k] for k in range(SUB)]) for row in negative
+            ]
             for i in [first + (g - first + 1 + i) % BAND for i in range(BAND - 1)]:
                 factors = [lane_rep(rows[i], at + k) for k in range(SUB)]
                 kept = jnp.where(inside, 0.0, rows[i])
                 rows[i] = kept - tree_sum([factors[k] * news[k] for k in range(SUB)])
                 ahead[i] = ahead[i] - tree_sum([factors[k] * news_ahead[k] for k in range(SUB)])
-            rows[g], ahead[g] = new, new_ahead
+            rows[g], ahead[g] = merge_rows(news), merge_rows(news_ahead)
             for piece in work[g * len(work) // count : (g + 1) * len(work) // count]:
                 piece()
         inside = (lane >= first * SUB) & (lane < (first + BAND) * SUB)
@@ -196,16 +209,15 @@
     count = width // SUB
     for g in range(count):
         at = g * SUB
-        inv, low = micro_factor([lane_rep(rows[g], at + k) for k in range(SUB)])
-        own = rows[g]
-        own_rep = [sub_rep(own, k) for k in range(SUB)]
-        new = tree_sum([inv[k] * own_rep[k] for k in range(SUB)])
-        news = [sub_rep(new, k) for k in range(SUB)]
+        low = micro_factor(spread_entries(rows[g], at))
+        own = [sub_rep(rows[g], k) for k in range(SUB)]
+        done = [tree_sum([low[i][k] * own[k] for k in range(i + 1)]) for i in range(SUB)]
+        news = [tree_sum([low[i][k] * done[i] for i in range(k, SUB)]) for k in range(SUB)]
         for i in range(g + 1, count):
             rows[i] = rows[i] - tree_sum(
                 [lane_rep(rows[i], at + k) * news[k] for k in range(SUB)]
             )
-        rows[g] = tree_sum([low[k] * own_rep[k] for k in range(SUB)])
+        rows[g] = merge_rows(done)
     return rows
 
 

time: 136 us -> 143 us (1.051)
  Pallas kernels: 69 us -> 77.2 us
  waiting for transfers between devices: 22.9 us -> 21.2 us
    pallas_call x1, Pallas kernels: 46.1 us -> 54.1 us  [run_inverse(): pl.pallas_call(functools.partial(inverse_kernel, own_rows), out_shape=(pl...]
    ppermute x6, waiting for transfers between devices: 1.8 us -> 0.02 us  [on_device(): lax.ppermute(source, 'col', [(i, (i + s) % col_count) for i in range(col_...]
  transfers between devices with their start and end apart: 8 -> 8, of which waited for: 2 -> 1; matrix products, arithmetic and copies ran while one was open for 2% -> 2% of each run, Pallas kernels for 34% -> 38%
where the time goes in v7:
time: 143 us; the launch traced here: 142 us
  Pallas kernels  77.2 us (54%)
  waiting for transfers between devices  21.2 us (15%)
  between operations  14.2 us (10%)
  starting transfers between devices  11.6 us (8%)
  blocking collectives  11.3 us (8%)
  local copies, waits for them, and re-layouts  5.87 us (4%)
    pallas_call x1, Pallas kernels, run_inverse(): pl.pallas_call(functools.partial(inverse_kernel, own_rows), out_shape=(pl...  54.1 us
    pallas_call x1, Pallas kernels, run_recompress(): pl.pallas_call(functools.partial(recompress_kernel, tiles, len(first)), o...  23.1 us
    all_gather x1, waiting for transfers between devices, on_device(): lax.all_gather(jnp.concatenate([own, values], axis=0), 'row', axis=0)  21.1 us
    ppermute x6, starting transfers between devices, on_device(): lax.ppermute(source, 'col', [(i, (i + s) % col_count) for i in range(col_...  11.6 us
    all_gather x1, blocking collectives, on_device(): all_products = lax.all_gather(products, 'row', axis=0)  11.3 us
  transfers between devices with their start and end apart: 8, of which 1 were waited for; matrix products, arithmetic and copies ran while one was open for 2% of the time, Pallas kernels for 38%

profile of v7, /device:TPU:0, one launch (start us, length us, event | category | flops | bytes accessed | tf_op | source)
XLA Modules:
  0.0 142.4 jit_solution(2805268537859458166)
XLA Ops:
  6.5 0.8 slice_bitcast_fusion.1
  7.3 1.1 slice_bitcast_fusion
  8.4 0.0 copy-start.4
  8.4 0.0 copy-start.5
  8.4 0.1 fusion
  8.5 0.8 pad_maximum_fusion.1
  9.3 0.0 all-gather.6.cloned.1.call-update
  9.3 0.0 all-gather.8.cloned.1.call-start
  9.4 1.0 slice.25.refs_0_
  10.3 5.1 %collective-permute-start.2 = (f32[2,2,64,256]{3,2,1,0:T(8,128)S(1)}, f32[2,2,64,256]{3,2,1,0:T(8,128)S(1)}, u32[]{:S(2)}, u32[]{:S(2)}) collective-permute-start(f32[2,2,64,256]{3,2,1,0:T(8,128)S(1)} %slice.25.refs_0_), channel_id=1, source_target_pairs={{0,3},{1,0},{2,1},{3,2},{4,7},{5,4},{6,5},{7,6},{8,11},{9,8},{10,9... | collective-permute-start | bytes 786440 | tf_op jit(solution)/shard_map/ppermute | solution.py:701
  15.4 0.0 collective-permute-start.1
  15.4 1.0 collective-permute-start
  16.4 1.2 fusion.1
  17.6 0.1 pad_maximum_fusion.refs_4_
  17.7 2.9 %collective-permute-start.5 = (f32[2,6,64,256]{3,2,1,0:T(8,128)S(1)}, f32[2,6,64,256]{3,2,1,0:T(8,128)S(1)}, u32[]{:S(2)}, u32[]{:S(2)}) collective-permute-start(f32[2,6,64,256]{3,2,1,0:T(8,128)S(1)} %pad_maximum_fusion.refs_4_), channel_id=1, source_target_pairs={{0,3},{1,0},{2,1},{3,2},{4,7},{5,4},{6,5},{7,6},{8,11},{9,8},{10,9... | collective-permute-start | bytes 2359304 | tf_op jit(solution)/shard_map/ppermute | solution.py:701
  20.6 1.1 collective-permute-start.4
  22.4 0.1 copy.12.tile_rank
  22.5 0.1 copy.13.keep_rank
  22.5 21.1 %all-gather.6.cloned.1.call-done = f32[1152,640]{1,0:T(8,128)} async-done(((f32[144,640]{1,0:T(8,128)}), f32[1152,640]{1,0:T(8,128)}) %all-gather.6.cloned.1.call-update) | async-done | bytes 2949136 | tf_op jit(solution)/shard_map/all_gather | solution.py:694
  43.7 0.0 all-gather.8.cloned.1.call-update
  43.7 0.0 copy-start.2
  43.7 0.0 collective-permute-done.2.refs_3_
  43.7 0.0 copy-start
  43.7 0.7 copy-done
  44.4 1.5 %collective-permute-start.3 = (f32[2,6,64,256]{3,2,1,0:T(8,128)S(1)}, f32[2,6,64,256]{3,2,1,0:T(8,128)S(1)}, u32[]{:S(2)}, u32[]{:S(2)}) collective-permute-start(f32[2,6,64,256]{3,2,1,0:T(8,128)S(1)} %pad_maximum_fusion.refs_4_), channel_id=1, source_target_pairs={{0,1},{1,2},{2,3},{3,0},{4,5},{5,6},{6,7},{7,4},{8,9},{9,10},{10,1... | collective-permute-start | bytes 2359304 | tf_op jit(solution)/shard_map/ppermute | solution.py:701
  45.9 54.1 %inverse.1 = (f32[1024,1024]{1,0:T(8,128)}, f32[64,1024]{1,0:T(8,128)S(1)}, f32[3,64,128]{2,1,0:T(8,128)S(1)}, f32[1,1024]{1,0:T(1,128)S(1)}) custom-call(f32[8,144,640]{2,1,0:T(8,128)} %bitcast.11, s32[1]{0:T(128)S(6)} %copy.14.col_rank, f32[4,128,1024]{2,1,0:T(8,128)} %diag.1), custom_call_target="tpu_custom_call" | custom-call | flops 40000000000 | bytes 10485760 | tf_op jit(solution)/shard_map/inverse/pallas_call | solution.py:374
  100.1 11.3 %all-gather.2 = f32[24,64,128]{2,1,0:T(8,128)} all-gather(f32[3,64,128]{2,1,0:T(8,128)S(1)} %get-tuple-element.16), channel_id=4, replica_groups=mesh['row'=8,'col'=4] {'row'}, dimensions={0}, use_global_device_ids=true | all-gather | bytes 884736 | tf_op jit(solution)/shard_map/all_gather | solution.py:711
  111.4 0.0 collective-permute-done.4.refs_6_
  111.4 0.0 all-gather.8.cloned.1.call-done
  111.5 0.0 copy-start.1
  111.5 0.9 copy-done.1
  112.4 23.1 %recompress.1 = f32[2,1,8,64,1024]{4,3,2,1,0:T(8,128)} custom-call(s32[1]{0:T(128)} %bitcast.place, s32[2]{0:T(128)S(1)} %copy-done.2, s32[1]{0:T(128)S(6)} %copy.14.col_rank, s32[2,1]{1,0:T(2,128)S(1)} %copy.12.tile_rank, s32[2,1]{1,0:T(2,128)S(1)} %copy.13.keep_rank, f32[2,2,64,256]{3,2,1,0:T(8,128)S(1)} %slice.25.refs_0_, ...), custom_call_target="tpu_custom_call" | custom-call | flops 10000000000 | bytes 20971520 | tf_op jit(solution)/shard_map/recompress/pallas_call | solution.py:634
  (12 shorter events, 0.0 us)
Async XLA Ops:
  6.5 37.1 %all-gather.6.cloned.1.call-start = ((), (), s32[]{:S(2)}) async-start(), calls=%async_computation | async-start | bytes 3317760 | tf_op jit(solution)/shard_map/all_gather | solution.py:694
  8.4 13.9 %copy-start.4 = (s32[2,1]{0,1:T(1,128)S(1)}, s32[2,1]{0,1:T(1,128)}, u32[]{:S(2)}) copy-start(s32[2,1]{0,1:T(1,128)} %param.16) | copy-start | bytes 28
  8.4 14.0 %copy-start.5 = (s32[2,1]{0,1:T(1,128)S(1)}, s32[2,1]{0,1:T(1,128)}, u32[]{:S(2)}) copy-start(s32[2,1]{0,1:T(1,128)} %param.17) | copy-start | bytes 28
  9.3 102.2 %all-gather.8.cloned.1.call-start = ((), (), s32[]{:S(2)}) async-start(), calls=%async_computation.1 | async-start | bytes 2359296 | tf_op jit(solution)/shard_map/all_gather | solution.py:704
  10.3 33.4 %collective-permute-start.2 = (f32[2,2,64,256]{3,2,1,0:T(8,128)S(1)}, f32[2,2,64,256]{3,2,1,0:T(8,128)S(1)}, u32[]{:S(2)}, u32[]{:S(2)}) collective-permute-start(f32[2,2,64,256]{3,2,1,0:T(8,128)S(1)} %slice.25.refs_0_), channel_id=1, source_target_pairs={{0,3},{1,0},{2,1},{3,2},{4,7},{5,4},{6,5},{7,6},{8,11},{9,8},{10,9... | collective-permute-start | bytes 786440 | tf_op jit(solution)/shard_map/ppermute | solution.py:701
  15.4 96.0 %collective-permute-start.1 = (f32[2,2,64,256]{3,2,1,0:T(8,128)S(1)}, f32[2,2,64,256]{3,2,1,0:T(8,128)}, u32[]{:S(2)}, u32[]{:S(2)}) collective-permute-start(f32[2,2,64,256]{3,2,1,0:T(8,128)S(1)} %slice.25.refs_0_), channel_id=1, source_target_pairs={{0,2},{1,3},{2,0},{3,1},{4,6},{5,7},{6,4},{7,5},{8,10},{9,11},{10,... | collective-permute-start | bytes 786440 | tf_op jit(solution)/shard_map/ppermute | solution.py:701
  15.4 96.0 %collective-permute-start = (f32[2,2,64,256]{3,2,1,0:T(8,128)S(1)}, f32[2,2,64,256]{3,2,1,0:T(8,128)}, u32[]{:S(2)}, u32[]{:S(2)}) collective-permute-start(f32[2,2,64,256]{3,2,1,0:T(8,128)S(1)} %slice.25.refs_0_), channel_id=1, source_target_pairs={{0,1},{1,2},{2,3},{3,0},{4,5},{5,6},{6,7},{7,4},{8,9},{9,10},{10,1... | collective-permute-start | bytes 786440 | tf_op jit(solution)/shard_map/ppermute | solution.py:701
  17.7 93.7 %collective-permute-start.5 = (f32[2,6,64,256]{3,2,1,0:T(8,128)S(1)}, f32[2,6,64,256]{3,2,1,0:T(8,128)S(1)}, u32[]{:S(2)}, u32[]{:S(2)}) collective-permute-start(f32[2,6,64,256]{3,2,1,0:T(8,128)S(1)} %pad_maximum_fusion.refs_4_), channel_id=1, source_target_pairs={{0,3},{1,0},{2,1},{3,2},{4,7},{5,4},{6,5},{7,6},{8,11},{9,8},{10,9... | collective-permute-start | bytes 2359304 | tf_op jit(solution)/shard_map/ppermute | solution.py:701
  20.6 90.8 %collective-permute-start.4 = (f32[2,6,64,256]{3,2,1,0:T(8,128)S(1)}, f32[2,6,64,256]{3,2,1,0:T(8,128)S(1)}, u32[]{:S(2)}, u32[]{:S(2)}) collective-permute-start(f32[2,6,64,256]{3,2,1,0:T(8,128)S(1)} %pad_maximum_fusion.refs_4_), channel_id=1, source_target_pairs={{0,2},{1,3},{2,0},{3,1},{4,6},{5,7},{6,4},{7,5},{8,10},{9,11},{10,... | collective-permute-start | bytes 2359304 | tf_op jit(solution)/shard_map/ppermute | solution.py:701
  43.7 67.8 %copy-start.2 = (s32[2]{0:T(128)S(1)}, s32[2]{0:T(128)}, u32[]{:S(2)}) copy-start(s32[2]{0:T(128)} %panel_rank.1) | copy-start | bytes 28
  43.7 0.7 copy-start
  44.4 67.0 %collective-permute-start.3 = (f32[2,6,64,256]{3,2,1,0:T(8,128)S(1)}, f32[2,6,64,256]{3,2,1,0:T(8,128)S(1)}, u32[]{:S(2)}, u32[]{:S(2)}) collective-permute-start(f32[2,6,64,256]{3,2,1,0:T(8,128)S(1)} %pad_maximum_fusion.refs_4_), channel_id=1, source_target_pairs={{0,1},{1,2},{2,3},{3,0},{4,5},{5,6},{6,7},{7,4},{8,9},{9,10},{10,1... | collective-permute-start | bytes 2359304 | tf_op jit(solution)/shard_map/ppermute | solution.py:701
  100.0 11.4 %copy-start.3 = (f32[64,1024]{1,0:T(8,128)}, f32[64,1024]{1,0:T(8,128)S(1)}, u32[]{:S(2)}) copy-start(f32[64,1024]{1,0:T(8,128)S(1)} %get-tuple-element.13.refs_11_) | copy-start | bytes 786436
  111.5 1.0 copy-start.1
Sparse Core Ops, SparseCore 0:
  9.4 34.1 all-gather.5
  45.5 27.9 all-gather.7

commit v8 on v6

--- a/solution.py
+++ b/solution.py
@@ -25,17 +25,16 @@
     return lax.dot_general(left, right, dims, precision=HIGHEST, preferred_element_type=F32)
 
 
+def split2(x):
+    hi = x.astype(BF16)
+    return hi, (x - hi.astype(F32)).astype(BF16)
+
+
 def split3(x):
     hi = x.astype(BF16)
     rest = x - hi.astype(F32)
     mid = rest.astype(BF16)
-    lo = (rest - mid.astype(F32)).astype(BF16)
-    return hi, mid, lo
-
-
-def split2(x):
-    hi = x.astype(BF16)
-    return hi, (x - hi.astype(F32)).astype(BF16)
+    return hi, mid, (rest - mid.astype(F32)).astype(BF16)
 
 
 def left_terms(x):
@@ -255,14 +254,25 @@
     if width < size:
         for c in range(steps):
             set_scale(c, gathered[c, :BLOCK, :BLOCK])
-        for r in range(steps):
-            for o in range(width // BLOCK):
-                c = (r + o) % steps
-                block = gathered[r, :BLOCK, part(o)] * scale_col[part(r), :] * scale_row[:, part(c)]
-                inverse[part(r), part(c)] = block
-                if 0 < o and 2 * o < steps:
-                    inverse[part(c), part(r)] = block.T
+
+
+        def place(r, o):
+            c = (r + o) % steps
+            block = gathered[r, :BLOCK, part(o)] * scale_col[part(r), :] * scale_row[:, part(c)]
+            inverse[part(r), part(c)] = block
+            if 0 < o and 2 * o < steps:
+                inverse[part(c), part(r)] = block.T
+
+        for r, o in ((0, 0), (0, 1), (1, 0)):
+            place(r, o)
+        beside = [
+            functools.partial(place, r, o)
+            for r in range(steps)
+            for o in range(width // BLOCK)
+            if (r, o) not in ((0, 0), (0, 1), (1, 0))
+        ]
     else:
+        beside = []
         for r in range(shards):
             inverse[part(r, own_rows), :] = gathered[r, :own_rows, :]
         for c in range(steps):
@@ -309,7 +319,7 @@
         upcoming[...] = jnp.concatenate(following, axis=0)
 
     one, two = part(0), part(1)
-    invert_to_pivot([inverse[one, one], inverse[one, two], inverse[two, one], inverse[two, two]], [])
+    invert_to_pivot([inverse[one, one], inverse[one, two], inverse[two, one], inverse[two, two]], beside)
 
     def step(k, carry):
         at = pl.ds(pl.multiple_of(k * BLOCK, BLOCK), BLOCK)
@@ -340,11 +350,22 @@
             pieces.append(gathered[r, at : at + own_ranks, :])
         values.append(jnp.concatenate(pieces, axis=1)[:, :size])
     values = keep_rows(jnp.concatenate(values, axis=0), col_rank[0])
-    z = mm(values * scale_row[...], inverse[...]) * scale_row[...]
+    z = dot_split(split2(values * scale_row[...]), split2(inverse[...])) * scale_row[...]
     solved[...] = z
     fetch.wait()
+    rows = 3 * own_rows
+    terms = lax.dot_general(
+        jnp.concatenate(split3(tangents[...].reshape(rows, size)), axis=0),
+        jnp.concatenate(split3(z), axis=0),
+        NT,
+        preferred_element_type=F32,
+    )
+    term = lambda i, k: terms[i * rows : (i + 1) * rows, k * rank_count : (k + 1) * rank_count]
+    total = term(0, 0) + (
+        (term(0, 1) + term(1, 0)) + (term(1, 1) + (term(0, 2) + term(2, 0)))
+    )
     for t in range(3):
-        products[t] = mm(z, tangents[t], NT)
+        products[t] = total[t * own_rows : (t + 1) * own_rows].T
     store.wait()
 
 

time: 136 us -> 136 us (level)
  Pallas kernels: 69 us -> 66.5 us
  waiting for transfers between devices: 22.9 us -> 25.4 us
    pallas_call x1, Pallas kernels: 46.1 us -> 43.7 us  [run_inverse(): pl.pallas_call(functools.partial(inverse_kernel, own_rows), out_shape=(pl...]
    ppermute x6, waiting for transfers between devices: 1.8 us -> 4.3 us  [on_device(): lax.ppermute(source, 'col', [(i, (i + s) % col_count) for i in range(col_...]
  transfers between devices with their start and end apart: 8 -> 8, of which waited for: 2 -> 2; matrix products, arithmetic and copies ran while one was open for 2% -> 2% of each run, Pallas kernels for 34% -> 32%
where the time goes in v8:
time: 136 us
  Pallas kernels  66.5 us (49%)
  waiting for transfers between devices  25.4 us (19%)
  between operations  14.2 us (10%)
  starting transfers between devices  11.6 us (9%)
  blocking collectives  11.3 us (8%)
  local copies, waits for them, and re-layouts  5.87 us (4%)
    pallas_call x1, Pallas kernels, run_inverse(): pl.pallas_call(functools.partial(inverse_kernel, own_rows), out_shape=(pl...  43.7 us
    pallas_call x1, Pallas kernels, run_recompress(): pl.pallas_call(functools.partial(recompress_kernel, tiles, len(first)), o...  22.9 us
    all_gather x1, waiting for transfers between devices, on_device(): lax.all_gather(jnp.concatenate([own, values], axis=0), 'row', axis=0)  21.1 us
    ppermute x6, starting transfers between devices, on_device(): lax.ppermute(source, 'col', [(i, (i + s) % col_count) for i in range(col_...  11.6 us
    all_gather x1, blocking collectives, on_device(): all_products = lax.all_gather(products, 'row', axis=0)  11.3 us
    ppermute x6, waiting for transfers between devices, on_device(): lax.ppermute(source, 'col', [(i, (i + s) % col_count) for i in range(col_...  4.3 us
  transfers between devices with their start and end apart: 8, of which 2 were waited for; matrix products, arithmetic and copies ran while one was open for 2% of the time, Pallas kernels for 32%

profile of v8, /device:TPU:0, one launch (start us, length us, event | category | flops | bytes accessed | tf_op | source)
XLA Modules:
  0.0 135.9 jit_solution(8374560236127814186)
XLA Ops:
  6.5 0.8 slice_bitcast_fusion.1
  7.3 1.1 slice_bitcast_fusion
  8.4 0.0 copy-start.4
  8.4 0.0 copy-start.5
  8.4 0.1 fusion
  8.5 0.8 pad_maximum_fusion.1
  9.3 0.0 all-gather.6.cloned.1.call-update
  9.3 0.0 all-gather.8.cloned.1.call-start
  9.4 1.0 slice.25.refs_0_
  10.3 5.1 %collective-permute-start.2 = (f32[2,2,64,256]{3,2,1,0:T(8,128)S(1)}, f32[2,2,64,256]{3,2,1,0:T(8,128)S(1)}, u32[]{:S(2)}, u32[]{:S(2)}) collective-permute-start(f32[2,2,64,256]{3,2,1,0:T(8,128)S(1)} %slice.25.refs_0_), channel_id=1, source_target_pairs={{0,3},{1,0},{2,1},{3,2},{4,7},{5,4},{6,5},{7,6},{8,11},{9,8},{10,9... | collective-permute-start | bytes 786440 | tf_op jit(solution)/shard_map/ppermute | solution.py:710
  15.4 0.0 collective-permute-start.1
  15.4 1.0 collective-permute-start
  16.4 1.2 fusion.1
  17.6 0.1 pad_maximum_fusion.refs_4_
  17.7 2.9 %collective-permute-start.5 = (f32[2,6,64,256]{3,2,1,0:T(8,128)S(1)}, f32[2,6,64,256]{3,2,1,0:T(8,128)S(1)}, u32[]{:S(2)}, u32[]{:S(2)}) collective-permute-start(f32[2,6,64,256]{3,2,1,0:T(8,128)S(1)} %pad_maximum_fusion.refs_4_), channel_id=1, source_target_pairs={{0,3},{1,0},{2,1},{3,2},{4,7},{5,4},{6,5},{7,6},{8,11},{9,8},{10,9... | collective-permute-start | bytes 2359304 | tf_op jit(solution)/shard_map/ppermute | solution.py:710
  20.6 1.1 collective-permute-start.4
  22.4 0.1 copy.12.tile_rank
  22.5 0.1 copy.13.keep_rank
  22.5 21.1 %all-gather.6.cloned.1.call-done = f32[1152,640]{1,0:T(8,128)} async-done(((f32[144,640]{1,0:T(8,128)}), f32[1152,640]{1,0:T(8,128)}) %all-gather.6.cloned.1.call-update) | async-done | bytes 2949136 | tf_op jit(solution)/shard_map/all_gather | solution.py:703
  43.7 0.0 all-gather.8.cloned.1.call-update
  43.7 0.0 copy-start.2
  43.7 0.0 collective-permute-done.2.refs_3_
  43.7 0.0 copy-start
  43.7 0.7 copy-done
  44.4 1.5 %collective-permute-start.3 = (f32[2,6,64,256]{3,2,1,0:T(8,128)S(1)}, f32[2,6,64,256]{3,2,1,0:T(8,128)S(1)}, u32[]{:S(2)}, u32[]{:S(2)}) collective-permute-start(f32[2,6,64,256]{3,2,1,0:T(8,128)S(1)} %pad_maximum_fusion.refs_4_), channel_id=1, source_target_pairs={{0,1},{1,2},{2,3},{3,0},{4,5},{5,6},{6,7},{7,4},{8,9},{9,10},{10,1... | collective-permute-start | bytes 2359304 | tf_op jit(solution)/shard_map/ppermute | solution.py:710
  45.9 43.7 %inverse.1 = (f32[1024,1024]{1,0:T(8,128)}, f32[64,1024]{1,0:T(8,128)S(1)}, f32[3,64,128]{2,1,0:T(8,128)S(1)}, f32[1,1024]{1,0:T(1,128)S(1)}) custom-call(f32[8,144,640]{2,1,0:T(8,128)} %bitcast.11, s32[1]{0:T(128)S(6)} %copy.14.col_rank, f32[4,128,1024]{2,1,0:T(8,128)} %diag.1), custom_call_target="tpu_custom_call" | custom-call | flops 40000000000 | bytes 10485760 | tf_op jit(solution)/shard_map/inverse/pallas_call | solution.py:383
  89.6 11.3 %all-gather.2 = f32[24,64,128]{2,1,0:T(8,128)} all-gather(f32[3,64,128]{2,1,0:T(8,128)S(1)} %get-tuple-element.16), channel_id=4, replica_groups=mesh['row'=8,'col'=4] {'row'}, dimensions={0}, use_global_device_ids=true | all-gather | bytes 884736 | tf_op jit(solution)/shard_map/all_gather | solution.py:720
  100.9 0.0 collective-permute-done.1.refs_2_
  100.9 4.3 %collective-permute-done.4.refs_6_ = f32[2,6,64,256]{3,2,1,0:T(8,128)S(1)} collective-permute-done((f32[2,6,64,256]{3,2,1,0:T(8,128)S(1)}, f32[2,6,64,256]{3,2,1,0:T(8,128)S(1)}, u32[]{:S(2)}, u32[]{:S(2)}) %collective-permute-start.4) | collective-permute-done | bytes 786464 | tf_op jit(solution)/shard_map/ppermute | solution.py:710
  105.2 0.0 copy-start.1
  105.2 0.9 copy-done.1
  106.2 22.9 %recompress.1 = f32[2,1,8,64,1024]{4,3,2,1,0:T(8,128)} custom-call(s32[1]{0:T(128)} %bitcast.place, s32[2]{0:T(128)S(1)} %copy-done.2, s32[1]{0:T(128)S(6)} %copy.14.col_rank, s32[2,1]{1,0:T(2,128)S(1)} %copy.12.tile_rank, s32[2,1]{1,0:T(2,128)S(1)} %copy.13.keep_rank, f32[2,2,64,256]{3,2,1,0:T(8,128)S(1)} %slice.25.refs_0_, ...), custom_call_target="tpu_custom_call" | custom-call | flops 10000000000 | bytes 20971520 | tf_op jit(solution)/shard_map/recompress/pallas_call | solution.py:643
  (12 shorter events, 0.0 us)
Async XLA Ops:
  6.5 37.1 %all-gather.6.cloned.1.call-start = ((), (), s32[]{:S(2)}) async-start(), calls=%async_computation | async-start | bytes 3317760 | tf_op jit(solution)/shard_map/all_gather | solution.py:703
  8.4 13.9 %copy-start.4 = (s32[2,1]{0,1:T(1,128)S(1)}, s32[2,1]{0,1:T(1,128)}, u32[]{:S(2)}) copy-start(s32[2,1]{0,1:T(1,128)} %param.16) | copy-start | bytes 28
  8.4 14.0 %copy-start.5 = (s32[2,1]{0,1:T(1,128)S(1)}, s32[2,1]{0,1:T(1,128)}, u32[]{:S(2)}) copy-start(s32[2,1]{0,1:T(1,128)} %param.17) | copy-start | bytes 28
  9.3 95.9 %all-gather.8.cloned.1.call-start = ((), (), s32[]{:S(2)}) async-start(), calls=%async_computation.1 | async-start | bytes 2359296 | tf_op jit(solution)/shard_map/all_gather | solution.py:713
  10.3 33.4 %collective-permute-start.2 = (f32[2,2,64,256]{3,2,1,0:T(8,128)S(1)}, f32[2,2,64,256]{3,2,1,0:T(8,128)S(1)}, u32[]{:S(2)}, u32[]{:S(2)}) collective-permute-start(f32[2,2,64,256]{3,2,1,0:T(8,128)S(1)} %slice.25.refs_0_), channel_id=1, source_target_pairs={{0,3},{1,0},{2,1},{3,2},{4,7},{5,4},{6,5},{7,6},{8,11},{9,8},{10,9... | collective-permute-start | bytes 786440 | tf_op jit(solution)/shard_map/ppermute | solution.py:710
  15.4 85.5 %collective-permute-start.1 = (f32[2,2,64,256]{3,2,1,0:T(8,128)S(1)}, f32[2,2,64,256]{3,2,1,0:T(8,128)}, u32[]{:S(2)}, u32[]{:S(2)}) collective-permute-start(f32[2,2,64,256]{3,2,1,0:T(8,128)S(1)} %slice.25.refs_0_), channel_id=1, source_target_pairs={{0,2},{1,3},{2,0},{3,1},{4,6},{5,7},{6,4},{7,5},{8,10},{9,11},{10,... | collective-permute-start | bytes 786440 | tf_op jit(solution)/shard_map/ppermute | solution.py:710
  15.4 85.5 %collective-permute-start = (f32[2,2,64,256]{3,2,1,0:T(8,128)S(1)}, f32[2,2,64,256]{3,2,1,0:T(8,128)}, u32[]{:S(2)}, u32[]{:S(2)}) collective-permute-start(f32[2,2,64,256]{3,2,1,0:T(8,128)S(1)} %slice.25.refs_0_), channel_id=1, source_target_pairs={{0,1},{1,2},{2,3},{3,0},{4,5},{5,6},{6,7},{7,4},{8,9},{9,10},{10,1... | collective-permute-start | bytes 786440 | tf_op jit(solution)/shard_map/ppermute | solution.py:710
  17.7 83.2 %collective-permute-start.5 = (f32[2,6,64,256]{3,2,1,0:T(8,128)S(1)}, f32[2,6,64,256]{3,2,1,0:T(8,128)S(1)}, u32[]{:S(2)}, u32[]{:S(2)}) collective-permute-start(f32[2,6,64,256]{3,2,1,0:T(8,128)S(1)} %pad_maximum_fusion.refs_4_), channel_id=1, source_target_pairs={{0,3},{1,0},{2,1},{3,2},{4,7},{5,4},{6,5},{7,6},{8,11},{9,8},{10,9... | collective-permute-start | bytes 2359304 | tf_op jit(solution)/shard_map/ppermute | solution.py:710
  20.6 84.6 %collective-permute-start.4 = (f32[2,6,64,256]{3,2,1,0:T(8,128)S(1)}, f32[2,6,64,256]{3,2,1,0:T(8,128)S(1)}, u32[]{:S(2)}, u32[]{:S(2)}) collective-permute-start(f32[2,6,64,256]{3,2,1,0:T(8,128)S(1)} %pad_maximum_fusion.refs_4_), channel_id=1, source_target_pairs={{0,2},{1,3},{2,0},{3,1},{4,6},{5,7},{6,4},{7,5},{8,10},{9,11},{10,... | collective-permute-start | bytes 2359304 | tf_op jit(solution)/shard_map/ppermute | solution.py:710
  43.7 61.5 %copy-start.2 = (s32[2]{0:T(128)S(1)}, s32[2]{0:T(128)}, u32[]{:S(2)}) copy-start(s32[2]{0:T(128)} %panel_rank.1) | copy-start | bytes 28
  43.7 0.7 copy-start
  44.4 60.8 %collective-permute-start.3 = (f32[2,6,64,256]{3,2,1,0:T(8,128)S(1)}, f32[2,6,64,256]{3,2,1,0:T(8,128)S(1)}, u32[]{:S(2)}, u32[]{:S(2)}) collective-permute-start(f32[2,6,64,256]{3,2,1,0:T(8,128)S(1)} %pad_maximum_fusion.refs_4_), channel_id=1, source_target_pairs={{0,1},{1,2},{2,3},{3,0},{4,5},{5,6},{6,7},{7,4},{8,9},{9,10},{10,1... | collective-permute-start | bytes 2359304 | tf_op jit(solution)/shard_map/ppermute | solution.py:710
  89.6 15.7 %copy-start.3 = (f32[64,1024]{1,0:T(8,128)}, f32[64,1024]{1,0:T(8,128)S(1)}, u32[]{:S(2)}) copy-start(f32[64,1024]{1,0:T(8,128)S(1)} %get-tuple-element.13.refs_11_) | copy-start | bytes 786436
  105.2 1.0 copy-start.1
Sparse Core Ops, SparseCore 0:
  9.4 34.1 all-gather.5
  45.5 27.9 all-gather.7

commit v9 on v8

--- a/solution.py
+++ b/solution.py
@@ -430,14 +430,26 @@
     refs[1][at] = lo
 
 
-def put_shards(refs, slot, sources, position, p, comp, rank):
-    count = len(sources)
-    width = sources[0].shape[-1]
-    rank_count = sources[0].shape[-2]
-    for s, ref in enumerate(sources):
+def shard_values(refs, position, count, p, comp):
+    value = lambda i: refs[i][p, comp]
+    if len(refs) == count:
+        return [value(i) for i in range(count)]
+    pick = lambda here, i, k: jnp.where(here, value(i), value(k))
+    return [
+        value(0),
+        pick(position == 0, 3, 1),
+        pick(position < 2, 4, 5),
+        pick(position == 3, 3, 2),
+    ]
+
+
+def put_shards(refs, slot, sources, position, count, p, comp, rank):
+    values = shard_values(sources, position, count, p, comp)
+    rank_count, width = values[0].shape
+    for s, value in enumerate(values):
         owner = lax.rem(position - s + count, count)
         at = pl.ds(pl.multiple_of(owner * width, width), width)
-        put(refs, (p, pl.ds(slot * rank_count, rank_count), at), keep_rows(ref[p, comp], rank))
+        put(refs, (p, pl.ds(slot * rank_count, rank_count), at), keep_rows(value, rank))
 
 
 def col_component(ref, comp, rank):
@@ -446,10 +458,9 @@
 
 
 def recompress_kernel(
-    tiles, shards, place, panel_rank, col_rank, tile_rank, keep_rank, *refs
+    tiles, shards, count, place, panel_rank, col_rank, tile_rank, keep_rank, *refs
 ):
-    first_any = refs[:shards]
-    second_any = refs[shards : 2 * shards]
+    rows_any = refs[:shards]
     (
         cols_any,
         trailing_any,
@@ -467,20 +478,18 @@
         panel_lo,
         cols,
         trailing,
-        first_all,
-        second_all,
+        rows_all,
         inverse,
         sketch,
         solved,
         products,
         out,
         sems,
-    ) = refs[2 * shards :]
-    first = [first_all.at[i] for i in range(shards)]
-    second = [second_all.at[i] for i in range(shards)]
+    ) = refs[shards:]
+    rows_in = [rows_all.at[i] for i in range(shards)]
     pairs = [(cols_any, cols)]
     pairs += [(trailing_any.at[p], trailing.at[p]) for p in range(tiles)]
-    pairs += list(zip(first_any, first)) + list(zip(second_any, second))
+    pairs += list(zip(rows_any, rows_in))
     pairs += [(sketch_any, sketch), (solved_any, solved), (products_any, products)]
     pairs.append((inverse_any, inverse))
     copies = [
@@ -523,11 +532,10 @@
     for copy in copies[1 + tiles : -1]:
         copy.wait()
     for p in range(tiles):
-        put_shards(lefts, 1, first, position, p, 0, panel_rank[p])
-        put_shards(panels, 0, first, position, p, 1, panel_rank[p])
-        for t in range(3):
-            put_shards(lefts, 5 + t, second, position, p, t, panel_rank[p])
-            put_shards(panels, 1 + t, second, position, p, 3 + t, panel_rank[p])
+        for t in range(4):
+            rank = panel_rank[p]
+            put_shards(lefts, 1 if t == 0 else 4 + t, rows_in, position, count, p, t, rank)
+            put_shards(panels, t, rows_in, position, count, p, 4 + t, rank)
 
     sides = []
     for t in range(3):
@@ -630,7 +638,7 @@
 
 
 def run_recompress(
-    place, ranks, first, second, cols, trailing, sketch, solved, inverse, scale, products
+    place, ranks, count, shards, cols, trailing, sketch, solved, inverse, scale, products
 ):
     tiles = trailing.shape[0]
     rank_count, size = sketch.shape
@@ -641,10 +649,10 @@
         cols, trailing, sketch, solved, inverse, products
     )
     return pl.pallas_call(
-        functools.partial(recompress_kernel, tiles, len(first)),
+        functools.partial(recompress_kernel, tiles, len(shards), count),
         out_shape=jax.ShapeDtypeStruct(trailing.shape, F32),
         in_specs=[smem] * 5
-        + [pl.BlockSpec(memory_space=pl.ANY)] * (2 * len(first))
+        + [pl.BlockSpec(memory_space=pl.ANY)] * len(shards)
         + [hbm] * 5
         + [vmem, hbm],
         out_specs=hbm,
@@ -653,21 +661,20 @@
         + [
             pltpu.VMEM(cols.shape, F32),
             pltpu.VMEM(trailing.shape, F32),
-            pltpu.VMEM((len(first),) + first[0].shape, F32),
-            pltpu.VMEM((len(second),) + second[0].shape, F32),
+            pltpu.VMEM((len(shards),) + shards[0].shape, F32),
             pltpu.VMEM(inverse.shape, F32),
             pltpu.VMEM(sketch.shape, F32),
             pltpu.VMEM(solved.shape, F32),
             pltpu.VMEM(products.shape, F32),
             pltpu.VMEM(trailing.shape, F32),
-            pltpu.SemaphoreType.DMA((5 + tiles + 2 * len(first) + 2 * tiles,)),
+            pltpu.SemaphoreType.DMA((5 + tiles + len(shards) + 2 * tiles,)),
         ],
         compiler_params=pltpu.CompilerParams(vmem_limit_bytes=RECOMPRESS_VMEM),
         cost_estimate=pl.CostEstimate(
             flops=10 * 10**9, bytes_accessed=20 * 2**20, transcendentals=0
         ),
         name="recompress",
-    )(place, *ranks, *first, *second, cols, trailing, sketch, solved, inverse, scale, products)
+    )(place, *ranks, *shards, cols, trailing, sketch, solved, inverse, scale, products)
 
 
 def on_device(
@@ -701,15 +708,27 @@
             [values[:, i : i + width] for i in range(0, values.shape[1], width)], axis=0
         )
     gathered = lax.all_gather(jnp.concatenate([own, values], axis=0), "row", axis=0)
-    first = panel_rows[:, 0::4]
-    second = jnp.concatenate([panel_rows[:, 1:4], panel_rows[:, 5:8]], axis=1)
-    first_shards, second_shards = [first], [second]
-    for source, shards in ((first, first_shards), (second, second_shards)):
-        for s in range(1, col_count):
-            shards.append(
-                lax.ppermute(source, "col", [(i, (i + s) % col_count) for i in range(col_count)])
-            )
-    late_cols, gathered = lax.optimization_barrier((panel_cols[0], gathered))
+    if col_count == 4:
+        send = lambda x, pairs: lax.ppermute(x, "col", pairs)
+        from_left = send(panel_rows, [(0, 1), (1, 2), (2, 3)])
+        from_right = send(panel_rows, [(1, 0), (2, 1), (3, 2)])
+        late_cols, late_rows, from_left, from_right, gathered = lax.optimization_barrier(
+            (panel_cols[0], panel_rows, from_left, from_right, gathered)
+        )
+        shards = [
+            panel_rows,
+            from_left,
+            from_right,
+            send(late_rows, [(0, 3), (3, 0)]),
+            send(from_right, [(1, 0), (2, 1)]),
+            send(from_left, [(1, 2), (2, 3)]),
+        ]
+    else:
+        shards = [panel_rows] + [
+            lax.ppermute(panel_rows, "col", [(i, (i + s) % col_count) for i in range(col_count)])
+            for s in range(1, col_count)
+        ]
+        late_cols, gathered = lax.optimization_barrier((panel_cols[0], gathered))
     cols = lax.all_gather(late_cols, "row", axis=0)
     if own_ranks != SUB:
         cols = cols.reshape(-1, SUB // own_ranks, comps, own_ranks, size)
@@ -723,8 +742,8 @@
     return run_recompress(
         place,
         ranks,
-        first_shards,
-        second_shards,
+        col_count,
+        shards,
         cols,
         trailing,
         sketch,

time: 136 us -> 143 us (1.051)
  local copies, waits for them, and re-layouts: 5.87 us -> 8.9 us
  starting transfers between devices: 11.6 us -> 14.2 us
    ppermute x6 -> x5, waiting for transfers between devices: 4.3 us -> 21.5 us  [on_device(): send = lambda x, pairs: lax.ppermute(x, 'col', pairs)]
    all_gather x1, waiting for transfers between devices: 21.1 us -> 5.02 us  [on_device(): lax.all_gather(jnp.concatenate([own, values], axis=0), 'row', axis=0)]
    unnamed x14 -> x24, local copies, waits for them, and re-layouts: 1.85 us -> 6.95 us
    ppermute x6 -> x5, starting transfers between devices: 11.6 us -> 14.2 us  [on_device(): send = lambda x, pairs: lax.ppermute(x, 'col', pairs)]
    slice x2 -> x0, local copies, waits for them, and re-layouts: 2.16 us -> none  [the longest x1 1.19 us: on_device(): second = jnp.concatenate([panel_rows[:, 1:4], panel_rows[:, 5:8]], axis=1)]
  transfers between devices with their start and end apart: 8 -> 7, of which waited for: 2 -> 3; matrix products, arithmetic and copies ran while one was open for 2% -> 0% of each run, Pallas kernels for 32% -> 31%
where the time goes in v9:
time: 143 us; the launch traced here: 142 us
  Pallas kernels  66.5 us (47%)
  waiting for transfers between devices  26.6 us (19%)
  starting transfers between devices  14.2 us (10%)
  between operations  14.2 us (10%)
  blocking collectives  11.3 us (8%)
  local copies, waits for them, and re-layouts  8.9 us (6%)
    pallas_call x1, Pallas kernels, run_inverse(): pl.pallas_call(functools.partial(inverse_kernel, own_rows), out_shape=(pl...  43.8 us
    pallas_call x1, Pallas kernels, run_recompress(): pl.pallas_call(functools.partial(recompress_kernel, tiles, len(shards), c...  22.8 us
    ppermute x5, waiting for transfers between devices, on_device(): send = lambda x, pairs: lax.ppermute(x, 'col', pairs)  21.5 us
    ppermute x5, starting transfers between devices, on_device(): send = lambda x, pairs: lax.ppermute(x, 'col', pairs)  14.2 us
    all_gather x1, blocking collectives, on_device(): all_products = lax.all_gather(products, 'row', axis=0)  11.3 us
    unnamed x24, local copies, waits for them, and re-layouts  6.95 us
    all_gather x1, waiting for transfers between devices, on_device(): lax.all_gather(jnp.concatenate([own, values], axis=0), 'row', axis=0)  5.02 us
  transfers between devices with their start and end apart: 7, of which 3 were waited for; matrix products, arithmetic and copies ran while one was open for 0% of the time, Pallas kernels for 31%

profile of v9, /device:TPU:0, one launch (start us, length us, event | category | flops | bytes accessed | tf_op | source)
XLA Modules:
  0.0 142.5 jit_solution(10624261465554998251)
XLA Ops:
  6.5 0.0 all-gather.6.cloned.1.call-start
  6.5 0.8 slice_bitcast_fusion.1
  7.4 1.1 slice_bitcast_fusion
  8.5 0.1 fusion
  8.6 0.8 pad_maximum_fusion
  9.4 0.0 all-gather.6.cloned.1.call-update
  9.4 0.0 all-gather.8.cloned.1.call-start
  9.4 1.3 collective-permute-start.1
  10.7 5.6 %collective-permute-start = (f32[2,8,64,256]{3,2,1,0:T(8,128)S(1)}, f32[2,8,64,256]{3,2,1,0:T(8,128)S(1)}, u32[]{:S(2)}, u32[]{:S(2)}) collective-permute-start(f32[2,8,64,256]{3,2,1,0:T(8,128)S(1)} %copy-done), channel_id=1, source_target_pairs={{0,1},{1,2},{2,3},{4,5},{5,6},{6,7},{8,9},{9,10},{10,11},{12,13},{... | collective-permute-start | bytes 3145736 | tf_op jit(solution)/shard_map/ppermute | solution.py:712
  17.0 0.1 copy.12.tile_rank
  17.1 0.1 copy.13.keep_rank
  17.2 20.3 %collective-permute-done.1.refs_2_ = f32[2,8,64,256]{3,2,1,0:T(8,128)S(1)} collective-permute-done((f32[2,8,64,256]{3,2,1,0:T(8,128)S(1)}, f32[2,8,64,256]{3,2,1,0:T(8,128)S(1)}, u32[]{:S(2)}, u32[]{:S(2)}) %collective-permute-start.1) | collective-permute-done | bytes 1048608 | tf_op jit(solution)/shard_map/ppermute | solution.py:712
  37.5 1.2 collective-permute-done.refs_1_
  38.7 5.0 %all-gather.6.cloned.1.call-done = f32[1152,640]{1,0:T(8,128)} async-done(((f32[144,640]{1,0:T(8,128)}), f32[1152,640]{1,0:T(8,128)}) %all-gather.6.cloned.1.call-update) | async-done | bytes 2949136 | tf_op jit(solution)/shard_map/all_gather | solution.py:710
  43.7 0.0 all-gather.8.cloned.1.call-update
  43.7 0.0 copy-start.7
  43.8 5.2 %collective-permute-start.2 = (f32[2,8,64,256]{3,2,1,0:T(8,128)S(1)}, f32[2,8,64,256]{3,2,1,0:T(8,128)S(1)}, u32[]{:S(2)}, u32[]{:S(2)}) collective-permute-start(f32[2,8,64,256]{3,2,1,0:T(8,128)S(1)} %copy-done), channel_id=1, source_target_pairs={{0,3},{3,0},{4,7},{7,4},{8,11},{11,8},{12,15},{15,12},{16,19},{19,... | collective-permute-start | bytes 3145736 | tf_op jit(solution)/shard_map/ppermute | solution.py:712
  49.0 0.7 collective-permute-start.4
  49.7 1.3 collective-permute-start.3
  51.0 43.8 %inverse.1 = (f32[1024,1024]{1,0:T(8,128)}, f32[64,1024]{1,0:T(8,128)S(1)}, f32[3,64,128]{2,1,0:T(8,128)S(1)}, f32[1,1024]{1,0:T(1,128)S(1)}) custom-call(f32[8,144,640]{2,1,0:T(8,128)} %bitcast.11, s32[1]{0:T(128)S(6)} %copy.14.col_rank, f32[4,128,1024]{2,1,0:T(8,128)} %diag.1), custom_call_target="tpu_custom_call" | custom-call | flops 40000000000 | bytes 10485760 | tf_op jit(solution)/shard_map/inverse/pallas_call | solution.py:383
  94.8 11.3 %all-gather.2 = f32[24,64,128]{2,1,0:T(8,128)} all-gather(f32[3,64,128]{2,1,0:T(8,128)S(1)} %get-tuple-element.22), channel_id=4, replica_groups=mesh['row'=8,'col'=4] {'row'}, dimensions={0}, use_global_device_ids=true | all-gather | bytes 884736 | tf_op jit(solution)/shard_map/all_gather | solution.py:739
  106.1 0.0 collective-permute-done.2.refs_3_
  106.1 1.0 copy-done.1
  107.1 0.0 collective-permute-done.4.refs_5_
  107.1 1.0 copy-done.3
  108.1 0.0 collective-permute-done.3.refs_4_
  108.1 1.1 copy-done.5
  109.2 0.0 copy-done.7
  109.2 1.2 copy-done.2
  110.4 1.2 copy-done.4
  111.6 1.2 copy-done.6
  112.9 22.8 %recompress.1 = f32[2,1,8,64,1024]{4,3,2,1,0:T(8,128)} custom-call(s32[1]{0:T(128)} %bitcast.place, s32[2]{0:T(128)S(1)} %copy-done.7, s32[1]{0:T(128)S(6)} %copy.14.col_rank, s32[2,1]{1,0:T(2,128)S(1)} %copy.12.tile_rank, s32[2,1]{1,0:T(2,128)S(1)} %copy.13.keep_rank, f32[2,8,64,256]{3,2,1,0:T(8,128)S(1)} %copy-done, ...), custom_call_target="tpu_custom_call" | custom-call | flops 10000000000 | bytes 20971520 | tf_op jit(solution)/shard_map/recompress/pallas_call | solution.py:651
  (17 shorter events, 0.1 us)
Async XLA Ops:
  6.5 2.9 %copy-start = (f32[2,8,64,256]{3,2,1,0:T(8,128)S(1)}, f32[2,8,64,256]{3,2,1,0:T(8,128)}, u32[]{:S(2)}) copy-start(f32[2,8,64,256]{3,2,1,0:T(8,128)} %refs_0_.1) | copy-start | bytes 3145732
  6.5 10.5 %copy-start.9 = (s32[2,1]{0,1:T(1,128)S(1)}, s32[2,1]{0,1:T(1,128)}, u32[]{:S(2)}) copy-start(s32[2,1]{0,1:T(1,128)} %param.16) | copy-start | bytes 28
  6.5 10.6 %copy-start.10 = (s32[2,1]{0,1:T(1,128)S(1)}, s32[2,1]{0,1:T(1,128)}, u32[]{:S(2)}) copy-start(s32[2,1]{0,1:T(1,128)} %param.17) | copy-start | bytes 28
  6.5 37.2 %all-gather.6.cloned.1.call-start = ((), (), s32[]{:S(2)}) async-start(), calls=%async_computation | async-start | bytes 3317760 | tf_op jit(solution)/shard_map/all_gather | solution.py:710
  9.4 99.8 %all-gather.8.cloned.1.call-start = ((), (), s32[]{:S(2)}) async-start(), calls=%async_computation.1 | async-start | bytes 2359296 | tf_op jit(solution)/shard_map/all_gather | solution.py:732
  9.4 28.1 %collective-permute-start.1 = (f32[2,8,64,256]{3,2,1,0:T(8,128)S(1)}, f32[2,8,64,256]{3,2,1,0:T(8,128)S(1)}, u32[]{:S(2)}, u32[]{:S(2)}) collective-permute-start(f32[2,8,64,256]{3,2,1,0:T(8,128)S(1)} %copy-done), channel_id=1, source_target_pairs={{1,0},{2,1},{3,2},{5,4},{6,5},{7,6},{9,8},{10,9},{11,10},{13,12},{... | collective-permute-start | bytes 3145736 | tf_op jit(solution)/shard_map/ppermute | solution.py:712
  10.7 28.0 %collective-permute-start = (f32[2,8,64,256]{3,2,1,0:T(8,128)S(1)}, f32[2,8,64,256]{3,2,1,0:T(8,128)S(1)}, u32[]{:S(2)}, u32[]{:S(2)}) collective-permute-start(f32[2,8,64,256]{3,2,1,0:T(8,128)S(1)} %copy-done), channel_id=1, source_target_pairs={{0,1},{1,2},{2,3},{4,5},{5,6},{6,7},{8,9},{9,10},{10,11},{12,13},{... | collective-permute-start | bytes 3145736 | tf_op jit(solution)/shard_map/ppermute | solution.py:712
  43.7 65.4 %copy-start.7 = (s32[2]{0:T(128)S(1)}, s32[2]{0:T(128)}, u32[]{:S(2)}) copy-start(s32[2]{0:T(128)} %panel_rank.1) | copy-start | bytes 28
  43.8 62.3 %collective-permute-start.2 = (f32[2,8,64,256]{3,2,1,0:T(8,128)S(1)}, f32[2,8,64,256]{3,2,1,0:T(8,128)S(1)}, u32[]{:S(2)}, u32[]{:S(2)}) collective-permute-start(f32[2,8,64,256]{3,2,1,0:T(8,128)S(1)} %copy-done), channel_id=1, source_target_pairs={{0,3},{3,0},{4,7},{7,4},{8,11},{11,8},{12,15},{15,12},{16,19},{19,... | collective-permute-start | bytes 3145736 | tf_op jit(solution)/shard_map/ppermute | solution.py:712
  49.0 58.1 %collective-permute-start.4 = (f32[2,8,64,256]{3,2,1,0:T(8,128)S(1)}, f32[2,8,64,256]{3,2,1,0:T(8,128)S(1)}, u32[]{:S(2)}, u32[]{:S(2)}) collective-permute-start(f32[2,8,64,256]{3,2,1,0:T(8,128)S(1)} %collective-permute-done.refs_1_), channel_id=1, source_target_pairs={{1,2},{2,3},{5,6},{6,7},{9,10},{10,11},{13,14},{14,15},{17,18},{18... | collective-permute-start | bytes 3145736 | tf_op jit(solution)/shard_map/ppermute | solution.py:712
  49.7 58.4 %collective-permute-start.3 = (f32[2,8,64,256]{3,2,1,0:T(8,128)S(1)}, f32[2,8,64,256]{3,2,1,0:T(8,128)S(1)}, u32[]{:S(2)}, u32[]{:S(2)}) collective-permute-start(f32[2,8,64,256]{3,2,1,0:T(8,128)S(1)} %collective-permute-done.1.refs_2_), channel_id=1, source_target_pairs={{1,0},{2,1},{5,4},{6,5},{9,8},{10,9},{13,12},{14,13},{17,16},{18,1... | collective-permute-start | bytes 3145736 | tf_op jit(solution)/shard_map/ppermute | solution.py:712
  94.8 12.3 %copy-start.8 = (f32[64,1024]{1,0:T(8,128)}, f32[64,1024]{1,0:T(8,128)S(1)}, u32[]{:S(2)}) copy-start(f32[64,1024]{1,0:T(8,128)S(1)} %get-tuple-element.19.refs_9_) | copy-start | bytes 786436
  106.1 1.0 copy-start.1
  107.1 1.0 copy-start.3
  108.1 1.1 copy-start.5
  109.2 1.2 copy-start.2
  110.4 1.2 copy-start.4
  111.6 1.2 copy-start.6
Sparse Core Ops, SparseCore 0:
  9.5 34.1 all-gather.5
  45.6 27.8 all-gather.7

commit v10 on v9

--- a/solution.py
+++ b/solution.py
@@ -645,6 +645,7 @@
     vmem = pl.BlockSpec(memory_space=pltpu.VMEM)
     smem = pl.BlockSpec(memory_space=pltpu.SMEM)
     hbm = pl.BlockSpec(memory_space=pltpu.HBM)
+    shards = in_hbm(*shards)
     cols, trailing, sketch, solved, inverse, products = in_hbm(
         cols, trailing, sketch, solved, inverse, products
     )
@@ -652,7 +653,7 @@
         functools.partial(recompress_kernel, tiles, len(shards), count),
         out_shape=jax.ShapeDtypeStruct(trailing.shape, F32),
         in_specs=[smem] * 5
-        + [pl.BlockSpec(memory_space=pl.ANY)] * len(shards)
+        + [hbm] * len(shards)
         + [hbm] * 5
         + [vmem, hbm],
         out_specs=hbm,

time: 143 us -> 140 us (0.979)
  local copies, waits for them, and re-layouts: 8.9 us -> 4.12 us
  Pallas kernels: 66.5 us -> 68.4 us
    unnamed x24 -> x18, local copies, waits for them, and re-layouts: 6.95 us -> 2.17 us
    pallas_call x1, Pallas kernels: 22.8 us -> 24.6 us  [run_recompress(): pl.pallas_call(functools.partial(recompress_kernel, tiles, len(shards), c...]
where the time goes in v10:
time: 140 us
  Pallas kernels  68.4 us (49%)
  waiting for transfers between devices  25.6 us (18%)
  starting transfers between devices  15.1 us (11%)
  between operations  14.2 us (10%)
  blocking collectives  11.5 us (8%)
  local copies, waits for them, and re-layouts  4.12 us (3%)
    pallas_call x1, Pallas kernels, run_inverse(): pl.pallas_call(functools.partial(inverse_kernel, own_rows), out_shape=(pl...  43.8 us
    pallas_call x1, Pallas kernels, run_recompress(): pl.pallas_call(functools.partial(recompress_kernel, tiles, len(shards), c...  24.6 us
    ppermute x5, waiting for transfers between devices, on_device(): send = lambda x, pairs: lax.ppermute(x, 'col', pairs)  20.6 us
    ppermute x5, starting transfers between devices, on_device(): send = lambda x, pairs: lax.ppermute(x, 'col', pairs)  15.1 us
    all_gather x1, blocking collectives, on_device(): all_products = lax.all_gather(products, 'row', axis=0)  11.5 us
    all_gather x1, waiting for transfers between devices, on_device(): lax.all_gather(jnp.concatenate([own, values], axis=0), 'row', axis=0)  5.02 us
  transfers between devices with their start and end apart: 7, of which 3 were waited for; matrix products, arithmetic and copies ran while one was open for 0% of the time, Pallas kernels for 31%

profile of v10, /device:TPU:0, one launch (start us, length us, event | category | flops | bytes accessed | tf_op | source)
XLA Modules:
  0.0 139.8 jit_solution(7955326713638494432)
XLA Ops:
  6.5 0.0 all-gather.6.cloned.1.call-start
  6.5 0.8 slice_bitcast_fusion.1
  7.4 1.1 slice_bitcast_fusion
  8.5 0.1 fusion
  8.6 0.8 pad_maximum_fusion
  9.4 0.0 all-gather.6.cloned.1.call-update
  9.4 0.0 all-gather.8.cloned.1.call-start
  9.4 0.0 copy-done.2
  9.4 1.3 collective-permute-start.1
  10.7 6.5 %collective-permute-start = (f32[2,8,64,256]{3,2,1,0:T(8,128)S(1)}, f32[2,8,64,256]{3,2,1,0:T(8,128)}, u32[]{:S(2)}, u32[]{:S(2)}) collective-permute-start(f32[2,8,64,256]{3,2,1,0:T(8,128)S(1)} %copy-done.2), channel_id=1, source_target_pairs={{0,1},{1,2},{2,3},{4,5},{5,6},{6,7},{8,9},{9,10},{10,11},{12,13},{... | collective-permute-start | bytes 3145736 | tf_op jit(solution)/shard_map/ppermute | solution.py:713
  17.9 0.0 copy-done.6
  17.9 0.1 copy.12.tile_rank
  18.0 0.0 copy-done.7
  18.0 0.1 copy.13.keep_rank
  18.1 19.4 %collective-permute-done.1.refs_2_ = f32[2,8,64,256]{3,2,1,0:T(8,128)S(1)} collective-permute-done((f32[2,8,64,256]{3,2,1,0:T(8,128)S(1)}, f32[2,8,64,256]{3,2,1,0:T(8,128)S(1)}, u32[]{:S(2)}, u32[]{:S(2)}) %collective-permute-start.1) | collective-permute-done | bytes 1048608 | tf_op jit(solution)/shard_map/ppermute | solution.py:713
  37.5 1.2 collective-permute-done.refs_1_
  38.7 5.0 %all-gather.6.cloned.1.call-done = f32[1152,640]{1,0:T(8,128)} async-done(((f32[144,640]{1,0:T(8,128)}), f32[1152,640]{1,0:T(8,128)}) %all-gather.6.cloned.1.call-update) | async-done | bytes 2949136 | tf_op jit(solution)/shard_map/all_gather | solution.py:711
  43.7 0.0 all-gather.8.cloned.1.call-update
  43.7 0.0 copy-start
  43.8 5.2 %collective-permute-start.2 = (f32[2,8,64,256]{3,2,1,0:T(8,128)S(1)}, f32[2,8,64,256]{3,2,1,0:T(8,128)S(1)}, u32[]{:S(2)}, u32[]{:S(2)}) collective-permute-start(f32[2,8,64,256]{3,2,1,0:T(8,128)S(1)} %copy-done.2), channel_id=1, source_target_pairs={{0,3},{3,0},{4,7},{7,4},{8,11},{11,8},{12,15},{15,12},{16,19},{19,... | collective-permute-start | bytes 3145736 | tf_op jit(solution)/shard_map/ppermute | solution.py:713
  49.0 0.7 collective-permute-start.4
  49.7 1.3 collective-permute-start.3
  51.0 43.8 %inverse.1 = (f32[1024,1024]{1,0:T(8,128)}, f32[64,1024]{1,0:T(8,128)S(1)}, f32[3,64,128]{2,1,0:T(8,128)S(1)}, f32[1,1024]{1,0:T(1,128)S(1)}) custom-call(f32[8,144,640]{2,1,0:T(8,128)} %bitcast.11, s32[1]{0:T(128)S(6)} %copy.14.col_rank, f32[4,128,1024]{2,1,0:T(8,128)} %diag.1), custom_call_target="tpu_custom_call" | custom-call | flops 40000000000 | bytes 10485760 | tf_op jit(solution)/shard_map/inverse/pallas_call | solution.py:383
  94.8 0.0 copy-done.3
  94.8 0.0 copy-start.1
  94.8 11.5 %all-gather.2 = f32[24,64,128]{2,1,0:T(8,128)} all-gather(f32[3,64,128]{2,1,0:T(8,128)S(1)} %get-tuple-element.22), channel_id=4, replica_groups=mesh['row'=8,'col'=4] {'row'}, dimensions={0}, use_global_device_ids=true | all-gather | bytes 884736 | tf_op jit(solution)/shard_map/all_gather | solution.py:740
  106.3 0.0 collective-permute-done.2.refs_3_
  106.3 1.0 copy-done.4
  107.3 0.0 collective-permute-done.4.refs_5_
  107.3 1.0 copy-done.5
  108.3 0.0 collective-permute-done.3.refs_4_
  108.3 24.6 %recompress.1 = f32[2,1,8,64,1024]{4,3,2,1,0:T(8,128)} custom-call(s32[1]{0:T(128)} %bitcast.place, s32[2]{0:T(128)S(1)} %copy-done, s32[1]{0:T(128)S(6)} %copy.14.col_rank, s32[2,1]{1,0:T(2,128)S(1)} %copy.12.tile_rank, s32[2,1]{1,0:T(2,128)S(1)} %copy.13.keep_rank, f32[2,8,64,256]{3,2,1,0:T(8,128)} %refs_0_.1, ...), custom_call_target="tpu_custom_call" | custom-call | flops 10000000000 | bytes 20971520 | tf_op jit(solution)/shard_map/recompress/pallas_call | solution.py:652
  (11 shorter events, 0.0 us)
Async XLA Ops:
  6.5 2.9 %copy-start.2 = (f32[2,8,64,256]{3,2,1,0:T(8,128)S(1)}, f32[2,8,64,256]{3,2,1,0:T(8,128)}, u32[]{:S(2)}) copy-start(f32[2,8,64,256]{3,2,1,0:T(8,128)} %refs_0_.1) | copy-start | bytes 3145732
  6.5 11.4 %copy-start.6 = (s32[2,1]{0,1:T(1,128)S(1)}, s32[2,1]{0,1:T(1,128)}, u32[]{:S(2)}) copy-start(s32[2,1]{0,1:T(1,128)} %param.16) | copy-start | bytes 28
  6.5 11.5 %copy-start.7 = (s32[2,1]{0,1:T(1,128)S(1)}, s32[2,1]{0,1:T(1,128)}, u32[]{:S(2)}) copy-start(s32[2,1]{0,1:T(1,128)} %param.17) | copy-start | bytes 28
  6.5 37.2 %all-gather.6.cloned.1.call-start = ((), (), s32[]{:S(2)}) async-start(), calls=%async_computation | async-start | bytes 3317760 | tf_op jit(solution)/shard_map/all_gather | solution.py:711
  9.4 98.9 %all-gather.8.cloned.1.call-start = ((), (), s32[]{:S(2)}) async-start(), calls=%async_computation.1 | async-start | bytes 2359296 | tf_op jit(solution)/shard_map/all_gather | solution.py:733
  9.4 28.1 %collective-permute-start.1 = (f32[2,8,64,256]{3,2,1,0:T(8,128)S(1)}, f32[2,8,64,256]{3,2,1,0:T(8,128)S(1)}, u32[]{:S(2)}, u32[]{:S(2)}) collective-permute-start(f32[2,8,64,256]{3,2,1,0:T(8,128)S(1)} %copy-done.2), channel_id=1, source_target_pairs={{1,0},{2,1},{3,2},{5,4},{6,5},{7,6},{9,8},{10,9},{11,10},{13,12},{... | collective-permute-start | bytes 3145736 | tf_op jit(solution)/shard_map/ppermute | solution.py:713
  10.7 28.0 %collective-permute-start = (f32[2,8,64,256]{3,2,1,0:T(8,128)S(1)}, f32[2,8,64,256]{3,2,1,0:T(8,128)}, u32[]{:S(2)}, u32[]{:S(2)}) collective-permute-start(f32[2,8,64,256]{3,2,1,0:T(8,128)S(1)} %copy-done.2), channel_id=1, source_target_pairs={{0,1},{1,2},{2,3},{4,5},{5,6},{6,7},{8,9},{9,10},{10,11},{12,13},{... | collective-permute-start | bytes 3145736 | tf_op jit(solution)/shard_map/ppermute | solution.py:713
  37.5 57.3 %copy-start.3 = (f32[2,8,64,256]{3,2,1,0:T(8,128)}, f32[2,8,64,256]{3,2,1,0:T(8,128)S(1)}, u32[]{:S(2)}) copy-start(f32[2,8,64,256]{3,2,1,0:T(8,128)S(1)} %collective-permute-done.1.refs_2_) | copy-start | bytes 3145732
  43.7 64.5 %copy-start = (s32[2]{0:T(128)S(1)}, s32[2]{0:T(128)}, u32[]{:S(2)}) copy-start(s32[2]{0:T(128)} %panel_rank.1) | copy-start | bytes 28
  43.8 62.6 %collective-permute-start.2 = (f32[2,8,64,256]{3,2,1,0:T(8,128)S(1)}, f32[2,8,64,256]{3,2,1,0:T(8,128)S(1)}, u32[]{:S(2)}, u32[]{:S(2)}) collective-permute-start(f32[2,8,64,256]{3,2,1,0:T(8,128)S(1)} %copy-done.2), channel_id=1, source_target_pairs={{0,3},{3,0},{4,7},{7,4},{8,11},{11,8},{12,15},{15,12},{16,19},{19,... | collective-permute-start | bytes 3145736 | tf_op jit(solution)/shard_map/ppermute | solution.py:713
  49.0 58.3 %collective-permute-start.4 = (f32[2,8,64,256]{3,2,1,0:T(8,128)}, f32[2,8,64,256]{3,2,1,0:T(8,128)S(1)}, u32[]{:S(2)}, u32[]{:S(2)}) collective-permute-start(f32[2,8,64,256]{3,2,1,0:T(8,128)} %collective-permute-done.refs_1_), channel_id=1, source_target_pairs={{1,2},{2,3},{5,6},{6,7},{9,10},{10,11},{13,14},{14,15},{17,18},{18... | collective-permute-start | bytes 3145736 | tf_op jit(solution)/shard_map/ppermute | solution.py:713
  49.7 58.5 %collective-permute-start.3 = (f32[2,8,64,256]{3,2,1,0:T(8,128)S(1)}, f32[2,8,64,256]{3,2,1,0:T(8,128)}, u32[]{:S(2)}, u32[]{:S(2)}) collective-permute-start(f32[2,8,64,256]{3,2,1,0:T(8,128)S(1)} %collective-permute-done.1.refs_2_), channel_id=1, source_target_pairs={{1,0},{2,1},{5,4},{6,5},{9,8},{10,9},{13,12},{14,13},{17,16},{18,1... | collective-permute-start | bytes 3145736 | tf_op jit(solution)/shard_map/ppermute | solution.py:713
  94.8 11.5 %copy-start.1 = (f32[64,1024]{1,0:T(8,128)}, f32[64,1024]{1,0:T(8,128)S(1)}, u32[]{:S(2)}) copy-start(f32[64,1024]{1,0:T(8,128)S(1)} %get-tuple-element.19.refs_9_) | copy-start | bytes 786436
  106.3 1.0 copy-start.4
  107.3 1.0 copy-start.5
Sparse Core Ops, SparseCore 0:
  9.5 34.1 all-gather.5
  45.6 27.8 all-gather.7

commit v11 on v10

--- a/solution.py
+++ b/solution.py
@@ -431,16 +431,7 @@
 
 
 def shard_values(refs, position, count, p, comp):
-    value = lambda i: refs[i][p, comp]
-    if len(refs) == count:
-        return [value(i) for i in range(count)]
-    pick = lambda here, i, k: jnp.where(here, value(i), value(k))
-    return [
-        value(0),
-        pick(position == 0, 3, 1),
-        pick(position < 2, 4, 5),
-        pick(position == 3, 3, 2),
-    ]
+    return [refs[i][p, comp] for i in range(count)]
 
 
 def put_shards(refs, slot, sources, position, count, p, comp, rank):
@@ -709,27 +700,11 @@
             [values[:, i : i + width] for i in range(0, values.shape[1], width)], axis=0
         )
     gathered = lax.all_gather(jnp.concatenate([own, values], axis=0), "row", axis=0)
-    if col_count == 4:
-        send = lambda x, pairs: lax.ppermute(x, "col", pairs)
-        from_left = send(panel_rows, [(0, 1), (1, 2), (2, 3)])
-        from_right = send(panel_rows, [(1, 0), (2, 1), (3, 2)])
-        late_cols, late_rows, from_left, from_right, gathered = lax.optimization_barrier(
-            (panel_cols[0], panel_rows, from_left, from_right, gathered)
-        )
-        shards = [
-            panel_rows,
-            from_left,
-            from_right,
-            send(late_rows, [(0, 3), (3, 0)]),
-            send(from_right, [(1, 0), (2, 1)]),
-            send(from_left, [(1, 2), (2, 3)]),
-        ]
-    else:
-        shards = [panel_rows] + [
-            lax.ppermute(panel_rows, "col", [(i, (i + s) % col_count) for i in range(col_count)])
-            for s in range(1, col_count)
-        ]
-        late_cols, gathered = lax.optimization_barrier((panel_cols[0], gathered))
+    shards = [panel_rows] + [
+        lax.ppermute(panel_rows, "col", [(i, (i + s) % col_count) for i in range(col_count)])
+        for s in range(1, col_count)
+    ]
+    late_cols, gathered = lax.optimization_barrier((panel_cols[0], gathered))
     cols = lax.all_gather(late_cols, "row", axis=0)
     if own_ranks != SUB:
         cols = cols.reshape(-1, SUB // own_ranks, comps, own_ranks, size)

time: 140 us -> 134 us (0.957)
  the two profiles are of different devices: /device:TPU:0 before, /device:TPU:17 now
where the time goes in v11:
time: 134 us
  Pallas kernels  67.7 us (51%)
  waiting for transfers between devices  34.8 us (26%)
  between operations  14.2 us (11%)
  blocking collectives  11.6 us (9%)
  starting transfers between devices  2.58 us (2%)
  local copies, waits for them, and re-layouts  2.16 us (2%)
    pallas_call x1, Pallas kernels, run_inverse(): pl.pallas_call(functools.partial(inverse_kernel, own_rows), out_shape=(pl...  43.7 us
    all_gather x1, waiting for transfers between devices, on_device(): lax.all_gather(jnp.concatenate([own, values], axis=0), 'row', axis=0)  29.7 us
    pallas_call x1, Pallas kernels, run_recompress(): pl.pallas_call(functools.partial(recompress_kernel, tiles, len(shards), c...  24 us
    all_gather x1, blocking collectives, on_device(): all_products = lax.all_gather(products, 'row', axis=0)  11.6 us
    ppermute x3, waiting for transfers between devices, on_device(): lax.ppermute(panel_rows, 'col', [(i, (i + s) % col_count) for i in range(...  5.11 us
  transfers between devices with their start and end apart: 5, of which 2 were waited for; matrix products, arithmetic and copies ran while one was open for 0% of the time, Pallas kernels for 33%

profile of v11, /device:TPU:17, one launch (start us, length us, event | category | flops | bytes accessed | tf_op | source)
XLA Modules:
  0.0 133.9 jit_solution(10058877406896120656)
XLA Ops:
  6.5 0.0 copy-start.2
  6.5 0.0 copy-start.4
  6.5 0.0 copy-start.5
  6.5 0.0 all-gather.6.cloned.1.call-start
  6.5 0.8 slice_bitcast_fusion.1
  7.4 1.1 slice_bitcast_fusion
  8.5 0.1 fusion
  8.6 0.8 pad_maximum_fusion
  9.4 0.0 all-gather.6.cloned.1.call-update
  9.4 0.0 all-gather.8.cloned.1.call-start
  9.4 0.0 copy-done.2
  9.4 0.1 collective-permute-start.1
  9.5 1.3 %collective-permute-start = (f32[2,8,64,256]{3,2,1,0:T(8,128)S(1)}, f32[2,8,64,256]{3,2,1,0:T(8,128)}, u32[]{:S(2)}, u32[]{:S(2)}) collective-permute-start(f32[2,8,64,256]{3,2,1,0:T(8,128)S(1)} %copy-done.2), channel_id=1, source_target_pairs={{0,1},{1,2},{2,3},{3,0},{4,5},{5,6},{6,7},{7,4},{8,9},{9,10},{10,1... | collective-permute-start | bytes 3145736 | tf_op jit(solution)/shard_map/ppermute | solution.py:704
  10.9 1.1 collective-permute-start.2
  12.6 0.0 copy-done.4
  12.6 0.1 copy.12.tile_rank
  12.7 0.0 copy-done.5
  12.7 0.1 copy.13.keep_rank
  12.8 29.7 %all-gather.6.cloned.1.call-done = f32[1152,640]{1,0:T(8,128)} async-done(((f32[144,640]{1,0:T(8,128)}), f32[1152,640]{1,0:T(8,128)}) %all-gather.6.cloned.1.call-update) | async-done | bytes 2949136 | tf_op jit(solution)/shard_map/all_gather | solution.py:702
  42.5 0.0 all-gather.8.cloned.1.call-update
  42.5 0.0 copy-start
  42.6 43.7 %inverse.1 = (f32[1024,1024]{1,0:T(8,128)}, f32[64,1024]{1,0:T(8,128)S(1)}, f32[3,64,128]{2,1,0:T(8,128)S(1)}, f32[1,1024]{1,0:T(1,128)S(1)}) custom-call(f32[8,144,640]{2,1,0:T(8,128)} %bitcast.11, s32[1]{0:T(128)S(6)} %copy.14.col_rank, f32[4,128,1024]{2,1,0:T(8,128)} %diag.1), custom_call_target="tpu_custom_call" | custom-call | flops 40000000000 | bytes 10485760 | tf_op jit(solution)/shard_map/inverse/pallas_call | solution.py:383
  86.2 0.0 copy-start.1
  86.3 11.6 %all-gather.2 = f32[24,64,128]{2,1,0:T(8,128)} all-gather(f32[3,64,128]{2,1,0:T(8,128)S(1)} %get-tuple-element.16), channel_id=4, replica_groups=mesh['row'=8,'col'=4] {'row'}, dimensions={0}, use_global_device_ids=true | all-gather | bytes 884736 | tf_op jit(solution)/shard_map/all_gather | solution.py:715
  97.9 0.0 copy-done.1
  97.9 0.0 collective-permute-done.1.refs_2_
  97.9 0.0 copy-start.3
  97.9 5.1 %collective-permute-done.refs_1_ = f32[2,8,64,256]{3,2,1,0:T(8,128)} collective-permute-done((f32[2,8,64,256]{3,2,1,0:T(8,128)S(1)}, f32[2,8,64,256]{3,2,1,0:T(8,128)}, u32[]{:S(2)}, u32[]{:S(2)}) %collective-permute-start) | collective-permute-done | bytes 1048608 | tf_op jit(solution)/shard_map/ppermute | solution.py:704
  103.0 0.0 collective-permute-done.2.refs_3_
  103.0 0.0 copy-done.3
  103.0 0.0 copy-done
  103.0 24.0 %recompress.1 = f32[2,1,8,64,1024]{4,3,2,1,0:T(8,128)} custom-call(s32[1]{0:T(128)} %bitcast.place, s32[2]{0:T(128)S(1)} %copy-done, s32[1]{0:T(128)S(6)} %copy.14.col_rank, s32[2,1]{1,0:T(2,128)S(1)} %copy.12.tile_rank, s32[2,1]{1,0:T(2,128)S(1)} %copy.13.keep_rank, f32[2,8,64,256]{3,2,1,0:T(8,128)} %refs_0_.1, ...), custom_call_target="tpu_custom_call" | custom-call | flops 10000000000 | bytes 20971520 | tf_op jit(solution)/shard_map/recompress/pallas_call | solution.py:643
  (3 shorter events, 0.0 us)
Async XLA Ops:
  6.5 2.9 %copy-start.2 = (f32[2,8,64,256]{3,2,1,0:T(8,128)S(1)}, f32[2,8,64,256]{3,2,1,0:T(8,128)}, u32[]{:S(2)}) copy-start(f32[2,8,64,256]{3,2,1,0:T(8,128)} %refs_0_.1) | copy-start | bytes 3145732
  6.5 6.1 %copy-start.4 = (s32[2,1]{0,1:T(1,128)S(1)}, s32[2,1]{0,1:T(1,128)}, u32[]{:S(2)}) copy-start(s32[2,1]{0,1:T(1,128)} %param.16) | copy-start | bytes 28
  6.5 6.2 %copy-start.5 = (s32[2,1]{0,1:T(1,128)S(1)}, s32[2,1]{0,1:T(1,128)}, u32[]{:S(2)}) copy-start(s32[2,1]{0,1:T(1,128)} %param.17) | copy-start | bytes 28
  6.5 36.0 %all-gather.6.cloned.1.call-start = ((), (), s32[]{:S(2)}) async-start(), calls=%async_computation | async-start | bytes 3317760 | tf_op jit(solution)/shard_map/all_gather | solution.py:702
  9.4 93.6 %all-gather.8.cloned.1.call-start = ((), (), s32[]{:S(2)}) async-start(), calls=%async_computation.1 | async-start | bytes 2359296 | tf_op jit(solution)/shard_map/all_gather | solution.py:708
  9.4 88.4 %collective-permute-start.1 = (f32[2,8,64,256]{3,2,1,0:T(8,128)S(1)}, f32[2,8,64,256]{3,2,1,0:T(8,128)S(1)}, u32[]{:S(2)}, u32[]{:S(2)}) collective-permute-start(f32[2,8,64,256]{3,2,1,0:T(8,128)S(1)} %copy-done.2), channel_id=1, source_target_pairs={{0,2},{1,3},{2,0},{3,1},{4,6},{5,7},{6,4},{7,5},{8,10},{9,11},{10,... | collective-permute-start | bytes 3145736 | tf_op jit(solution)/shard_map/ppermute | solution.py:704
  9.5 93.5 %collective-permute-start = (f32[2,8,64,256]{3,2,1,0:T(8,128)S(1)}, f32[2,8,64,256]{3,2,1,0:T(8,128)}, u32[]{:S(2)}, u32[]{:S(2)}) collective-permute-start(f32[2,8,64,256]{3,2,1,0:T(8,128)S(1)} %copy-done.2), channel_id=1, source_target_pairs={{0,1},{1,2},{2,3},{3,0},{4,5},{5,6},{6,7},{7,4},{8,9},{9,10},{10,1... | collective-permute-start | bytes 3145736 | tf_op jit(solution)/shard_map/ppermute | solution.py:704
  10.9 92.1 %collective-permute-start.2 = (f32[2,8,64,256]{3,2,1,0:T(8,128)S(1)}, f32[2,8,64,256]{3,2,1,0:T(8,128)}, u32[]{:S(2)}, u32[]{:S(2)}) collective-permute-start(f32[2,8,64,256]{3,2,1,0:T(8,128)S(1)} %copy-done.2), channel_id=1, source_target_pairs={{0,3},{1,0},{2,1},{3,2},{4,7},{5,4},{6,5},{7,6},{8,11},{9,8},{10,9... | collective-permute-start | bytes 3145736 | tf_op jit(solution)/shard_map/ppermute | solution.py:704
  42.5 60.5 %copy-start = (s32[2]{0:T(128)S(1)}, s32[2]{0:T(128)}, u32[]{:S(2)}) copy-start(s32[2]{0:T(128)} %panel_rank.1) | copy-start | bytes 28
  86.2 11.6 %copy-start.1 = (f32[64,1024]{1,0:T(8,128)}, f32[64,1024]{1,0:T(8,128)S(1)}, u32[]{:S(2)}) copy-start(f32[64,1024]{1,0:T(8,128)S(1)} %get-tuple-element.13.refs_7_) | copy-start | bytes 786436
  97.9 5.1 %copy-start.3 = (f32[2,8,64,256]{3,2,1,0:T(8,128)}, f32[2,8,64,256]{3,2,1,0:T(8,128)S(1)}, u32[]{:S(2)}) copy-start(f32[2,8,64,256]{3,2,1,0:T(8,128)S(1)} %collective-permute-done.1.refs_2_) | copy-start | bytes 3145732
Sparse Core Ops, SparseCore 0:
  9.5 32.9 all-gather.5
  44.4 27.8 all-gather.7
